TPU v7x, 256 devices: a whole 4x4x8 slice. The times are simulated.
256 devices in a mesh: row: 8 (over z), col: 16 (over x, y), tm: 2 (over core).
Axes of the slice: x: 4, y: 4, z: 8, core: 2. Of those that a mesh axis runs over, the one named last changes fastest.
Arguments:
- records: bfloat16 [2, 32768, 7680], P('tm', ('row', 'col')), may hold values from -6 to 6
- taper: float32 [1200], replicated, may hold values from 0.25 to 1
- pairs: int32 [128, 4], P(('row', 'col')), may hold values from -1 to 127, as said below
Outputs:
- correlations: float32 [128, 4, 256, 256], P(('row', 'col'), None, 'tm')
Inputs may be any that keep to these rules, and one draw needn't show every extreme that they name: `pairs`: each entry of row a is a + o with 1 <= o <= 7, or -1 exactly where a + o would pass the last block; the entries of a row are distinct offsets.
All inputs are finite; a program needn't handle non-finite values.
Results may differ from a plain program's by a relative error of at most 0.0053.
Values may be sent and summed in bfloat16 or wider, within the bound.
No kernel may reach another device: no remote copies, remote signals or barrier semaphores. Data moves between devices by JAX's collectives and lax.ppermute only.
A program may use at most 128 MiB of HBM per device.

v0:
```python
import math

import jax
import jax.numpy as jnp
from jax import lax
from jax.sharding import PartitionSpec as P

SAMPLES = 7680
FREQS = 1200
FIRST_BIN = 32
LAGS = 256
SMOOTH = 4
PARTNERS = 4
REACH = 7


WATER = 0.3
RESCALE = 2.0


def from_behind(value, axis, steps):
    count = lax.axis_size(axis)
    leading, last = (max(0, -steps), min(count, count - steps))
    return lax.ppermute(value, axis, [(source, source + steps) for source in range(leading, last)])


def dft_table(start, block_len, freqs):
    samples = start + jnp.arange(block_len, dtype=jnp.int32)
    phase = samples[:, None] * freqs[None, :] % SAMPLES
    angle = phase.astype(jnp.float32) * (2.0 * math.pi / SAMPLES)
    return jnp.concatenate([jnp.cos(angle), -jnp.sin(angle)], axis=1).astype(jnp.bfloat16)


def spectra(series):
    block_len = math.gcd(SAMPLES, 512)
    freqs = FIRST_BIN + jnp.arange(FREQS, dtype=jnp.int32)

    def advance(total, start):
        piece = lax.dynamic_slice_in_dim(series, start, block_len, 1)
        return (
            total
            + jnp.dot(
                piece, dft_table(start, block_len, freqs), preferred_element_type=jnp.float32
            ),
            None,
        )

    starts = jnp.arange(SAMPLES // block_len, dtype=jnp.int32) * block_len
    total, unused = lax.scan(advance, jnp.zeros((series.shape[0], 2 * FREQS), jnp.float32), starts)
    return total


def whiten(spectrum, taper):
    real_part = spectrum[:, :FREQS]
    imag_part = spectrum[:, FREQS:]
    amplitude = jnp.sqrt(real_part * real_part + imag_part * imag_part)
    padded = jnp.pad(amplitude, ((0, 0), (SMOOTH, SMOOTH)))
    smoothed = padded[:, 0:FREQS]
    for offset in range(1, 2 * SMOOTH + 1):
        smoothed = smoothed + padded[:, offset : offset + FREQS]
    smoothed = smoothed / (2 * SMOOTH + 1)
    water_level = jnp.mean(amplitude, axis=1, keepdims=True)
    scaling = taper[None, :] / (smoothed + WATER * water_level + 1e-05)
    return jnp.concatenate([real_part * scaling, imag_part * scaling], axis=1).astype(jnp.bfloat16)


def lag_table():
    freqs = FIRST_BIN + jnp.arange(FREQS, dtype=jnp.int32)
    lag_steps = jnp.arange(LAGS, dtype=jnp.int32) - LAGS // 2 + SAMPLES
    phase = freqs[:, None] * lag_steps[None, :] % SAMPLES
    angle = phase.astype(jnp.float32) * (2.0 * math.pi / SAMPLES)
    return jnp.concatenate([jnp.cos(angle), -jnp.sin(angle)], axis=0)


def cross_spectrum(first, second):
    first = first.astype(jnp.float32)
    second = second.astype(jnp.float32)
    first_re = first[..., :FREQS]
    first_im = first[..., FREQS:]
    second_re = second[..., :FREQS]
    second_im = second[..., FREQS:]
    return jnp.concatenate(
        [first_re * second_re + first_im * second_im, first_im * second_re - first_re * second_im],
        axis=-1,
    )


def fetch_partners(local):
    received = [from_behind(local, ("row", "col"), -offset) for offset in range(1, REACH + 1)]
    return jnp.stack(received, axis=0)


def per_device(records, taper, pairs):
    series = records.reshape(-1, records.shape[-1])
    white = whiten(spectra(series), taper)
    window_count = records.shape[0] * lax.axis_size("tm")
    factor = RESCALE / math.sqrt(FREQS * window_count)
    local = white[None]
    partners = fetch_partners(local)
    position = lax.axis_index(("row", "col"))
    wanted = pairs[0]
    picked_rows = jnp.clip(wanted - position - 1, 0, REACH - 1)
    second = jnp.take(partners, picked_rows, axis=0)
    spec_sum = jnp.sum(cross_spectrum(local[None], second), axis=1)
    channels_here = local.shape[1]
    lagged = jnp.dot(
        spec_sum.reshape(-1, 2 * FREQS),
        lag_table(),
        precision=lax.Precision.HIGHEST,
        preferred_element_type=jnp.float32,
    )
    lagged = lagged.reshape(PARTNERS, channels_here, LAGS) * factor
    lagged = jnp.where(wanted[:, None, None] >= 0, lagged, jnp.zeros_like(lagged))
    stacked = lax.psum_scatter(lagged, "tm", scatter_dimension=1, tiled=True)
    return stacked[None]


def solution(mesh):
    return jax.shard_map(
        per_device,
        mesh=mesh,
        in_specs=(P("tm", ("row", "col"), None), P(), P(("row", "col"), None)),
        out_specs=P(("row", "col"), None, "tm", None),
        check_vma=False,
    )
```

profile of v0, /device:TPU:96, one launch (start us, length us, event | category | flops | bytes accessed | tf_op | source)
XLA Modules:
  0.0 668.4 jit_solution(6993236060508580210)
XLA Ops:
  6.5 301.5 %while.13 = (s32[]{:T(128)}, f32[256,2400]{0,1:T(8,128)S(1)}, s32[15]{0:T(128)S(1)}, bf16[256,7680]{1,0:T(8,128)(2,1)}, s32[]{:T(128)}, /*index=5*/s32[]{:T(128)}, s32[]{:T(128)}) while((s32[]{:T(128)}, f32[256,2400]{0,1:T(8,128)S(1)}, s32[15]{0:T(128)S(1)}, bf16[256,7680]{1,0:T(8,128)(2,1)}, s32[]{:T(128)}, /*index=5*/s32[]{:T(128)}, ...), condition=%wide.region_1.2_spmd.clone, body=%wide.region_0.1_spmd.clone.sunk | while | flops 642664128 | bytes 10270221 | solution.py:49
  10.0 12.2 %cosine_convert_fusion.2 = (bf16[512,1200]{1,0:T(8,128)(2,1)}, bf16[512,1200]{1,0:T(8,128)(2,1)}) fusion(s32[1200]{0:T(1024)S(1)} %iota_add_fusion.6, s32[512]{0:T(512)S(1)} %iota_add_fusion.7), kind=kLoop, calls=%fused_computation.7.clone.1 | loop fusion | flops 7372800 | bytes 2464448 | tf_op jit(solution)/shard_map/convert
  22.2 4.5 convolution_add_fusion.2
  30.1 12.2 %cosine_convert_fusion.2 = (bf16[512,1200]{1,0:T(8,128)(2,1)}, bf16[512,1200]{1,0:T(8,128)(2,1)}) fusion(s32[1200]{0:T(1024)S(1)} %iota_add_fusion.6, s32[512]{0:T(512)S(1)} %iota_add_fusion.7), kind=kLoop, calls=%fused_computation.7.clone.1 | loop fusion | flops 7372800 | bytes 2464448 | tf_op jit(solution)/shard_map/convert
  42.3 4.5 convolution_add_fusion.2
  50.2 12.2 %cosine_convert_fusion.2 = (bf16[512,1200]{1,0:T(8,128)(2,1)}, bf16[512,1200]{1,0:T(8,128)(2,1)}) fusion(s32[1200]{0:T(1024)S(1)} %iota_add_fusion.6, s32[512]{0:T(512)S(1)} %iota_add_fusion.7), kind=kLoop, calls=%fused_computation.7.clone.1 | loop fusion | flops 7372800 | bytes 2464448 | tf_op jit(solution)/shard_map/convert
  62.4 4.5 convolution_add_fusion.2
  70.3 12.2 %cosine_convert_fusion.2 = (bf16[512,1200]{1,0:T(8,128)(2,1)}, bf16[512,1200]{1,0:T(8,128)(2,1)}) fusion(s32[1200]{0:T(1024)S(1)} %iota_add_fusion.6, s32[512]{0:T(512)S(1)} %iota_add_fusion.7), kind=kLoop, calls=%fused_computation.7.clone.1 | loop fusion | flops 7372800 | bytes 2464448 | tf_op jit(solution)/shard_map/convert
  82.5 4.5 convolution_add_fusion.2
  90.4 12.2 %cosine_convert_fusion.2 = (bf16[512,1200]{1,0:T(8,128)(2,1)}, bf16[512,1200]{1,0:T(8,128)(2,1)}) fusion(s32[1200]{0:T(1024)S(1)} %iota_add_fusion.6, s32[512]{0:T(512)S(1)} %iota_add_fusion.7), kind=kLoop, calls=%fused_computation.7.clone.1 | loop fusion | flops 7372800 | bytes 2464448 | tf_op jit(solution)/shard_map/convert
  102.6 4.5 convolution_add_fusion.2
  110.5 12.2 %cosine_convert_fusion.2 = (bf16[512,1200]{1,0:T(8,128)(2,1)}, bf16[512,1200]{1,0:T(8,128)(2,1)}) fusion(s32[1200]{0:T(1024)S(1)} %iota_add_fusion.6, s32[512]{0:T(512)S(1)} %iota_add_fusion.7), kind=kLoop, calls=%fused_computation.7.clone.1 | loop fusion | flops 7372800 | bytes 2464448 | tf_op jit(solution)/shard_map/convert
  122.7 4.5 convolution_add_fusion.2
  130.6 12.2 %cosine_convert_fusion.2 = (bf16[512,1200]{1,0:T(8,128)(2,1)}, bf16[512,1200]{1,0:T(8,128)(2,1)}) fusion(s32[1200]{0:T(1024)S(1)} %iota_add_fusion.6, s32[512]{0:T(512)S(1)} %iota_add_fusion.7), kind=kLoop, calls=%fused_computation.7.clone.1 | loop fusion | flops 7372800 | bytes 2464448 | tf_op jit(solution)/shard_map/convert
  142.8 4.5 convolution_add_fusion.2
  150.7 12.2 %cosine_convert_fusion.2 = (bf16[512,1200]{1,0:T(8,128)(2,1)}, bf16[512,1200]{1,0:T(8,128)(2,1)}) fusion(s32[1200]{0:T(1024)S(1)} %iota_add_fusion.6, s32[512]{0:T(512)S(1)} %iota_add_fusion.7), kind=kLoop, calls=%fused_computation.7.clone.1 | loop fusion | flops 7372800 | bytes 2464448 | tf_op jit(solution)/shard_map/convert
  162.9 4.5 convolution_add_fusion.2
  170.8 12.2 %cosine_convert_fusion.2 = (bf16[512,1200]{1,0:T(8,128)(2,1)}, bf16[512,1200]{1,0:T(8,128)(2,1)}) fusion(s32[1200]{0:T(1024)S(1)} %iota_add_fusion.6, s32[512]{0:T(512)S(1)} %iota_add_fusion.7), kind=kLoop, calls=%fused_computation.7.clone.1 | loop fusion | flops 7372800 | bytes 2464448 | tf_op jit(solution)/shard_map/convert
  183.0 4.5 convolution_add_fusion.2
  190.9 12.2 %cosine_convert_fusion.2 = (bf16[512,1200]{1,0:T(8,128)(2,1)}, bf16[512,1200]{1,0:T(8,128)(2,1)}) fusion(s32[1200]{0:T(1024)S(1)} %iota_add_fusion.6, s32[512]{0:T(512)S(1)} %iota_add_fusion.7), kind=kLoop, calls=%fused_computation.7.clone.1 | loop fusion | flops 7372800 | bytes 2464448 | tf_op jit(solution)/shard_map/convert
  203.1 4.5 convolution_add_fusion.2
  211.0 12.2 %cosine_convert_fusion.2 = (bf16[512,1200]{1,0:T(8,128)(2,1)}, bf16[512,1200]{1,0:T(8,128)(2,1)}) fusion(s32[1200]{0:T(1024)S(1)} %iota_add_fusion.6, s32[512]{0:T(512)S(1)} %iota_add_fusion.7), kind=kLoop, calls=%fused_computation.7.clone.1 | loop fusion | flops 7372800 | bytes 2464448 | tf_op jit(solution)/shard_map/convert
  223.2 4.5 convolution_add_fusion.2
  231.1 12.2 %cosine_convert_fusion.2 = (bf16[512,1200]{1,0:T(8,128)(2,1)}, bf16[512,1200]{1,0:T(8,128)(2,1)}) fusion(s32[1200]{0:T(1024)S(1)} %iota_add_fusion.6, s32[512]{0:T(512)S(1)} %iota_add_fusion.7), kind=kLoop, calls=%fused_computation.7.clone.1 | loop fusion | flops 7372800 | bytes 2464448 | tf_op jit(solution)/shard_map/convert
  243.3 4.5 convolution_add_fusion.2
  251.2 12.2 %cosine_convert_fusion.2 = (bf16[512,1200]{1,0:T(8,128)(2,1)}, bf16[512,1200]{1,0:T(8,128)(2,1)}) fusion(s32[1200]{0:T(1024)S(1)} %iota_add_fusion.6, s32[512]{0:T(512)S(1)} %iota_add_fusion.7), kind=kLoop, calls=%fused_computation.7.clone.1 | loop fusion | flops 7372800 | bytes 2464448 | tf_op jit(solution)/shard_map/convert
  263.4 4.5 convolution_add_fusion.2
  271.3 12.2 %cosine_convert_fusion.2 = (bf16[512,1200]{1,0:T(8,128)(2,1)}, bf16[512,1200]{1,0:T(8,128)(2,1)}) fusion(s32[1200]{0:T(1024)S(1)} %iota_add_fusion.6, s32[512]{0:T(512)S(1)} %iota_add_fusion.7), kind=kLoop, calls=%fused_computation.7.clone.1 | loop fusion | flops 7372800 | bytes 2464448 | tf_op jit(solution)/shard_map/convert
  283.5 4.5 convolution_add_fusion.2
  291.4 12.2 %cosine_convert_fusion.2 = (bf16[512,1200]{1,0:T(8,128)(2,1)}, bf16[512,1200]{1,0:T(8,128)(2,1)}) fusion(s32[1200]{0:T(1024)S(1)} %iota_add_fusion.6, s32[512]{0:T(512)S(1)} %iota_add_fusion.7), kind=kLoop, calls=%fused_computation.7.clone.1 | loop fusion | flops 7372800 | bytes 2464448 | tf_op jit(solution)/shard_map/convert
  303.6 4.4 convolution_add_fusion.2
  311.8 6.7 collective-permute-start
  318.5 2.5 collective-permute-start.1
  321.0 3.1 collective-permute-start.2
  324.2 2.4 collective-permute-start.3
  326.7 4.1 collective-permute-start.4
  334.1 7.0 %fusion.23 = (f32[1200,256]{1,0:T(8,128)}, f32[1200,256]{1,0:T(8,128)}) fusion(s32[256]{0:T(256)S(1)} %iota_add_fusion.3, s32[1200]{0:T(1024)S(1)} %iota_add_fusion.2), kind=kLoop, calls=%fused_computation.49 | loop fusion | flops 3072000 | bytes 2463424 | tf_op jit(solution)/shard_map/cos | solution.py:72
  341.1 54.6 %collective-permute-done = bf16[1,256,2400]{1,2,0:T(8,128)(2,1)} collective-permute-done((bf16[1,256,2400]{1,2,0:T(8,128)(2,1)}, bf16[1,256,2400]{1,2,0:T(8,128)(2,1)}, u32[]{:S(2)}, u32[]{:S(2)}) %collective-permute-start) | collective-permute-done | bytes 1228832 | tf_op jit(solution)/shard_map/ppermute | solution.py:24
  400.1 53.9 %collective-permute-done.1 = bf16[1,256,2400]{1,2,0:T(8,128)(2,1)} collective-permute-done((bf16[1,256,2400]{1,2,0:T(8,128)(2,1)}, bf16[1,256,2400]{1,2,0:T(8,128)(2,1)}, u32[]{:S(2)}, u32[]{:S(2)}) %collective-permute-start.1) | collective-permute-done | bytes 1228832 | tf_op jit(solution)/shard_map/ppermute | solution.py:24
  458.3 25.4 %collective-permute-done.2 = bf16[1,256,2400]{1,2,0:T(8,128)(2,1)} collective-permute-done((bf16[1,256,2400]{1,2,0:T(8,128)(2,1)}, bf16[1,256,2400]{1,2,0:T(8,128)(2,1)}, u32[]{:S(2)}, u32[]{:S(2)}) %collective-permute-start.2) | collective-permute-done | bytes 1228832 | tf_op jit(solution)/shard_map/ppermute | solution.py:24
  486.1 74.7 %collective-permute-done.3 = bf16[1,256,2400]{1,2,0:T(8,128)(2,1)} collective-permute-done((bf16[1,256,2400]{1,2,0:T(8,128)(2,1)}, bf16[1,256,2400]{1,2,0:T(8,128)(2,1)}, u32[]{:S(2)}, u32[]{:S(2)}) %collective-permute-start.3) | collective-permute-done | bytes 1228832 | tf_op jit(solution)/shard_map/ppermute | solution.py:24
  563.2 2.4 bitcast_dynamic-update-slice_fusion.2
  565.6 20.1 %collective-permute-done.5 = bf16[1,256,2400]{1,2,0:T(8,128)(2,1)S(1)} collective-permute-done((bf16[1,256,2400]{1,2,0:T(8,128)(2,1)}, bf16[1,256,2400]{1,2,0:T(8,128)(2,1)S(1)}, u32[]{:S(2)}, u32[]{:S(2)}) %collective-permute-start.5) | collective-permute-done | bytes 1228832 | tf_op jit(solution)/shard_map/ppermute | solution.py:24
  586.8 24.1 %collective-permute-done.6 = bf16[1,256,2400]{1,2,0:T(8,128)(2,1)S(1)} collective-permute-done((bf16[1,256,2400]{1,2,0:T(8,128)(2,1)}, bf16[1,256,2400]{1,2,0:T(8,128)(2,1)S(1)}, u32[]{:S(2)}, u32[]{:S(2)}) %collective-permute-start.6) | collective-permute-done | bytes 1228832 | tf_op jit(solution)/shard_map/ppermute | solution.py:24
  612.0 6.6 gather_fusion
  618.6 3.2 fusion.16
  623.6 16.9 %multiply_select_fusion = f32[4,256,256]{2,1,0:T(8,128)} fusion(f32[1200,256]{1,0:T(8,128)S(1)} %copy-done.4, f32[1200,256]{1,0:T(8,128)S(1)} %copy-done.3, f32[4,1,256,1200]{2,3,0,1:T(8,128)S(1)} %get-tuple-element.104, f32[4,1,256,1200]{2,3,0,1:T(8,128)S(1)} %get-tuple-element.103, pred[4]{0:T(512)(128)(4,1)S(1)} %compare_bitcast_fusion), kind=kOutput, calls=%fused_computation.60 | convolution fusion | flops 7553343488 | bytes 13336580 | tf_op jit(solution)/shard_map/dot_general | solution.py:106
  640.5 21.0 %reduce-scatter.2.cloned.1.call-done = f32[4,128,256]{2,1,0:T(8,128)} async-done(((f32[4,256,256]{2,1,0:T(8,128)}), f32[4,128,256]{2,1,0:T(8,128)}) %reduce-scatter.2.cloned.1.call-update) | async-done | bytes 524304 | tf_op jit(solution)/shard_map/reduce_scatter | solution.py:114
  (87 shorter events, 44.8 us)
Async XLA Ops:
  6.5 655.0 %reduce-scatter.2.cloned.1.call-start = ((), (), s32[]{:S(2)}) async-start(), calls=%async_computation.1 | async-start | bytes 1572864 | tf_op jit(solution)/shard_map/reduce_scatter | solution.py:114
  308.0 0.7 copy-start.5
  310.4 1.5 copy-start
  310.4 20.4 %copy-start.6 = (s32[1,4]{1,0:T(1,128)S(1)}, s32[1,4]{1,0:T(1,128)}, u32[]{:S(2)}) copy-start(s32[1,4]{1,0:T(1,128)} %param.7) | copy-start | bytes 52
  311.8 83.9 %collective-permute-start = (bf16[1,256,2400]{1,2,0:T(8,128)(2,1)}, bf16[1,256,2400]{1,2,0:T(8,128)(2,1)}, u32[]{:S(2)}, u32[]{:S(2)}) collective-permute-start(bf16[1,256,2400]{1,2,0:T(8,128)(2,1)} %pad_maximum_fusion), channel_id=1, source_target_pairs={{2,0},{4,2},{6,4},{8,6},{10,8},{12,10},{14,12},{16,14},{18,16},{20... | collective-permute-start | bytes 3686408 | tf_op jit(solution)/shard_map/ppermute | solution.py:24
  318.5 135.5 %collective-permute-start.1 = (bf16[1,256,2400]{1,2,0:T(8,128)(2,1)}, bf16[1,256,2400]{1,2,0:T(8,128)(2,1)}, u32[]{:S(2)}, u32[]{:S(2)}) collective-permute-start(bf16[1,256,2400]{1,2,0:T(8,128)(2,1)} %pad_maximum_fusion), channel_id=1, source_target_pairs={{4,0},{6,2},{8,4},{10,6},{12,8},{14,10},{16,12},{18,14},{20,16},{2... | collective-permute-start | bytes 3686408 | tf_op jit(solution)/shard_map/ppermute | solution.py:24
  321.0 162.6 %collective-permute-start.2 = (bf16[1,256,2400]{1,2,0:T(8,128)(2,1)}, bf16[1,256,2400]{1,2,0:T(8,128)(2,1)}, u32[]{:S(2)}, u32[]{:S(2)}) collective-permute-start(bf16[1,256,2400]{1,2,0:T(8,128)(2,1)} %pad_maximum_fusion), channel_id=1, source_target_pairs={{6,0},{8,2},{10,4},{12,6},{14,8},{16,10},{18,12},{20,14},{22,16},{... | collective-permute-start | bytes 3686408 | tf_op jit(solution)/shard_map/ppermute | solution.py:24
  324.2 236.5 %collective-permute-start.3 = (bf16[1,256,2400]{1,2,0:T(8,128)(2,1)}, bf16[1,256,2400]{1,2,0:T(8,128)(2,1)}, u32[]{:S(2)}, u32[]{:S(2)}) collective-permute-start(bf16[1,256,2400]{1,2,0:T(8,128)(2,1)} %pad_maximum_fusion), channel_id=1, source_target_pairs={{8,0},{10,2},{12,4},{14,6},{16,8},{18,10},{20,12},{22,14},{24,16},... | collective-permute-start | bytes 3686408 | tf_op jit(solution)/shard_map/ppermute | solution.py:24
  326.7 236.5 %collective-permute-start.4 = (bf16[1,256,2400]{1,2,0:T(8,128)(2,1)}, bf16[1,256,2400]{1,2,0:T(8,128)(2,1)}, u32[]{:S(2)}, u32[]{:S(2)}) collective-permute-start(bf16[1,256,2400]{1,2,0:T(8,128)(2,1)} %pad_maximum_fusion), channel_id=1, source_target_pairs={{10,0},{12,2},{14,4},{16,6},{18,8},{20,10},{22,12},{24,14},{26,16}... | collective-permute-start | bytes 3686408 | tf_op jit(solution)/shard_map/ppermute | solution.py:24
  395.7 189.9 %collective-permute-start.5 = (bf16[1,256,2400]{1,2,0:T(8,128)(2,1)}, bf16[1,256,2400]{1,2,0:T(8,128)(2,1)S(1)}, u32[]{:S(2)}, u32[]{:S(2)}) collective-permute-start(bf16[1,256,2400]{1,2,0:T(8,128)(2,1)} %pad_maximum_fusion), channel_id=1, source_target_pairs={{12,0},{14,2},{16,4},{18,6},{20,8},{22,10},{24,12},{26,14},{28,16}... | collective-permute-start | bytes 3686408 | tf_op jit(solution)/shard_map/ppermute | solution.py:24
  454.0 156.9 %collective-permute-start.6 = (bf16[1,256,2400]{1,2,0:T(8,128)(2,1)}, bf16[1,256,2400]{1,2,0:T(8,128)(2,1)S(1)}, u32[]{:S(2)}, u32[]{:S(2)}) collective-permute-start(bf16[1,256,2400]{1,2,0:T(8,128)(2,1)} %pad_maximum_fusion), channel_id=1, source_target_pairs={{14,0},{16,2},{18,4},{20,6},{22,8},{24,10},{26,12},{28,14},{30,16}... | collective-permute-start | bytes 3686408 | tf_op jit(solution)/shard_map/ppermute | solution.py:24
  618.6 3.3 copy-start.1
  618.6 3.3 copy-start.2
  621.9 1.4 copy-start.3
  621.9 1.6 copy-start.4
Sparse Core Ops, SparseCore 0:
  640.6 20.8 reduce-scatter.1
where the time goes:
time: 673 us; the launch traced here: 668 us
  waiting for transfers between devices  274 us (41%)
  other arithmetic  210 us (31%)
  matrix products  83.8 us (12%)
  local copies, waits for them, and re-layouts  33.1 us (5%)
  loops' own time  31.5 us (5%)
  starting transfers between devices  22.7 us (3%)
  between operations  13.6 us (2%)
    ppermute x7, waiting for transfers between devices, from_behind(): lax.ppermute(value, axis, [(source, source + steps) for source in range(l...  253 us
    another operation x16, other arithmetic  184 us
    dot_general x15, matrix products, advance(): jnp.dot(piece, dft_table(start, block_len, freqs), preferred_element_type...  66.9 us
    another operation x1, loops' own time, spectra(): lax.scan(advance, jnp.zeros((series.shape[0], 2 * FREQS), jnp.float32), s...  31.5 us
    ppermute x7, starting transfers between devices, from_behind(): lax.ppermute(value, axis, [(source, source + steps) for source in range(l...  22.7 us
    reduce_scatter x1, waiting for transfers between devices, per_device(): stacked = lax.psum_scatter(lagged, 'tm', scatter_dimension=1, tiled=True)  21 us
    dot_general x1, matrix products, per_device(): jnp.dot(spec_sum.reshape(-1, 2 * FREQS), lag_table(), precision=lax.Preci...  16.9 us
    unnamed x20, local copies, waits for them, and re-layouts  13.7 us
  transfers between devices with their start and end apart: 8, of which 7 were waited for; matrix products, arithmetic and copies ran while one was open for 4% of the time, Pallas kernels for 0%

commit v1 on v0

v1 whole, which is shorter than its diff:
```python
import math

import jax
import jax.numpy as jnp
import ml_dtypes
import numpy as np
from jax import lax
from jax.experimental import pallas as pl
from jax.experimental.pallas import tpu as pltpu
from jax.sharding import PartitionSpec as P

SAMPLES = 7680
FREQS = 1200
FIRST_BIN = 32
LAGS = 256
SMOOTH = 4
PARTNERS = 4
REACH = 7
BLOCK = 256
WINDOWS = 2
WATER = 0.3
RESCALE = 2.0

QUARTER = SAMPLES // 4
HALF = BLOCK // 2
PER = FREQS // 4
BODY = 256
TAIL = PER - BODY
COLS = 2 * BODY + 128
WIDE = 4 * COLS
RESIDUES = (0, 2, 1, 3)
PLANE = 16
MINE = BLOCK // (2 * PLANE)
VMEM = 56 * 1024 * 1024


def spread(cos, sin):
    out = np.zeros(cos.shape[:-1] + (COLS,), np.float64)
    out[..., :BODY] = cos[..., :BODY]
    out[..., BODY : 2 * BODY] = sin[..., :BODY]
    out[..., 2 * BODY : 2 * BODY + TAIL] = cos[..., BODY:]
    out[..., 2 * BODY + 64 : 2 * BODY + 64 + TAIL] = sin[..., BODY:]
    return out


def residue_bins(residue):
    return FIRST_BIN + 4 * np.arange(PER) + residue


def dft_table():
    samples = np.arange(QUARTER)
    blocks = []
    for residue in RESIDUES:
        angle = (samples[:, None] * residue_bins(residue)[None, :] % SAMPLES) * (
            2.0 * math.pi / SAMPLES
        )
        blocks.append(spread(np.cos(angle), -np.sin(angle)))
    return np.stack(blocks).astype(np.float32).astype(ml_dtypes.bfloat16)


def lag_tables():
    lag_steps = np.arange(LAGS) - LAGS // 2 + SAMPLES
    factor = RESCALE / math.sqrt(FREQS * WINDOWS)
    blocks = []
    for residue in RESIDUES:
        angle = (lag_steps[:, None] * residue_bins(residue)[None, :] % SAMPLES) * (
            2.0 * math.pi / SAMPLES
        )
        blocks.append(spread(np.cos(angle), -np.sin(angle)).T)
    table = (np.concatenate(blocks) * factor).astype(np.float32)
    high = table.astype(ml_dtypes.bfloat16)
    low = (table - high.astype(np.float32)).astype(ml_dtypes.bfloat16)
    return high, low


def spread_taper(taper):
    parts = taper.reshape(PER, 4).T
    tail = jnp.pad(parts[:, BODY:], ((0, 0), (0, 64 - TAIL)))
    parts = jnp.concatenate([parts[:, :BODY], tail, tail], axis=1)
    return jnp.stack([parts[residue] for residue in RESIDUES])


def dft_kernel(x_ref, taper_ref, table_ref, mine_ref, theirs_ref, y_ref, s_ref):
    step = pl.program_id(0)
    core = lax.axis_index("tm")

    @pl.when(step == 0)
    def split():
        def rows(i, carry):
            at = pl.ds(pl.multiple_of(i * 16, 16), 16)
            x = [
                x_ref[at, n * QUARTER : (n + 1) * QUARTER].astype(jnp.float32) for n in range(4)
            ]
            even, odd = x[0] + x[2], x[1] + x[3]
            parts = (even + odd, even - odd, x[0] - x[2], x[1] - x[3])
            for n, part in enumerate(parts):
                y_ref[pl.ds(pl.multiple_of(n * BLOCK + i * 16, 16), 16), :] = part.astype(
                    jnp.bfloat16
                )
            return carry

        lax.fori_loop(0, BLOCK // 16, rows, 0)

    @pl.when(step < 2)
    def real_sums():
        at = pl.ds(pl.multiple_of(step * BLOCK, BLOCK), BLOCK)
        s_ref[at, :] = jnp.dot(y_ref[at, :], table_ref[0], preferred_element_type=jnp.float32)

    @pl.when(step >= 2)
    def complex_sums():
        at = pl.ds(pl.multiple_of((step - 1) * 2 * BLOCK, BLOCK), 2 * BLOCK)
        s_ref[at, :] = jnp.dot(
            y_ref[2 * BLOCK :, :], table_ref[0], preferred_element_type=jnp.float32
        )

    @pl.when(step == 3)
    def whiten():
        lane = lax.broadcasted_iota(jnp.int32, (16, 128), 1)
        low = lane < 64
        sign = jnp.where(low, 1.0, -1.0)

        def rows(i, first, out_ref):
            row = first + i * 16

            def load(base):
                block = s_ref[pl.ds(pl.multiple_of(base * BLOCK + row, 16), 16), :]
                return block[:, :BODY], block[:, BODY : 2 * BODY], block[:, 2 * BODY :]

            spectrum = [load(0), load(1)]
            for base, way in ((2, 1.0), (4, -1.0)):
                u_cos, u_sin, u_tail = load(base)
                v_cos, v_sin, v_tail = load(base + 1)
                spectrum.append(
                    (
                        u_cos + way * v_sin,
                        u_sin - way * v_cos,
                        u_tail + way * sign * pltpu.roll(v_tail, 64, 1),
                    )
                )
            amplitude = [None] * 4
            for residue, (re, im, tail) in zip(RESIDUES, spectrum):
                square = tail * tail
                square = jnp.where(low, square + pltpu.roll(square, 64, 1), 0.0)
                amplitude[residue] = jnp.concatenate(
                    [jnp.sqrt(re * re + im * im), jnp.sqrt(square)], axis=1
                )
            total = (amplitude[0] + amplitude[1]) + (amplitude[2] + amplitude[3])
            floor = WATER * jnp.sum(total, axis=1, keepdims=True) / FREQS + 1e-05
            before = [pltpu.roll(a, 1, 1) for a in amplitude]
            after = [pltpu.roll(a, BODY + 128 - 1, 1) for a in amplitude]
            for place, (residue, (re, im, tail)) in enumerate(zip(RESIDUES, spectrum)):
                smoothed = total + before[residue] + after[residue]
                for other in range(4):
                    if other > residue:
                        smoothed = smoothed + before[other]
                    if other < residue:
                        smoothed = smoothed + after[other]
                scale = taper_ref[place : place + 1, :] / (smoothed / (2 * SMOOTH + 1) + floor)
                last = scale[:, BODY:]
                last = jnp.where(low, last, pltpu.roll(last, 64, 1))
                white = jnp.concatenate([re * scale[:, :BODY], im * scale[:, :BODY], tail * last], 1)
                out_ref[
                    pl.ds(pl.multiple_of(i * 16, 16), 16), place * COLS : (place + 1) * COLS
                ] = white.astype(jnp.bfloat16)

        def theirs(i, carry):
            rows(i, (1 - core) * HALF, theirs_ref)
            return carry

        def mine(i, carry):
            rows(i, core * HALF, mine_ref)
            return carry

        lax.fori_loop(0, HALF // 16, theirs, 0)
        lax.fori_loop(0, HALF // 16, mine, 0)


def whitened(series, taper):
    half = jax.ShapeDtypeStruct((HALF, WIDE), jnp.bfloat16)
    table = jnp.asarray(dft_table())
    return pl.pallas_call(
        dft_kernel,
        grid=(4,),
        in_specs=[
            pl.BlockSpec((BLOCK, SAMPLES), lambda i: (0, 0)),
            pl.BlockSpec((4, BODY + 128), lambda i: (0, 0)),
            pl.BlockSpec((1, QUARTER, COLS), lambda i: (i, 0, 0)),
        ],
        out_specs=[pl.BlockSpec((HALF, WIDE), lambda i: (0, 0))] * 2,
        out_shape=[half, half],
        scratch_shapes=[
            pltpu.VMEM((4 * BLOCK, QUARTER), jnp.bfloat16),
            pltpu.VMEM((6 * BLOCK, COLS), jnp.float32),
        ],
        compiler_params=pltpu.CompilerParams(vmem_limit_bytes=VMEM),
        name="dft_whiten",
    )(series, spread_taper(taper), table)


def corr_kernel(pairs_ref, plane_ref, halo_ref, high_ref, low_ref, out_ref, w_ref, xh_ref, xl_ref, sems):
    base = lax.axis_index("row") * PLANE
    copies = [
        pltpu.make_async_copy(plane_ref, w_ref.at[:PLANE], sems.at[0]),
        pltpu.make_async_copy(halo_ref, w_ref.at[PLANE:], sems.at[1]),
    ]
    for copy in copies:
        copy.start()
    for copy in copies:
        copy.wait()
    lane = lax.broadcasted_iota(jnp.int32, (MINE, 128), 1)
    low = lane < 64

    def one_block(a, carry):
        first = w_ref[a].astype(jnp.float32)
        for slot in range(0, PARTNERS, 2):
            at = pl.ds(pl.multiple_of((a * PARTNERS + slot) * MINE, 16), 2 * MINE)
            seconds = []
            for k in (slot, slot + 1):
                index = jnp.clip(pairs_ref[a * PARTNERS + k] - base, 0, PLANE + REACH - 1)
                seconds.append(w_ref[index].astype(jnp.float32))
            for place in range(4):
                here = place * COLS
                pieces = []
                for second in seconds:
                    re, im = 0.0, 0.0
                    straight, crossed = 0.0, 0.0
                    for w in range(WINDOWS):
                        rows = slice(w * MINE, (w + 1) * MINE)
                        a_re = first[rows, here : here + BODY]
                        a_im = first[rows, here + BODY : here + 2 * BODY]
                        a_tail = first[rows, here + 2 * BODY : here + COLS]
                        b_re = second[rows, here : here + BODY]
                        b_im = second[rows, here + BODY : here + 2 * BODY]
                        b_tail = second[rows, here + 2 * BODY : here + COLS]
                        re = re + a_re * b_re + a_im * b_im
                        im = im + a_im * b_re - a_re * b_im
                        straight = straight + a_tail * b_tail
                        crossed = crossed + a_tail * pltpu.roll(b_tail, 64, 1)
                    tail = jnp.where(
                        low,
                        straight + pltpu.roll(straight, 64, 1),
                        crossed - pltpu.roll(crossed, 64, 1),
                    )
                    pieces.append(jnp.concatenate([re, im, tail], axis=1))
                cross = jnp.concatenate(pieces, axis=0)
                high = cross.astype(jnp.bfloat16)
                xh_ref[at, here : here + COLS] = high
                xl_ref[at, here : here + COLS] = (cross - high.astype(jnp.float32)).astype(
                    jnp.bfloat16
                )
        return carry

    lax.fori_loop(0, PLANE, one_block, 0)
    lagged = jnp.dot(xh_ref[...], high_ref[...], preferred_element_type=jnp.float32)
    lagged += jnp.dot(xh_ref[...], low_ref[...], preferred_element_type=jnp.float32)
    lagged += jnp.dot(xl_ref[...], high_ref[...], preferred_element_type=jnp.float32)
    out_ref[...] = lagged.reshape(out_ref.shape)

    def mask(i, carry):
        @pl.when(pairs_ref[i] < 0)
        def clear():
            out_ref[i] = jnp.zeros((MINE, LAGS), jnp.float32)

        return carry

    lax.fori_loop(0, PLANE * PARTNERS, mask, 0)


def correlated(pairs, plane, halo):
    high, low = lag_tables()
    rows = PLANE * PARTNERS * MINE
    vmem = pl.BlockSpec(memory_space=pltpu.VMEM)
    return pl.pallas_call(
        corr_kernel,
        in_specs=[
            pl.BlockSpec(memory_space=pltpu.SMEM),
            pl.BlockSpec(memory_space=pl.ANY),
            pl.BlockSpec(memory_space=pl.ANY),
            vmem,
            vmem,
        ],
        out_specs=vmem,
        out_shape=jax.ShapeDtypeStruct((PLANE * PARTNERS, MINE, LAGS), jnp.float32),
        scratch_shapes=[
            pltpu.VMEM((PLANE + REACH, 2 * MINE, WIDE), jnp.bfloat16),
            pltpu.VMEM((rows, WIDE), jnp.bfloat16),
            pltpu.VMEM((rows, WIDE), jnp.bfloat16),
            pltpu.SemaphoreType.DMA((2,)),
        ],
        compiler_params=pltpu.CompilerParams(vmem_limit_bytes=VMEM),
        name="correlate",
    )(pairs, plane, halo, jnp.asarray(high), jnp.asarray(low))


def per_device(records, taper, pairs):
    plane_pairs = lax.all_gather(pairs.reshape(-1), "col", axis=0, tiled=True)
    mine, theirs = whitened(records[0], taper)
    got = lax.ppermute(theirs, "tm", [(0, 1), (1, 0)])
    send = jnp.concatenate(
        [mine.reshape(PLANE, MINE, WIDE), got.reshape(PLANE, MINE, WIDE)], axis=1
    )
    plane = lax.all_to_all(send, "col", 0, 0, tiled=True)
    count = lax.axis_size("row")
    halo = lax.ppermute(plane[:REACH], "row", [(z, z - 1) for z in range(1, count)])
    lagged = correlated(plane_pairs, plane, halo)
    lagged = lagged.reshape(PLANE, PARTNERS, MINE, LAGS)
    back = lax.all_to_all(lagged, "col", 0, 0, tiled=True)
    return back.transpose(1, 0, 2, 3).reshape(1, PARTNERS, HALF, LAGS)


def solution(mesh):
    return jax.shard_map(
        per_device,
        mesh=mesh,
        in_specs=(P("tm", ("row", "col"), None), P(), P(("row", "col"), None)),
        out_specs=P(("row", "col"), None, "tm", None),
        check_vma=False,
    )
```

time: 673 us -> 94.4 us (0.14)
  waiting for transfers between devices: 274 us -> 2.31 us
  other arithmetic: 210 us -> 1.9 us
  matrix products: 83.8 us -> 0 us
  blocking collectives: 0 us -> 55.6 us
  loops' own time: 31.5 us -> 0 us
  local copies, waits for them, and re-layouts: 33.1 us -> 3.37 us
  Pallas kernels: 0 us -> 27.1 us
  starting transfers between devices: 22.7 us -> 2.02 us
  between operations: 13.6 us -> 0.75 us
    ppermute x7 -> x2, waiting for transfers between devices: 253 us -> 2.31 us  [the longest x1 2.31 us: per_device(): got = lax.ppermute(theirs, 'tm', [(0, 1), (1, 0)])]
    another operation x16 -> x1, other arithmetic: 184 us -> 0.61 us  [spread_taper(): return jnp.stack([parts[residue] for residue in RESIDUES])]
    dot_general x16 -> x0, matrix products: 83.8 us -> none  [the longest x15 66.9 us: advance(): jnp.dot(piece, dft_table(start, block_len, freqs), preferred_element_type...]
    all_to_all x0 -> x2, blocking collectives: none -> 42.1 us  [the longest x1 26.9 us: per_device(): plane = lax.all_to_all(send, 'col', 0, 0, tiled=True)]
    another operation x1 -> x0, loops' own time: 31.5 us -> none  [spectra(): lax.scan(advance, jnp.zeros((series.shape[0], 2 * FREQS), jnp.float32), s...]
    pallas_call x0 -> x2, Pallas kernels: none -> 27.1 us  [the longest x1 16.8 us: whitened(): pl.pallas_call(dft_kernel, grid=(4,), in_specs=[pl.BlockSpec((BLOCK, SAMP...]
    reduce_scatter x1 -> x0, waiting for transfers between devices: 21 us -> none  [per_device(): stacked = lax.psum_scatter(lagged, 'tm', scatter_dimension=1, tiled=True)]
    ppermute x7 -> x2, starting transfers between devices: 22.7 us -> 2.02 us  [the longest x1 2.02 us: per_device(): lax.ppermute(plane[:REACH], 'row', [(z, z - 1) for z in range(1, count)])]
  transfers between devices with their start and end apart: 8 -> 2, of which waited for: 7 -> 1; matrix products, arithmetic and copies ran while one was open for 4% -> 1% of each run, Pallas kernels for 0% -> 0%
where the time goes in v1:
time: 94.4 us; the launch traced here: 93 us
  blocking collectives  55.6 us (59%)
  Pallas kernels  27.1 us (29%)
  local copies, waits for them, and re-layouts  3.37 us (4%)
  waiting for transfers between devices  2.31 us (2%)
  starting transfers between devices  2.02 us (2%)
  other arithmetic  1.9 us (2%)
    all_to_all x1, blocking collectives, per_device(): plane = lax.all_to_all(send, 'col', 0, 0, tiled=True)  26.9 us
    pallas_call x1, Pallas kernels, whitened(): pl.pallas_call(dft_kernel, grid=(4,), in_specs=[pl.BlockSpec((BLOCK, SAMP...  16.8 us
    all_to_all x1, blocking collectives, per_device(): back = lax.all_to_all(lagged, 'col', 0, 0, tiled=True)  15.2 us
    all_gather x1, blocking collectives, per_device(): plane_pairs = lax.all_gather(pairs.reshape(-1), 'col', axis=0, tiled=True)  13.5 us
    pallas_call x1, Pallas kernels, correlated(): pl.pallas_call(corr_kernel, in_specs=[pl.BlockSpec(memory_space=pltpu.SME...  10.3 us
    ppermute x1, waiting for transfers between devices, per_device(): got = lax.ppermute(theirs, 'tm', [(0, 1), (1, 0)])  2.31 us
    ppermute x1, starting transfers between devices, per_device(): lax.ppermute(plane[:REACH], 'row', [(z, z - 1) for z in range(1, count)])  2.02 us
  transfers between devices with their start and end apart: 2, of which 1 were waited for; matrix products, arithmetic and copies ran while one was open for 1% of the time, Pallas kernels for 0%

profile of v1, /device:TPU:96, one launch (start us, length us, event | category | flops | bytes accessed | tf_op | source)
XLA Modules:
  0.0 93.0 jit_solution(4230444066114000863)
XLA Ops:
  0.0 0.8 reshape.19
  0.9 0.1 copy.8
  1.0 0.1 pad_maximum_fusion.1
  1.1 0.6 pad_maximum_fusion.2.taper_ref
  1.7 16.8 %dft_whiten.1 = (bf16[128,2560]{1,0:T(8,128)(2,1)}, bf16[128,2560]{1,0:T(8,128)(2,1)}) custom-call(bf16[256,7680]{1,0:T(8,128)(2,1)} %bitcast.13, f32[4,384]{1,0:T(4,128)} %pad_maximum_fusion.2.taper_ref, bf16[4,1920,640]{2,1,0:T(8,128)(2,1)} %constant.9.clone.table_ref), custom_call_target="tpu_custom_call" | custom-call | tf_op jit(solution)/shard_map/dft_whiten/pallas_call | solution.py:181
  18.5 0.0 collective-permute-start
  18.5 2.3 %collective-permute-done = bf16[128,2560]{1,0:T(8,128)(2,1)S(1)} collective-permute-done((bf16[128,2560]{1,0:T(8,128)(2,1)}, bf16[128,2560]{1,0:T(8,128)(2,1)S(1)}, u32[]{:S(2)}, u32[]{:S(2)}) %collective-permute-start) | collective-permute-done | bytes 655392 | tf_op jit(solution)/shard_map/ppermute | solution.py:298
  20.8 1.2 %pad_maximum_fusion = bf16[16,16,2560]{2,1,0:T(8,128)(2,1)S(1)} fusion(bf16[16,8,2560]{2,1,0:T(8,128)(2,1)S(1)} %bitcast.16, bf16[16,8,2560]{2,1,0:T(8,128)(2,1)} %bitcast.15), kind=kLoop, calls=%fused_computation | loop fusion | flops 2621440 | bytes 2621440 | tf_op jit(solution)/shard_map/concatenate | solution.py:299
  22.0 0.0 copy-start.3
  22.0 0.0 copy-start.2
  22.0 26.9 %all_to_all.10.plane_ref = bf16[16,16,2560]{2,1,0:T(8,128)(2,1)S(1)} all-to-all(bf16[16,16,2560]{2,1,0:T(8,128)(2,1)S(1)} %pad_maximum_fusion), channel_id=1, replica_groups=mesh['row'=8,'col'=16,'tm'=2] {'col'}, dimensions={0} | all-to-all | bytes 2621440 | tf_op jit(solution)/shard_map/all_to_all | solution.py:302
  48.9 0.0 copy-start
  48.9 2.0 %collective-permute-start.1 = (bf16[7,16,2560]{2,1,0:T(8,128)(2,1)S(1)}, bf16[7,16,2560]{2,1,0:T(8,128)(2,1)S(1)}, u32[]{:S(2)}, u32[]{:S(2)}) collective-permute-start(bf16[7,16,2560]{2,1,0:T(8,128)(2,1)S(1)} %slice.34), channel_id=1, source_target_pairs={{32,0},{64,32},{96,64},{128,96},{160,128},{192,160},{224,192},{33,... | collective-permute-start | bytes 1720328 | tf_op jit(solution)/shard_map/ppermute | solution.py:304
  51.0 0.0 copy-done.3
  51.0 0.6 dynamic-slice
  52.2 0.0 copy-done.2
  52.2 0.1 bitcast_dynamic-update-slice_fusion
  52.3 13.5 %all-reduce.1.pairs_ref = s32[64]{0:T(128)} all-reduce(s32[64]{0:T(128)S(1)} %bitcast_dynamic-update-slice_fusion), channel_id=2, replica_groups=mesh['row'=8,'col'=16,'tm'=2] {'col'}, use_global_device_ids=true, to_apply=%add.1 | all-reduce | flops 64 | bytes 512 | tf_op jit(solution)/shard_map/all_gather | solution.py:296
  65.9 0.0 collective-permute-done.1.halo_ref
  65.9 0.0 copy-done
  65.9 0.0 copy-start.1
  65.9 0.8 copy-done.1
  66.7 10.3 %correlate.1 = f32[64,8,256]{2,1,0:T(8,128)} custom-call(s32[64]{0:T(128)} %all-reduce.1.pairs_ref, bf16[16,16,2560]{2,1,0:T(8,128)(2,1)} %copy-done, bf16[7,16,2560]{2,1,0:T(8,128)(2,1)} %copy-done.1, bf16[2560,256]{1,0:T(8,128)(2,1)} %constant.10.clone.high_ref, bf16[2560,256]{1,0:T(8,128)(2,1)} %constant.11.clone.low_ref), custom_call_target="tpu_custom_call" | custom-call | tf_op jit(solution)/shard_map/correlate/pallas_call | solution.py:273
  77.0 15.2 %all_to_all.11 = f32[16,4,8,256]{3,2,1,0:T(8,128)S(1)} all-to-all(f32[16,4,8,256]{3,2,1,0:T(8,128)} %bitcast.14), channel_id=1, replica_groups=mesh['row'=8,'col'=16,'tm'=2] {'col'}, dimensions={0} | all-to-all | bytes 1048576 | tf_op jit(solution)/shard_map/all_to_all | solution.py:307
  92.2 0.8 copy_bitcast_fusion
  (6 shorter events, 0.1 us)
Async XLA Ops:
  18.5 2.3 %collective-permute-start = (bf16[128,2560]{1,0:T(8,128)(2,1)}, bf16[128,2560]{1,0:T(8,128)(2,1)S(1)}, u32[]{:S(2)}, u32[]{:S(2)}) collective-permute-start(bf16[128,2560]{1,0:T(8,128)(2,1)} %get-tuple-element.8), channel_id=1, source_target_pairs={{0,1},{1,0},{2,3},{3,2},{4,5},{5,4},{6,7},{7,6},{8,9},{9,8},{10,11... | collective-permute-start | bytes 1966088 | tf_op jit(solution)/shard_map/ppermute | solution.py:298
  22.0 29.0 %copy-start.3 = (u32[256]{0:T(256)S(1)}, u32[256]{0:T(256)}, u32[]{:S(2)}) copy-start(u32[256]{0:T(256)} %constant.18) | copy-start | bytes 3076
  22.0 30.2 %copy-start.2 = (s32[1,4]{1,0:T(1,128)S(1)}, s32[1,4]{1,0:T(1,128)}, u32[]{:S(2)}) copy-start(s32[1,4]{1,0:T(1,128)} %param.8) | copy-start | bytes 52
  48.9 17.0 %copy-start = (bf16[16,16,2560]{2,1,0:T(8,128)(2,1)}, bf16[16,16,2560]{2,1,0:T(8,128)(2,1)S(1)}, u32[]{:S(2)}) copy-start(bf16[16,16,2560]{2,1,0:T(8,128)(2,1)S(1)} %all_to_all.10.plane_ref) | copy-start | bytes 3932164
  48.9 16.9 %collective-permute-start.1 = (bf16[7,16,2560]{2,1,0:T(8,128)(2,1)S(1)}, bf16[7,16,2560]{2,1,0:T(8,128)(2,1)S(1)}, u32[]{:S(2)}, u32[]{:S(2)}) collective-permute-start(bf16[7,16,2560]{2,1,0:T(8,128)(2,1)S(1)} %slice.34), channel_id=1, source_target_pairs={{32,0},{64,32},{96,64},{128,96},{160,128},{192,160},{224,192},{33,... | collective-permute-start | bytes 1720328 | tf_op jit(solution)/shard_map/ppermute | solution.py:304
  65.9 0.8 copy-start.1

commit v2 on v0

v2 whole, which is shorter than its diff:
```python
import math

import jax
import jax.numpy as jnp
import ml_dtypes
import numpy as np
from jax import lax
from jax.experimental import pallas as pl
from jax.experimental.pallas import tpu as pltpu
from jax.sharding import PartitionSpec as P

SAMPLES = 7680
FREQS = 1200
FIRST_BIN = 32
LAGS = 256
SMOOTH = 4
PARTNERS = 4
REACH = 7
BLOCK = 256
WINDOWS = 2
WATER = 0.3
RESCALE = 2.0

RADIX = 10
PART = SAMPLES // RADIX
HALF = BLOCK // 2
PER = FREQS // RADIX
LANES = 128
WIDE = RADIX * 2 * LANES
ORDER = (0, 5, 2, 8, 4, 6, 3, 7, 1, 9)
PAIRS = len(ORDER) // 2 - 1
PLANE = 16
INNER = PLANE - REACH
MINE = HALF // PLANE
CHUNKS = 4
VMEM = 56 * 1024 * 1024


def residue_bins(residue):
    first = (residue - FIRST_BIN) % RADIX
    return FIRST_BIN + first + RADIX * np.arange(PER)


def place_in_band(residue):
    return (residue - FIRST_BIN) % RADIX


def angles(steps, residue):
    phase = steps[:, None] * residue_bins(residue)[None, :] % SAMPLES
    angle = phase * (2.0 * math.pi / SAMPLES)
    fill = ((0, 0), (0, LANES - PER))
    return np.concatenate([np.pad(np.cos(angle), fill), np.pad(-np.sin(angle), fill)], axis=1)


def dft_table():
    columns = [angles(np.arange(PART), residue) for residue in ORDER]
    chunks = [np.concatenate(columns[i : i + 2], axis=1) for i in range(0, RADIX, 2)]
    return np.stack(chunks).astype(np.float32).astype(ml_dtypes.bfloat16)


def lag_tables():
    lag_steps = np.arange(LAGS) - LAGS // 2 + SAMPLES
    factor = RESCALE / math.sqrt(FREQS * WINDOWS)
    table = np.concatenate([angles(lag_steps, residue).T for residue in ORDER]) * factor
    table = table.astype(np.float32)
    high = table.astype(ml_dtypes.bfloat16)
    low = (table - high.astype(np.float32)).astype(ml_dtypes.bfloat16)
    return high, low


def taper_columns(taper):
    parts = jnp.pad((taper * taper).reshape(PER, RADIX).T, ((0, 0), (0, LANES - PER)))
    return jnp.stack([parts[place_in_band(residue)] for residue in ORDER])


def five_point(x):
    cos = [math.cos(2.0 * math.pi * k / 5) for k in (1, 2)]
    sin = [math.sin(2.0 * math.pi * k / 5) for k in (1, 2)]
    near, far = x[1] + x[4], x[2] + x[3]
    near_gap, far_gap = x[1] - x[4], x[2] - x[3]
    return (
        x[0] + near + far,
        x[0] + cos[0] * near + cos[1] * far,
        sin[0] * near_gap + sin[1] * far_gap,
        x[0] + cos[1] * near + cos[0] * far,
        sin[1] * near_gap - sin[0] * far_gap,
    )


def dft_kernel(
    pairs_ref, x_hbm, table_hbm, mine_ref, theirs_ref, x_ref, table_ref, y_ref, real_ref, pair_ref, x_sems, t_sems
):
    core = lax.axis_index("tm")
    block = lax.axis_index("row") * PLANE + lax.axis_index("col")
    size = BLOCK // CHUNKS
    x_copies = [
        pltpu.make_async_copy(
            x_hbm.at[pl.ds(c * size, size)], x_ref.at[pl.ds(c * size, size)], x_sems.at[c]
        )
        for c in range(CHUNKS)
    ]
    t_copies = [
        pltpu.make_async_copy(table_hbm.at[c], table_ref.at[c], t_sems.at[c])
        for c in range(PAIRS + 1)
    ]
    for copy in x_copies + t_copies:
        copy.start()

    def split(i, carry):
        at = pl.ds(pl.multiple_of(i * 16, 16), 16)
        for lane in range(0, PART, LANES):
            x = [
                x_ref[at, n * PART + lane : n * PART + lane + LANES].astype(jnp.float32)
                for n in range(RADIX)
            ]
            even = five_point([x[n] + x[n + 5] for n in range(5)])
            odd = five_point([x[n] - x[n + 5] if n % 2 == 0 else x[n + 5] - x[n] for n in range(5)])
            parts = (even[0], odd[0]) + even[1:] + odd[1:3] + odd[3:]
            for n, part in enumerate(parts):
                y_ref[
                    pl.ds(pl.multiple_of(n * BLOCK + i * 16, 16), 16), lane : lane + LANES
                ] = part.astype(jnp.bfloat16)
        return carry

    for c in range(CHUNKS):
        x_copies[c].wait()
        lax.fori_loop(c * size // 16, (c + 1) * size // 16, split, 0)

    t_copies[0].wait()
    for n in range(2):
        real_ref[n] = jnp.dot(
            y_ref[n * BLOCK : (n + 1) * BLOCK, :],
            table_ref[0, :, n * 2 * LANES : (n + 1) * 2 * LANES],
            preferred_element_type=jnp.float32,
        )
    for n in range(PAIRS):
        t_copies[n + 1].wait()
        pair_ref[n] = jnp.dot(
            y_ref[(n + 1) * 2 * BLOCK : (n + 2) * 2 * BLOCK, :],
            table_ref[n + 1],
            preferred_element_type=jnp.float32,
        )

    lane = lax.broadcasted_iota(jnp.int32, (16, LANES), 1)
    offsets = jnp.zeros((16, LANES), jnp.float32)
    for k in range(PARTNERS):
        partner = pairs_ref[0, k]
        offset = jnp.where(partner < 0, 0, partner - block).astype(jnp.float32)
        offsets = jnp.where(lane == PER + k, offset, offsets)

    def white_rows(row):
        at = pl.ds(pl.multiple_of(row, 16), 16)
        under = pl.ds(pl.multiple_of(row + BLOCK, 16), 16)
        spectrum = [(real_ref[n, at, :LANES], real_ref[n, at, LANES:]) for n in range(2)]
        for n in range(PAIRS):
            for side, way in ((0, 1.0), (1, -1.0)):
                if n >= PAIRS // 2:
                    way = -way
                first = slice(2 * side * LANES, (2 * side + 1) * LANES)
                second = slice((2 * side + 1) * LANES, (2 * side + 2) * LANES)
                u_cos, u_sin = pair_ref[n, at, first], pair_ref[n, at, second]
                v_cos, v_sin = pair_ref[n, under, first], pair_ref[n, under, second]
                spectrum.append((u_cos + way * v_sin, u_sin - way * v_cos))
        band = [None] * RADIX
        for residue, (re, im) in zip(ORDER, spectrum):
            square = re * re + im * im
            band[place_in_band(residue)] = square * lax.rsqrt(jnp.maximum(square, 1e-30))
        total = band[0]
        for amplitude in band[1:]:
            total = total + amplitude
        floor = WATER / FREQS * jnp.sum(total, axis=1, keepdims=True) + 1e-05
        line = [pltpu.roll(a, 1, 1) for a in band[RADIX - SMOOTH :]]
        line = line + band + [pltpu.roll(a, LANES - 1, 1) for a in band[:SMOOTH]]
        two = [line[i] + line[i + 1] for i in range(len(line) - 1)]
        four = [two[i] + two[i + 2] for i in range(len(two) - 2)]
        out = []
        for residue, (re, im) in zip(ORDER, spectrum):
            i = place_in_band(residue)
            smoothed = (four[i] + four[i + 4] + line[i + 8]) * (1.0 / (2 * SMOOTH + 1))
            level = smoothed + floor
            scale = pl.reciprocal(level, approx=True)
            scale = scale * (2.0 - level * scale)
            out.append((re * scale, im * scale))
        first = jnp.where(lane >= PER, offsets, out[0][0])
        out[0] = (first, out[0][1])
        return out

    def theirs(i, carry):
        for n, parts in enumerate(white_rows((1 - core) * HALF + i * 16)):
            for side, part in enumerate(parts):
                here = (2 * n + side) * LANES
                theirs_ref[pl.ds(pl.multiple_of(i * 16, 16), 16), here : here + LANES] = (
                    part.astype(jnp.bfloat16)
                )
        return carry

    def mine(i, carry):
        for n, parts in enumerate(white_rows(core * HALF + i * 16)):
            for side, part in enumerate(parts):
                here = (2 * n + side) * LANES
                for j in range(2):
                    rows = part[j * MINE : (j + 1) * MINE]
                    mine_ref[i * 2 + j, :, here : here + LANES] = jnp.concatenate(
                        [rows, rows], axis=0
                    ).astype(jnp.bfloat16)
        return carry

    lax.fori_loop(0, HALF // 16, theirs, 0)
    lax.fori_loop(0, HALF // 16, mine, 0)


def whitened(series, pairs):
    hbm = pl.BlockSpec(memory_space=pl.ANY)
    vmem = pl.BlockSpec(memory_space=pltpu.VMEM)
    return pl.pallas_call(
        dft_kernel,
        in_specs=[pl.BlockSpec(memory_space=pltpu.SMEM), hbm, hbm],
        out_specs=[vmem, vmem],
        out_shape=[
            jax.ShapeDtypeStruct((PLANE, 2 * MINE, WIDE), jnp.bfloat16),
            jax.ShapeDtypeStruct((HALF, WIDE), jnp.bfloat16),
        ],
        scratch_shapes=[
            pltpu.VMEM((BLOCK, SAMPLES), jnp.bfloat16),
            pltpu.VMEM((PAIRS + 1, PART, 4 * LANES), jnp.bfloat16),
            pltpu.VMEM((RADIX * BLOCK, PART), jnp.bfloat16),
            pltpu.VMEM((2, BLOCK, 2 * LANES), jnp.float32),
            pltpu.VMEM((PAIRS, 2 * BLOCK, 4 * LANES), jnp.float32),
            pltpu.SemaphoreType.DMA((CHUNKS,)),
            pltpu.SemaphoreType.DMA((PAIRS + 1,)),
        ],
        compiler_params=pltpu.CompilerParams(vmem_limit_bytes=VMEM),
        name="dft_whiten",
    )(pairs, series, jnp.asarray(dft_table()))


def corr_kernel(
    first_block,
    count,
    with_halo,
    taper_ref,
    plane_ref,
    *refs,
):
    if with_halo:
        halo_ref, high_ref, low_ref, done_ref, out_ref = refs[:5]
        refs = refs[5:]
    else:
        high_ref, low_ref, out_ref = refs[:3]
        refs = refs[3:]
    w_ref, xh_ref, xl_ref, lag_ref, number_ref, scalar_ref, sems = refs
    inside = PLANE - first_block
    copies = [
        pltpu.make_async_copy(
            plane_ref.at[pl.ds(first_block, inside)], w_ref.at[pl.ds(0, inside)], sems.at[0]
        )
    ]
    if with_halo:
        copies.append(
            pltpu.make_async_copy(halo_ref, w_ref.at[pl.ds(inside, REACH)], sems.at[1])
        )
    for copy in copies:
        copy.start()
    for copy in copies:
        copy.wait()
    for a in range(count):
        number_ref[a : a + 1, :] = (
            w_ref[a, :, :LANES].astype(jnp.float32)[:1].astype(jnp.int32)
        )
    numbers = pltpu.make_async_copy(number_ref, scalar_ref, sems.at[2])
    numbers.start()
    numbers.wait()

    def one_block(a, carry):
        seconds = [a + scalar_ref[a, PER + k] for k in range(PARTNERS)]
        for n in range(RADIX):
            here = 2 * n * LANES

            def load(index):
                both = w_ref[index, :, here : here + 2 * LANES].astype(jnp.float32)
                return [
                    (both[w * MINE : (w + 1) * MINE, :LANES], both[w * MINE : (w + 1) * MINE, LANES:])
                    for w in range(WINDOWS)
                ]

            taper = taper_ref[n : n + 1, :]
            first = [(re * taper, im * taper) for re, im in load(a)]
            for slot in range(0, PARTNERS, 2):
                at = pl.ds(pl.multiple_of((a * PARTNERS + slot) * MINE, 16), 2 * MINE)
                re, im = [], []
                for k in (slot, slot + 1):
                    (a_re, a_im), (c_re, c_im) = first
                    (b_re, b_im), (d_re, d_im) = load(seconds[k])
                    re.append((a_re * b_re + a_im * b_im) + (c_re * d_re + c_im * d_im))
                    im.append((a_im * b_re - a_re * b_im) + (c_im * d_re - c_re * d_im))
                for side, both in enumerate((re, im)):
                    cross = jnp.concatenate(both, axis=0)
                    high = cross.astype(jnp.bfloat16)
                    columns = slice(here + side * LANES, here + (side + 1) * LANES)
                    xh_ref[at, columns] = high
                    xl_ref[at, columns] = (cross - high.astype(jnp.float32)).astype(jnp.bfloat16)
        return carry

    lax.fori_loop(0, count, one_block, 0)
    lagged = jnp.dot(xh_ref[...], high_ref[...], preferred_element_type=jnp.float32)
    lagged += jnp.dot(xh_ref[...], low_ref[...], preferred_element_type=jnp.float32)
    lagged += jnp.dot(xl_ref[...], high_ref[...], preferred_element_type=jnp.float32)
    lag_ref[...] = lagged.reshape(lag_ref.shape)

    def mask(a, carry):
        for k in range(PARTNERS):

            @pl.when(scalar_ref[a, PER + k] == 0)
            def clear():
                lag_ref[a * PARTNERS + k] = jnp.zeros((MINE, LAGS), jnp.float32)

        return carry

    lax.fori_loop(0, count, mask, 0)
    write = pltpu.make_async_copy(
        lag_ref, out_ref.at[pl.ds(first_block * PARTNERS, count * PARTNERS)], sems.at[0]
    )
    write.start()
    write.wait()


def correlated(taper, plane, halo=None, done=None):
    high, low = lag_tables()
    with_halo = halo is not None
    first_block, count = (INNER, REACH) if with_halo else (0, INNER)
    held = PLANE + REACH - first_block if with_halo else PLANE
    rows = count * PARTNERS * MINE
    vmem = pl.BlockSpec(memory_space=pltpu.VMEM)
    hbm = pl.BlockSpec(memory_space=pl.ANY)
    operands = [taper, plane] + ([halo] if with_halo else []) + [jnp.asarray(high), jnp.asarray(low)]
    specs = [vmem, hbm] + ([hbm] if with_halo else []) + [vmem, vmem]
    aliases = {}
    if with_halo:
        aliases = {len(operands): 0}
        operands.append(done)
        specs.append(hbm)

    def body(*refs):
        corr_kernel(first_block, count, with_halo, *refs)

    return pl.pallas_call(
        body,
        in_specs=specs,
        out_specs=hbm,
        out_shape=jax.ShapeDtypeStruct((PLANE * PARTNERS, MINE, LAGS), jnp.float32),
        scratch_shapes=[
            pltpu.VMEM((held, 2 * MINE, WIDE), jnp.bfloat16),
            pltpu.VMEM((rows, WIDE), jnp.bfloat16),
            pltpu.VMEM((rows, WIDE), jnp.bfloat16),
            pltpu.VMEM((count * PARTNERS, MINE, LAGS), jnp.float32),
            pltpu.VMEM((PLANE, LANES), jnp.int32),
            pltpu.SMEM((PLANE, LANES), jnp.int32),
            pltpu.SemaphoreType.DMA((3,)),
        ],
        input_output_aliases=aliases,
        compiler_params=pltpu.CompilerParams(vmem_limit_bytes=VMEM),
        cost_estimate=pl.CostEstimate(
            flops=6 * rows * WIDE * LAGS, bytes_accessed=4 << 20, transcendentals=0
        ),
        name="correlate_halo" if with_halo else "correlate_inner",
    )(*operands)


def per_device(records, taper, pairs):
    mine, theirs = whitened(records[0], pairs)
    got = lax.ppermute(theirs, "tm", [(0, 1), (1, 0)])
    send = mine.at[:, MINE:].set(got.reshape(PLANE, MINE, WIDE))
    plane = lax.all_to_all(send, "col", 0, 0, tiled=True)
    count = lax.axis_size("row")
    halo = lax.ppermute(plane[:REACH], "row", [(z, z - 1) for z in range(1, count)])
    plane, taper = lax.optimization_barrier((plane, taper))
    squared = taper_columns(taper)
    lagged = correlated(squared, plane)
    lagged = correlated(squared, plane, halo, lagged)
    lagged = lagged.reshape(PLANE, PARTNERS, MINE, LAGS)
    back = lax.all_to_all(lagged, "col", 0, 0, tiled=True)
    return back.transpose(1, 0, 2, 3).reshape(1, PARTNERS, HALF, LAGS)


def solution(mesh):
    return jax.shard_map(
        per_device,
        mesh=mesh,
        in_specs=(P("tm", ("row", "col"), None), P(), P(("row", "col"), None)),
        out_specs=P(("row", "col"), None, "tm", None),
        check_vma=False,
    )
```

time: 673 us -> 80.8 us (0.12)
  waiting for transfers between devices: 274 us -> 8.04 us
  other arithmetic: 210 us -> 0.01 us
  matrix products: 83.8 us -> 0 us
  blocking collectives: 0 us -> 41.2 us
  loops' own time: 31.5 us -> 0 us
  local copies, waits for them, and re-layouts: 33.1 us -> 4.05 us
  Pallas kernels: 0 us -> 24.9 us
  starting transfers between devices: 22.7 us -> 2.11 us
  between operations: 13.6 us -> 0.08 us
    ppermute x7 -> x2, waiting for transfers between devices: 253 us -> 8.04 us  [the longest x1 5.74 us: per_device(): lax.ppermute(plane[:REACH], 'row', [(z, z - 1) for z in range(1, count)])]
    another operation x16 -> x0, other arithmetic: 184 us -> none
    dot_general x16 -> x0, matrix products: 83.8 us -> none  [the longest x15 66.9 us: advance(): jnp.dot(piece, dft_table(start, block_len, freqs), preferred_element_type...]
    all_to_all x0 -> x2, blocking collectives: none -> 41.2 us  [the longest x1 27.2 us: per_device(): plane = lax.all_to_all(send, 'col', 0, 0, tiled=True)]
    another operation x1 -> x0, loops' own time: 31.5 us -> none  [spectra(): lax.scan(advance, jnp.zeros((series.shape[0], 2 * FREQS), jnp.float32), s...]
    pallas_call x0 -> x3, Pallas kernels: none -> 24.9 us  [the longest x2 14.5 us: correlated(): pl.pallas_call(body, in_specs=specs, out_specs=hbm, out_shape=jax.ShapeDt...]
    reduce_scatter x1 -> x0, waiting for transfers between devices: 21 us -> none  [per_device(): stacked = lax.psum_scatter(lagged, 'tm', scatter_dimension=1, tiled=True)]
    ppermute x7 -> x2, starting transfers between devices: 22.7 us -> 2.11 us  [the longest x1 2.02 us: per_device(): lax.ppermute(plane[:REACH], 'row', [(z, z - 1) for z in range(1, count)])]
  transfers between devices with their start and end apart: 8 -> 2, of which waited for: 7 -> 2; matrix products, arithmetic and copies ran while one was open for 4% -> 2% of each run, Pallas kernels for 0% -> 10%
where the time goes in v2:
time: 80.8 us; the launch traced here: 80.4 us
  blocking collectives  41.2 us (51%)
  Pallas kernels  24.9 us (31%)
  waiting for transfers between devices  8.04 us (10%)
  local copies, waits for them, and re-layouts  4.05 us (5%)
  starting transfers between devices  2.11 us (3%)
    all_to_all x1, blocking collectives, per_device(): plane = lax.all_to_all(send, 'col', 0, 0, tiled=True)  27.2 us
    pallas_call x2, Pallas kernels, correlated(): pl.pallas_call(body, in_specs=specs, out_specs=hbm, out_shape=jax.ShapeDt...  14.5 us
    all_to_all x1, blocking collectives, per_device(): back = lax.all_to_all(lagged, 'col', 0, 0, tiled=True)  14 us
    pallas_call x1, Pallas kernels, whitened(): pl.pallas_call(dft_kernel, in_specs=[pl.BlockSpec(memory_space=pltpu.SMEM...  10.4 us
    ppermute x1, waiting for transfers between devices, per_device(): lax.ppermute(plane[:REACH], 'row', [(z, z - 1) for z in range(1, count)])  5.74 us
    ppermute x1, waiting for transfers between devices, per_device(): got = lax.ppermute(theirs, 'tm', [(0, 1), (1, 0)])  2.3 us
    ppermute x1, starting transfers between devices, per_device(): lax.ppermute(plane[:REACH], 'row', [(z, z - 1) for z in range(1, count)])  2.02 us
  transfers between devices with their start and end apart: 2, of which 2 were waited for; matrix products, arithmetic and copies ran while one was open for 2% of the time, Pallas kernels for 10%

profile of v2, /device:TPU:96, one launch (start us, length us, event | category | flops | bytes accessed | tf_op | source)
XLA Modules:
  0.0 80.4 jit_solution(11682582463168467636)
XLA Ops:
  0.0 10.4 %dft_whiten.1 = (bf16[16,16,2560]{2,1,0:T(8,128)(2,1)}, bf16[128,2560]{1,0:T(8,128)(2,1)}) custom-call(s32[1,4]{1,0:T(1,128)} %pairs_ref.1, bf16[256,7680]{1,0:T(8,128)(2,1)} %bitcast.11, bf16[5,768,512]{2,1,0:T(8,128)(2,1)} %constant.38.clone.table_hbm), custom_call_target="tpu_custom_call" | custom-call | tf_op jit(solution)/shard_map/dft_whiten/pallas_call | solution.py:215
  10.4 0.1 collective-permute-start
  10.5 2.3 %collective-permute-done = bf16[128,2560]{1,0:T(8,128)(2,1)S(1)} collective-permute-done((bf16[128,2560]{1,0:T(8,128)(2,1)}, bf16[128,2560]{1,0:T(8,128)(2,1)S(1)}, u32[]{:S(2)}, u32[]{:S(2)}) %collective-permute-start) | collective-permute-done | bytes 655392 | tf_op jit(solution)/shard_map/ppermute | solution.py:371
  12.8 0.9 %bitcast_dynamic-update-slice_fusion = bf16[16,16,2560]{2,1,0:T(8,128)(2,1)} fusion(bf16[16,16,2560]{2,1,0:T(8,128)(2,1)} %get-tuple-element.21, bf16[128,2560]{1,0:T(8,128)(2,1)S(1)} %collective-permute-done), kind=kLoop, calls=%fused_computation | loop fusion | bytes 1310720 | tf_op jit(solution)/shard_map/scatter | solution.py:372
  13.7 0.0 copy-start.2
  13.7 27.2 %all_to_all.10.refs_1_ = bf16[16,16,2560]{2,1,0:T(8,128)(2,1)S(1)} all-to-all(bf16[16,16,2560]{2,1,0:T(8,128)(2,1)} %bitcast_dynamic-update-slice_fusion), channel_id=1, replica_groups=mesh['row'=8,'col'=16,'tm'=2] {'col'}, dimensions={0} | all-to-all | bytes 2621440 | tf_op jit(solution)/shard_map/all_to_all | solution.py:373
  40.9 0.0 copy-start
  41.0 2.0 %collective-permute-start.1 = (bf16[7,16,2560]{2,1,0:T(8,128)(2,1)S(1)}, bf16[7,16,2560]{2,1,0:T(8,128)(2,1)S(1)}, u32[]{:S(2)}, u32[]{:S(2)}) collective-permute-start(bf16[7,16,2560]{2,1,0:T(8,128)(2,1)S(1)} %slice.66), channel_id=1, source_target_pairs={{32,0},{64,32},{96,64},{128,96},{160,128},{192,160},{224,192},{33,... | collective-permute-start | bytes 1720328 | tf_op jit(solution)/shard_map/ppermute | solution.py:375
  43.0 0.0 copy-done.2
  43.0 0.1 reshape.44
  43.2 0.1 copy.11
  43.3 1.2 %stack.3.refs_0_ = f32[10,128]{1,0:T(8,128)} concatenate(f32[1,128]{1,0:T(1,128)S(1)} %get-tuple-element.34, f32[1,128]{1,0:T(1,128)S(1)} %get-tuple-element.26, f32[1,128]{1,0:T(1,128)S(1)} %get-tuple-element.27, f32[1,128]{1,0:T(1,128)S(1)} %get-tuple-element.28, f32[1,128]{1,0:T(1,128)S(1)} %get-tuple-element.29, f32[1,128]{1,0:T(1,128)S(1)} %get-tuple-element.30, ...), dimensions={0} | concatenate | bytes 10240 | tf_op jit(solution)/shard_map/stack | solution.py:73
  44.5 0.0 copy-done
  44.5 7.6 %correlate_inner.1.refs_5_ = f32[64,8,256]{2,1,0:T(8,128)} custom-call(f32[10,128]{1,0:T(8,128)} %stack.3.refs_0_, bf16[16,16,2560]{2,1,0:T(8,128)(2,1)} %copy-done, bf16[2560,256]{1,0:T(8,128)(2,1)} %constant.39.clone.refs_2_.refs_3_, bf16[2560,256]{1,0:T(8,128)(2,1)} %constant.40.clone.refs_3_.refs_4_), custom_call_target="tpu_custom_call" | custom-call | flops 1132462080 | bytes 4194304 | tf_op jit(solution)/shard_map/correlate_inner/pallas_call | solution.py:346
  52.1 5.7 %collective-permute-done.1.refs_2_ = bf16[7,16,2560]{2,1,0:T(8,128)(2,1)S(1)} collective-permute-done((bf16[7,16,2560]{2,1,0:T(8,128)(2,1)S(1)}, bf16[7,16,2560]{2,1,0:T(8,128)(2,1)S(1)}, u32[]{:S(2)}, u32[]{:S(2)}) %collective-permute-start.1) | collective-permute-done | bytes 573472 | tf_op jit(solution)/shard_map/ppermute | solution.py:375
  57.9 0.0 copy-start.1
  57.9 0.8 %copy-done.1 = bf16[7,16,2560]{2,1,0:T(8,128)(2,1)} copy-done((bf16[7,16,2560]{2,1,0:T(8,128)(2,1)}, bf16[7,16,2560]{2,1,0:T(8,128)(2,1)S(1)}, u32[]{:S(2)}) %copy-start.1) | copy-done | bytes 573464
  58.7 6.9 %correlate_halo.1 = f32[64,8,256]{2,1,0:T(8,128)} custom-call(f32[10,128]{1,0:T(8,128)} %stack.3.refs_0_, bf16[16,16,2560]{2,1,0:T(8,128)(2,1)} %copy-done, bf16[7,16,2560]{2,1,0:T(8,128)(2,1)} %copy-done.1, bf16[2560,256]{1,0:T(8,128)(2,1)} %constant.39.clone.refs_2_.refs_3_, ...), custom_call_target="tpu_custom_call", output_to_operand_aliasing={{}: (5, {})} | custom-call | flops 880803840 | bytes 4194304 | tf_op jit(solution)/shard_map/correlate_halo/pallas_call | solution.py:346
  65.6 14.0 %all_to_all.11 = f32[16,4,8,256]{3,2,1,0:T(8,128)S(1)} all-to-all(f32[16,4,8,256]{3,2,1,0:T(8,128)} %bitcast.10), channel_id=1, replica_groups=mesh['row'=8,'col'=16,'tm'=2] {'col'}, dimensions={0} | all-to-all | bytes 1048576 | tf_op jit(solution)/shard_map/all_to_all | solution.py:381
  79.6 0.8 %copy_bitcast_fusion = f32[1,4,128,256]{3,2,1,0:T(8,128)} fusion(f32[16,4,8,256]{3,2,1,0:T(8,128)S(1)} %all_to_all.11), kind=kLoop, calls=%fused_computation.1 | loop fusion | bytes 1048576 | tf_op jit(solution)/shard_map/reshape | solution.py:382
  (3 shorter events, 0.1 us)
Async XLA Ops:
  10.4 2.4 %collective-permute-start = (bf16[128,2560]{1,0:T(8,128)(2,1)}, bf16[128,2560]{1,0:T(8,128)(2,1)S(1)}, u32[]{:S(2)}, u32[]{:S(2)}) collective-permute-start(bf16[128,2560]{1,0:T(8,128)(2,1)} %get-tuple-element.22), channel_id=1, source_target_pairs={{0,1},{1,0},{2,3},{3,2},{4,5},{5,4},{6,7},{7,6},{8,9},{9,8},{10,11... | collective-permute-start | bytes 1966088 | tf_op jit(solution)/shard_map/ppermute | solution.py:371
  13.7 29.3 %copy-start.2 = (f32[1200]{0:T(1024)S(1)}, f32[1200]{0:T(1024)}, u32[]{:S(2)}) copy-start(f32[1200]{0:T(1024)} %param.11) | copy-start | bytes 14404
  40.9 3.5 %copy-start = (bf16[16,16,2560]{2,1,0:T(8,128)(2,1)}, bf16[16,16,2560]{2,1,0:T(8,128)(2,1)S(1)}, u32[]{:S(2)}) copy-start(bf16[16,16,2560]{2,1,0:T(8,128)(2,1)S(1)} %all_to_all.10.refs_1_) | copy-start | bytes 3932164
  41.0 16.9 %collective-permute-start.1 = (bf16[7,16,2560]{2,1,0:T(8,128)(2,1)S(1)}, bf16[7,16,2560]{2,1,0:T(8,128)(2,1)S(1)}, u32[]{:S(2)}, u32[]{:S(2)}) collective-permute-start(bf16[7,16,2560]{2,1,0:T(8,128)(2,1)S(1)} %slice.66), channel_id=1, source_target_pairs={{32,0},{64,32},{96,64},{128,96},{160,128},{192,160},{224,192},{33,... | collective-permute-start | bytes 1720328 | tf_op jit(solution)/shard_map/ppermute | solution.py:375
  57.9 0.8 %copy-start.1 = (bf16[7,16,2560]{2,1,0:T(8,128)(2,1)}, bf16[7,16,2560]{2,1,0:T(8,128)(2,1)S(1)}, u32[]{:S(2)}) copy-start(bf16[7,16,2560]{2,1,0:T(8,128)(2,1)S(1)} %collective-permute-done.1.refs_2_) | copy-start | bytes 1720324

commit v3 on v2

v3 whole, which is shorter than its diff:
```python
import math

import jax
import jax.numpy as jnp
import ml_dtypes
import numpy as np
from jax import lax
from jax.experimental import pallas as pl
from jax.experimental.pallas import tpu as pltpu
from jax.sharding import PartitionSpec as P

SAMPLES = 7680
FREQS = 1200
FIRST_BIN = 32
LAGS = 256
SMOOTH = 4
PARTNERS = 4
REACH = 7
BLOCK = 256
WINDOWS = 2
WATER = 0.3
RESCALE = 2.0

RADIX = 10
PART = SAMPLES // RADIX
HALF = BLOCK // 2
PER = FREQS // RADIX
LANES = 128
WIDE = RADIX * 2 * LANES
ORDER = (0, 5, 2, 8, 4, 6, 3, 7, 1, 9)
PAIRS = len(ORDER) // 2 - 1
PLANE = 16
INNER = PLANE - REACH
MINE = HALF // PLANE
CHUNKS = 4


def residue_bins(residue):
    first = (residue - FIRST_BIN) % RADIX
    return FIRST_BIN + first + RADIX * np.arange(PER)


def place_in_band(residue):
    return (residue - FIRST_BIN) % RADIX


def angles(steps, residue):
    phase = steps[:, None] * residue_bins(residue)[None, :] % SAMPLES
    angle = phase * (2.0 * math.pi / SAMPLES)
    fill = ((0, 0), (0, LANES - PER))
    return np.concatenate([np.pad(np.cos(angle), fill), np.pad(-np.sin(angle), fill)], axis=1)


def dft_table():
    columns = [angles(np.arange(PART), residue) for residue in ORDER]
    chunks = [np.concatenate(columns[i : i + 2], axis=1) for i in range(0, RADIX, 2)]
    return np.stack(chunks).astype(np.float32).astype(ml_dtypes.bfloat16)


def lag_tables():
    lag_steps = np.arange(LAGS) - LAGS // 2 + SAMPLES
    factor = RESCALE / math.sqrt(FREQS * WINDOWS)
    table = np.concatenate([angles(lag_steps, residue).T for residue in ORDER]) * factor
    table = table.astype(np.float32)
    high = table.astype(ml_dtypes.bfloat16)
    low = (table - high.astype(np.float32)).astype(ml_dtypes.bfloat16)
    return high, low


def taper_columns(taper):
    parts = jnp.pad((taper * taper).reshape(PER, RADIX).T, ((0, 0), (0, LANES - PER)))
    return jnp.stack([parts[place_in_band(residue)] for residue in ORDER])


def five_point(x):
    cos = [math.cos(2.0 * math.pi * k / 5) for k in (1, 2)]
    sin = [math.sin(2.0 * math.pi * k / 5) for k in (1, 2)]
    near, far = x[1] + x[4], x[2] + x[3]
    near_gap, far_gap = x[1] - x[4], x[2] - x[3]
    return (
        x[0] + near + far,
        x[0] + cos[0] * near + cos[1] * far,
        sin[0] * near_gap + sin[1] * far_gap,
        x[0] + cos[1] * near + cos[0] * far,
        sin[1] * near_gap - sin[0] * far_gap,
    )


def dft_kernel(
    x_hbm, table_hbm, theirs_ref, real_ref, pair_ref, x_ref, table_ref, y_ref, x_sems, t_sems
):
    core = lax.axis_index("tm")
    size = BLOCK // CHUNKS
    x_copies = [
        pltpu.make_async_copy(
            x_hbm.at[pl.ds(c * size, size)], x_ref.at[pl.ds(c * size, size)], x_sems.at[c]
        )
        for c in range(CHUNKS)
    ]
    t_copies = [
        pltpu.make_async_copy(table_hbm.at[c], table_ref.at[c], t_sems.at[c])
        for c in range(PAIRS + 1)
    ]
    for copy in x_copies:
        copy.start()

    def split(i, carry):
        at = pl.ds(pl.multiple_of(i * 16, 16), 16)
        for lane in range(0, PART, LANES):
            x = [
                x_ref[at, n * PART + lane : n * PART + lane + LANES].astype(jnp.float32)
                for n in range(RADIX)
            ]
            even = five_point([x[n] + x[n + 5] for n in range(5)])
            odd = five_point([x[n] - x[n + 5] if n % 2 == 0 else x[n + 5] - x[n] for n in range(5)])
            parts = (even[0], odd[0]) + even[1:] + odd[1:]
            for n, part in enumerate(parts):
                y_ref[
                    pl.ds(pl.multiple_of(n * BLOCK + i * 16, 16), 16), lane : lane + LANES
                ] = part.astype(jnp.bfloat16)
        return carry

    for c in range(CHUNKS):
        x_copies[c].wait()
        if c == CHUNKS - 2:
            for copy in t_copies:
                copy.start()
        lax.fori_loop(c * size // 16, (c + 1) * size // 16, split, 0)

    t_copies[0].wait()
    for n in range(2):
        real_ref[n] = jnp.dot(
            y_ref[n * BLOCK : (n + 1) * BLOCK, :],
            table_ref[0, :, n * 2 * LANES : (n + 1) * 2 * LANES],
            preferred_element_type=jnp.float32,
        )
    for n in range(PAIRS):
        t_copies[n + 1].wait()
        pair_ref[n] = jnp.dot(
            y_ref[(n + 1) * 2 * BLOCK : (n + 2) * 2 * BLOCK, :],
            table_ref[n + 1],
            preferred_element_type=jnp.float32,
        )

    def rows(i, carry):
        row = (1 - core) * HALF + i * 16
        parts = [white_rows(real_ref, pair_ref, row + j * MINE) for j in range(2)]
        for n in range(2 * RADIX):
            theirs_ref[pl.ds(pl.multiple_of(i * 16, 16), 16), n * LANES : (n + 1) * LANES] = (
                jnp.concatenate([parts[0][n], parts[1][n]], axis=0).astype(jnp.bfloat16)
            )
        return carry

    lax.fori_loop(0, HALF // 16, rows, 0)


def spectrum_part(real_ref, pair_ref, row, place):
    at = pl.ds(pl.multiple_of(row, MINE), MINE)
    if place < 2:
        return real_ref[place, at, :LANES], real_ref[place, at, LANES:]
    n, side = (place - 2) // 2, place % 2
    plain = (side == 0) == (n < PAIRS // 2)
    under = pl.ds(pl.multiple_of(row + BLOCK, MINE), MINE)
    first = slice(2 * side * LANES, (2 * side + 1) * LANES)
    second = slice((2 * side + 1) * LANES, (2 * side + 2) * LANES)
    u_cos, u_sin = pair_ref[n, at, first], pair_ref[n, at, second]
    v_cos, v_sin = pair_ref[n, under, first], pair_ref[n, under, second]
    if plain:
        return u_cos + v_sin, u_sin - v_cos
    return u_cos - v_sin, u_sin + v_cos


def white_rows(real_ref, pair_ref, row):
    band = [None] * RADIX
    for place, residue in enumerate(ORDER):
        re, im = spectrum_part(real_ref, pair_ref, row, place)
        square = re * re + im * im
        band[place_in_band(residue)] = square * lax.rsqrt(jnp.maximum(square, 1e-30))
    total = band[0]
    for amplitude in band[1:]:
        total = total + amplitude
    floor = WATER / FREQS * jnp.sum(total, axis=1, keepdims=True) + 1e-05
    line = [pltpu.roll(a, 1, 1) for a in band[RADIX - SMOOTH :]]
    line = line + band + [pltpu.roll(a, LANES - 1, 1) for a in band[:SMOOTH]]
    two = [line[i] + line[i + 1] for i in range(len(line) - 1)]
    four = [two[i] + two[i + 2] for i in range(len(two) - 2)]
    out = []
    for place, residue in enumerate(ORDER):
        i = place_in_band(residue)
        smoothed = (four[i] + four[i + 4] + line[i + 8]) * (1.0 / (2 * SMOOTH + 1))
        level = smoothed + floor
        scale = pl.reciprocal(level, approx=True)
        scale = scale * (2.0 - level * scale)
        re, im = spectrum_part(real_ref, pair_ref, row, place)
        out += [re * scale, im * scale]
    return out


def own_kernel(pairs_ref, real_ref, pair_ref, mine_ref):
    core = lax.axis_index("tm")
    block = lax.axis_index("row") * PLANE + lax.axis_index("col")
    lane = lax.broadcasted_iota(jnp.int32, (MINE, LANES), 1)
    offsets = jnp.zeros((MINE, LANES), jnp.float32)
    for k in range(PARTNERS):
        partner = pairs_ref[0, k]
        offset = jnp.where(partner < 0, 0, partner - block).astype(jnp.float32)
        offsets = jnp.where(lane == PER + k, offset, offsets)

    def rows(j, carry):
        parts = white_rows(real_ref, pair_ref, core * HALF + j * MINE)
        parts[0] = jnp.where(lane >= PER, offsets, parts[0])
        for n, part in enumerate(parts):
            mine_ref[j, :, n * LANES : (n + 1) * LANES] = jnp.concatenate(
                [part, part], axis=0
            ).astype(jnp.bfloat16)
        return carry

    lax.fori_loop(0, PLANE, rows, 0)


def in_vmem(array):
    return pltpu.with_memory_space_constraint(array, pltpu.VMEM)


def spectra(series):
    hbm = pl.BlockSpec(memory_space=pltpu.HBM)
    vmem = pl.BlockSpec(memory_space=pltpu.VMEM)
    return pl.pallas_call(
        dft_kernel,
        in_specs=[hbm, hbm],
        out_specs=[vmem, vmem, vmem],
        out_shape=[
            pltpu.VMEM((HALF, WIDE), jnp.bfloat16),
            pltpu.VMEM((2, BLOCK, 2 * LANES), jnp.float32),
            pltpu.VMEM((PAIRS, 2 * BLOCK, 4 * LANES), jnp.float32),
        ],
        scratch_shapes=[
            pltpu.VMEM((BLOCK, SAMPLES), jnp.bfloat16),
            pltpu.VMEM((PAIRS + 1, PART, 4 * LANES), jnp.bfloat16),
            pltpu.VMEM((RADIX * BLOCK, PART), jnp.bfloat16),
            pltpu.SemaphoreType.DMA((CHUNKS,)),
            pltpu.SemaphoreType.DMA((PAIRS + 1,)),
        ],
        compiler_params=pltpu.CompilerParams(vmem_limit_bytes=20 << 20),
        name="dft_whiten",
    )(*[pltpu.with_memory_space_constraint(a, pltpu.HBM) for a in (series, jnp.asarray(dft_table()))])


def own_half(pairs, real, pair):
    vmem = pl.BlockSpec(memory_space=pltpu.VMEM)
    return pl.pallas_call(
        own_kernel,
        in_specs=[pl.BlockSpec(memory_space=pltpu.SMEM), vmem, vmem],
        out_specs=vmem,
        out_shape=pltpu.VMEM((PLANE, 2 * MINE, WIDE), jnp.bfloat16),
        compiler_params=pltpu.CompilerParams(vmem_limit_bytes=4 << 20),
        cost_estimate=pl.CostEstimate(
            flops=40 * HALF * WIDE, bytes_accessed=5 << 20, transcendentals=0
        ),
        name="whiten_own",
    )(pairs, in_vmem(real), in_vmem(pair))


def corr_kernel(first_block, count, taper_ref, plane_ref, *refs):
    with_halo = first_block > 0
    if with_halo:
        halo_ref, high_ref, low_ref, _, out_ref, xh_ref, xl_ref, number_ref, scalar_ref, sem, w_ref = refs
    else:
        high_ref, low_ref, out_ref, xh_ref, xl_ref, number_ref, scalar_ref, sem = refs
        w_ref = plane_ref
    for a in range(count):
        number_ref[a : a + 1, :] = (
            plane_ref[first_block + a, :, :LANES].astype(jnp.float32)[:1].astype(jnp.int32)
        )
    numbers = pltpu.make_async_copy(number_ref, scalar_ref, sem)
    numbers.start()
    if with_halo:

        def own(i, carry):
            w_ref[i] = plane_ref[first_block + i]
            w_ref[count + i] = halo_ref[i]
            return carry

        lax.fori_loop(0, REACH, own, 0)
    numbers.wait()

    def one_block(a, carry):
        seconds = [a + scalar_ref[a, PER + k] for k in range(PARTNERS)]
        for n in range(RADIX):
            here = 2 * n * LANES

            def load(index):
                both = w_ref[index, :, here : here + 2 * LANES].astype(jnp.float32)
                return [
                    (both[w * MINE : (w + 1) * MINE, :LANES], both[w * MINE : (w + 1) * MINE, LANES:])
                    for w in range(WINDOWS)
                ]

            taper = taper_ref[n : n + 1, :]
            first = [(re * taper, im * taper) for re, im in load(a)]
            for slot in range(0, PARTNERS, 2):
                at = pl.ds(pl.multiple_of((a * PARTNERS + slot) * MINE, 16), 2 * MINE)
                re, im = [], []
                for k in (slot, slot + 1):
                    (a_re, a_im), (c_re, c_im) = first
                    (b_re, b_im), (d_re, d_im) = load(seconds[k])
                    re.append((a_re * b_re + a_im * b_im) + (c_re * d_re + c_im * d_im))
                    im.append((a_im * b_re - a_re * b_im) + (c_im * d_re - c_re * d_im))
                for side, both in enumerate((re, im)):
                    cross = jnp.concatenate(both, axis=0)
                    high = cross.astype(jnp.bfloat16)
                    columns = slice(here + side * LANES, here + (side + 1) * LANES)
                    xh_ref[at, columns] = high
                    xl_ref[at, columns] = (cross - high.astype(jnp.float32)).astype(jnp.bfloat16)
        return carry

    lax.fori_loop(0, count, one_block, 0)
    lagged = jnp.dot(xh_ref[...], high_ref[...], preferred_element_type=jnp.float32)
    lagged += jnp.dot(xh_ref[...], low_ref[...], preferred_element_type=jnp.float32)
    lagged += jnp.dot(xl_ref[...], high_ref[...], preferred_element_type=jnp.float32)
    start = first_block * PARTNERS
    out_ref[start : start + count * PARTNERS] = lagged.reshape(count * PARTNERS, MINE, LAGS)

    def mask(a, carry):
        for k in range(PARTNERS):

            @pl.when(scalar_ref[a, PER + k] == 0)
            def clear():
                out_ref[start + a * PARTNERS + k] = jnp.zeros((MINE, LAGS), jnp.float32)

        return carry

    lax.fori_loop(0, count, mask, 0)


def correlated(taper, plane, high, low, halo=None, done=None):
    with_halo = halo is not None
    first_block, count = (INNER, REACH) if with_halo else (0, INNER)
    rows = count * PARTNERS * MINE
    vmem = pl.BlockSpec(memory_space=pltpu.VMEM)
    operands = [taper, plane] + ([halo] if with_halo else []) + [high, low]
    aliases = {}
    scratch = [
        pltpu.VMEM((rows, WIDE), jnp.bfloat16),
        pltpu.VMEM((rows, WIDE), jnp.bfloat16),
        pltpu.VMEM((PLANE, LANES), jnp.int32),
        pltpu.SMEM((PLANE, LANES), jnp.int32),
        pltpu.SemaphoreType.DMA(()),
    ]
    if with_halo:
        aliases = {len(operands): 0}
        operands.append(done)
        scratch.append(pltpu.VMEM((2 * REACH, 2 * MINE, WIDE), jnp.bfloat16))

    def body(*refs):
        corr_kernel(first_block, count, *refs)

    return pl.pallas_call(
        body,
        in_specs=[vmem] * len(operands),
        out_specs=vmem,
        out_shape=pltpu.VMEM((PLANE * PARTNERS, MINE, LAGS), jnp.float32),
        scratch_shapes=scratch,
        input_output_aliases=aliases,
        compiler_params=pltpu.CompilerParams(vmem_limit_bytes=10 << 20),
        cost_estimate=pl.CostEstimate(
            flops=6 * rows * WIDE * LAGS, bytes_accessed=4 << 20, transcendentals=0
        ),
        name="correlate_halo" if with_halo else "correlate_inner",
    )(*[in_vmem(operand) for operand in operands])


def per_device(records, taper, pairs):
    theirs, real, pair = spectra(records[0])
    got = lax.ppermute(theirs, "tm", [(0, 1), (1, 0)])
    mine = own_half(pairs, real, pair)
    send = mine.at[:, MINE:].set(got.reshape(PLANE, MINE, WIDE))
    plane = lax.all_to_all(send, "col", 0, 0, tiled=True)
    count = lax.axis_size("row")
    halo = lax.ppermute(plane[:REACH], "row", [(z, z - 1) for z in range(1, count)])
    plane, taper = lax.optimization_barrier((plane, taper))
    squared = taper_columns(taper)
    high, low = (jnp.asarray(table) for table in lag_tables())
    lagged = correlated(squared, plane, high, low)
    lagged = correlated(squared, plane, high, low, halo, lagged)
    lagged = lagged.reshape(PLANE, PARTNERS, MINE, LAGS)
    back = lax.all_to_all(lagged, "col", 0, 0, tiled=True)
    return back.transpose(1, 0, 2, 3).reshape(1, PARTNERS, HALF, LAGS)


def solution(mesh):
    return jax.shard_map(
        per_device,
        mesh=mesh,
        in_specs=(P("tm", ("row", "col"), None), P(), P(("row", "col"), None)),
        out_specs=P(("row", "col"), None, "tm", None),
        check_vma=False,
    )
```

time: 80.8 us -> 73.8 us (0.913)
  Pallas kernels: 24.9 us -> 16.9 us
  waiting for transfers between devices: 8.04 us -> 9.68 us
    pallas_call x3 -> x4, Pallas kernels: 24.9 us -> 16.9 us  [the longest x1 7.18 us: spectra(): pl.pallas_call(dft_kernel, in_specs=[hbm, hbm], out_specs=[vmem, vmem, vm...]
    ppermute x1, waiting for transfers between devices: 5.74 us -> 9.67 us  [per_device(): lax.ppermute(plane[:REACH], 'row', [(z, z - 1) for z in range(1, count)])]
    ppermute x1, waiting for transfers between devices: 2.3 us -> 0.01 us  [per_device(): got = lax.ppermute(theirs, 'tm', [(0, 1), (1, 0)])]
    another operation x1, local copies, waits for them, and re-layouts: 1.22 us -> 0.05 us  [taper_columns(): return jnp.stack([parts[place_in_band(residue)] for residue in ORDER])]
    scatter x1, local copies, waits for them, and re-layouts: 0.92 us -> 0.06 us  [per_device(): send = mine.at[:, MINE:].set(got.reshape(PLANE, MINE, WIDE))]
  transfers between devices with their start and end apart: 2 -> 2, of which waited for: 2 -> 1; matrix products, arithmetic and copies ran while one was open for 2% -> 0% of each run, Pallas kernels for 10% -> 9%
where the time goes in v3:
time: 73.8 us; the launch traced here: 73.6 us
  blocking collectives  41.5 us (56%)
  Pallas kernels  16.9 us (23%)
  waiting for transfers between devices  9.68 us (13%)
  local copies, waits for them, and re-layouts  3.33 us (5%)
  starting transfers between devices  2.1 us (3%)
    all_to_all x1, blocking collectives, per_device(): plane = lax.all_to_all(send, 'col', 0, 0, tiled=True)  27.2 us
    all_to_all x1, blocking collectives, per_device(): back = lax.all_to_all(lagged, 'col', 0, 0, tiled=True)  14.3 us
    ppermute x1, waiting for transfers between devices, per_device(): lax.ppermute(plane[:REACH], 'row', [(z, z - 1) for z in range(1, count)])  9.67 us
    pallas_call x1, Pallas kernels, spectra(): pl.pallas_call(dft_kernel, in_specs=[hbm, hbm], out_specs=[vmem, vmem, vm...  7.18 us
    pallas_call x2, Pallas kernels, correlated(): pl.pallas_call(body, in_specs=[vmem] * len(operands), out_specs=vmem, out...  7.13 us
    pallas_call x1, Pallas kernels, own_half(): pl.pallas_call(own_kernel, in_specs=[pl.BlockSpec(memory_space=pltpu.SMEM...  2.55 us
    ppermute x1, starting transfers between devices, per_device(): lax.ppermute(plane[:REACH], 'row', [(z, z - 1) for z in range(1, count)])  2 us
  transfers between devices with their start and end apart: 2, of which 1 were waited for; matrix products, arithmetic and copies ran while one was open for 0% of the time, Pallas kernels for 9%

profile of v3, /device:TPU:96, one launch (start us, length us, event | category | flops | bytes accessed | tf_op | source)
XLA Modules:
  0.0 73.6 jit_solution(15299868234428902356)
XLA Ops:
  0.0 0.0 copy-start.2
  0.0 7.2 %dft_whiten.1 = (bf16[128,2560]{1,0:T(8,128)(2,1)S(1)}, f32[2,256,256]{2,1,0:T(8,128)S(1)}, f32[4,512,512]{2,1,0:T(8,128)S(1)}) custom-call(bf16[256,7680]{1,0:T(8,128)(2,1)} %bitcast.11, bf16[5,768,512]{2,1,0:T(8,128)(2,1)} %constant.38.clone.table_hbm), custom_call_target="tpu_custom_call" | custom-call | tf_op jit(solution)/shard_map/dft_whiten/pallas_call | solution.py:228
  7.2 0.1 collective-permute-start
  7.3 0.0 copy-done.2
  7.3 2.5 %whiten_own.1 = bf16[16,16,2560]{2,1,0:T(8,128)(2,1)S(1)} custom-call(s32[1,4]{1,0:T(1,128)S(1)} %copy-done.2, f32[2,256,256]{2,1,0:T(8,128)S(1)} %get-tuple-element.22.real_ref, f32[4,512,512]{2,1,0:T(8,128)S(1)} %get-tuple-element.23.pair_ref), custom_call_target="tpu_custom_call" | custom-call | flops 13107200 | bytes 5242880 | tf_op jit(solution)/shard_map/whiten_own/pallas_call | solution.py:251
  9.9 0.0 collective-permute-done
  9.9 0.1 bitcast_dynamic-update-slice_fusion
  9.9 0.0 copy-start.3
  9.9 27.2 %all_to_all.10.refs_1_ = bf16[16,16,2560]{2,1,0:T(8,128)(2,1)S(1)} all-to-all(bf16[16,16,2560]{2,1,0:T(8,128)(2,1)S(1)} %bitcast_dynamic-update-slice_fusion), channel_id=1, replica_groups=mesh['row'=8,'col'=16,'tm'=2] {'col'}, dimensions={0} | all-to-all | bytes 2621440 | tf_op jit(solution)/shard_map/all_to_all | solution.py:378
  37.2 0.0 copy-start
  37.2 0.8 %slice.66 = bf16[7,16,2560]{2,1,0:T(8,128)(2,1)} slice(bf16[16,16,2560]{2,1,0:T(8,128)(2,1)S(1)} %all_to_all.10.refs_1_), slice={[0:7], [0:16], [0:2560]} | slice | bytes 1146880 | tf_op jit(solution)/shard_map/slice | solution.py:380
  38.0 2.0 %collective-permute-start.1 = (bf16[7,16,2560]{2,1,0:T(8,128)(2,1)}, bf16[7,16,2560]{2,1,0:T(8,128)(2,1)S(1)}, u32[]{:S(2)}, u32[]{:S(2)}) collective-permute-start(bf16[7,16,2560]{2,1,0:T(8,128)(2,1)} %slice.66), channel_id=1, source_target_pairs={{32,0},{64,32},{96,64},{128,96},{160,128},{192,160},{224,192},{33,... | collective-permute-start | bytes 1720328 | tf_op jit(solution)/shard_map/ppermute | solution.py:380
  40.0 0.0 copy-done.3
  40.1 0.1 reshape.44
  40.2 0.1 copy.9
  40.3 0.0 copy-done
  40.3 0.0 copy-start.1
  40.3 1.3 %copy-done.1 = bf16[2560,256]{1,0:T(8,128)(2,1)S(1)} copy-done((bf16[2560,256]{1,0:T(8,128)(2,1)S(1)}, bf16[2560,256]{1,0:T(8,128)(2,1)}, u32[]{:S(2)}) %copy-start.1) | copy-done | bytes 1310744
  41.7 3.9 %correlate_inner.1.refs_5_ = f32[64,8,256]{2,1,0:T(8,128)S(1)} custom-call(f32[10,128]{1,0:T(8,128)S(1)} %stack.3.refs_0_, bf16[16,16,2560]{2,1,0:T(8,128)(2,1)S(1)} %all_to_all.10.refs_1_, bf16[2560,256]{1,0:T(8,128)(2,1)S(1)} %copy-done.1, bf16[2560,256]{1,0:T(8,128)(2,1)S(1)} %copy-done), custom_call_target="tpu_custom_call" | custom-call | flops 1132462080 | bytes 4194304 | tf_op jit(solution)/shard_map/correlate_inner/pallas_call | solution.py:358
  45.6 9.7 %collective-permute-done.1.refs_2_ = bf16[7,16,2560]{2,1,0:T(8,128)(2,1)S(1)} collective-permute-done((bf16[7,16,2560]{2,1,0:T(8,128)(2,1)}, bf16[7,16,2560]{2,1,0:T(8,128)(2,1)S(1)}, u32[]{:S(2)}, u32[]{:S(2)}) %collective-permute-start.1) | collective-permute-done | bytes 573472 | tf_op jit(solution)/shard_map/ppermute | solution.py:380
  55.3 3.2 %correlate_halo.1 = f32[64,8,256]{2,1,0:T(8,128)S(1)} custom-call(f32[10,128]{1,0:T(8,128)S(1)} %stack.3.refs_0_, bf16[16,16,2560]{2,1,0:T(8,128)(2,1)S(1)} %all_to_all.10.refs_1_, bf16[7,16,2560]{2,1,0:T(8,128)(2,1)S(1)} %collective-permute-done.1.refs_2_, bf16[2560,256]{1,0:T(8,128)(2,1)S(1)} %copy-done.1, ...), custom_call_target="tpu_custom_call", output_to_operand_aliasing={{}: (5, {})} | custom-call | flops 880803840 | bytes 4194304 | tf_op jit(solution)/shard_map/correlate_halo/pallas_call | solution.py:358
  58.5 14.3 %all_to_all.11 = f32[16,4,8,256]{3,2,1,0:T(8,128)S(1)} all-to-all(f32[16,4,8,256]{3,2,1,0:T(8,128)S(1)} %bitcast.10), channel_id=1, replica_groups=mesh['row'=8,'col'=16,'tm'=2] {'col'}, dimensions={0} | all-to-all | bytes 1048576 | tf_op jit(solution)/shard_map/all_to_all | solution.py:387
  72.8 0.8 %copy_bitcast_fusion = f32[1,4,128,256]{3,2,1,0:T(8,128)} fusion(f32[16,4,8,256]{3,2,1,0:T(8,128)S(1)} %all_to_all.11), kind=kLoop, calls=%fused_computation.1 | loop fusion | bytes 1048576 | tf_op jit(solution)/shard_map/reshape | solution.py:388
  (3 shorter events, 0.1 us)
Async XLA Ops:
  0.0 7.3 %copy-start.2 = (s32[1,4]{1,0:T(1,128)S(1)}, s32[1,4]{1,0:T(1,128)}, u32[]{:S(2)}) copy-start(s32[1,4]{1,0:T(1,128)} %pairs_ref.1) | copy-start | bytes 52
  7.2 2.7 %collective-permute-start = (bf16[128,2560]{1,0:T(8,128)(2,1)S(1)}, bf16[128,2560]{1,0:T(8,128)(2,1)S(1)}, u32[]{:S(2)}, u32[]{:S(2)}) collective-permute-start(bf16[128,2560]{1,0:T(8,128)(2,1)S(1)} %get-tuple-element.24), channel_id=1, source_target_pairs={{0,1},{1,0},{2,3},{3,2},{4,5},{5,4},{6,7},{7,6},{8,9},{9,8},{10,11... | collective-permute-start | bytes 1966088 | tf_op jit(solution)/shard_map/ppermute | solution.py:375
  9.9 30.1 %copy-start.3 = (f32[1200]{0:T(1024)S(1)}, f32[1200]{0:T(1024)}, u32[]{:S(2)}) copy-start(f32[1200]{0:T(1024)} %param.9) | copy-start | bytes 14404
  37.2 3.2 %copy-start = (bf16[2560,256]{1,0:T(8,128)(2,1)S(1)}, bf16[2560,256]{1,0:T(8,128)(2,1)}, u32[]{:S(2)}) copy-start(bf16[2560,256]{1,0:T(8,128)(2,1)} %constant.40.clone.refs_3_.refs_4_) | copy-start | bytes 3932164
  38.0 17.2 %collective-permute-start.1 = (bf16[7,16,2560]{2,1,0:T(8,128)(2,1)}, bf16[7,16,2560]{2,1,0:T(8,128)(2,1)S(1)}, u32[]{:S(2)}, u32[]{:S(2)}) collective-permute-start(bf16[7,16,2560]{2,1,0:T(8,128)(2,1)} %slice.66), channel_id=1, source_target_pairs={{32,0},{64,32},{96,64},{128,96},{160,128},{192,160},{224,192},{33,... | collective-permute-start | bytes 1720328 | tf_op jit(solution)/shard_map/ppermute | solution.py:380
  40.3 1.3 %copy-start.1 = (bf16[2560,256]{1,0:T(8,128)(2,1)S(1)}, bf16[2560,256]{1,0:T(8,128)(2,1)}, u32[]{:S(2)}) copy-start(bf16[2560,256]{1,0:T(8,128)(2,1)} %constant.39.clone.refs_2_.refs_3_) | copy-start | bytes 3932164

commit v4 on v3

--- a/solution.py
+++ b/solution.py
@@ -27,6 +27,7 @@
 PER = FREQS // RADIX
 LANES = 128
 WIDE = RADIX * 2 * LANES
+HALF_WIDE = WIDE // 2
 ORDER = (0, 5, 2, 8, 4, 6, 3, 7, 1, 9)
 PAIRS = len(ORDER) // 2 - 1
 PLANE = 16
@@ -125,7 +126,7 @@
         if c == CHUNKS - 2:
             for copy in t_copies:
                 copy.start()
-        lax.fori_loop(c * size // 16, (c + 1) * size // 16, split, 0)
+        lax.fori_loop(c * size // 16, (c + 1) * size // 16, split, 0, unroll=2)
 
     t_copies[0].wait()
     for n in range(2):
@@ -151,7 +152,7 @@
             )
         return carry
 
-    lax.fori_loop(0, HALF // 16, rows, 0)
+    lax.fori_loop(0, HALF // 16, rows, 0, unroll=2)
 
 
 def spectrum_part(real_ref, pair_ref, row, place):
@@ -215,7 +216,7 @@
             ).astype(jnp.bfloat16)
         return carry
 
-    lax.fori_loop(0, PLANE, rows, 0)
+    lax.fori_loop(0, PLANE, rows, 0, unroll=4)
 
 
 def in_vmem(array):
@@ -261,33 +262,39 @@
     )(pairs, in_vmem(real), in_vmem(pair))
 
 
-def corr_kernel(first_block, count, taper_ref, plane_ref, *refs):
-    with_halo = first_block > 0
-    if with_halo:
-        halo_ref, high_ref, low_ref, _, out_ref, xh_ref, xl_ref, number_ref, scalar_ref, sem, w_ref = refs
-    else:
-        high_ref, low_ref, out_ref, xh_ref, xl_ref, number_ref, scalar_ref, sem = refs
-        w_ref = plane_ref
+def head_kernel(plane_ref, *halves):
+    for part, half_ref in enumerate(halves):
+        for i in range(REACH):
+            half_ref[i] = plane_ref[i, :, part * HALF_WIDE : (part + 1) * HALF_WIDE]
+
+
+def plane_head(plane):
+    vmem = pl.BlockSpec(memory_space=pltpu.VMEM)
+    return pl.pallas_call(
+        head_kernel,
+        in_specs=[vmem],
+        out_specs=[vmem, vmem],
+        out_shape=[pltpu.VMEM((REACH, 2 * MINE, HALF_WIDE), jnp.bfloat16)] * 2,
+        compiler_params=pltpu.CompilerParams(vmem_limit_bytes=2 << 20),
+        name="plane_head",
+    )(in_vmem(plane))
+
+
+def read_offsets(plane_ref, first_block, count, number_ref, scalar_ref, sem):
     for a in range(count):
         number_ref[a : a + 1, :] = (
             plane_ref[first_block + a, :, :LANES].astype(jnp.float32)[:1].astype(jnp.int32)
         )
     numbers = pltpu.make_async_copy(number_ref, scalar_ref, sem)
     numbers.start()
-    if with_halo:
-
-        def own(i, carry):
-            w_ref[i] = plane_ref[first_block + i]
-            w_ref[count + i] = halo_ref[i]
-            return carry
-
-        lax.fori_loop(0, REACH, own, 0)
-    numbers.wait()
-
+    return numbers
+
+
+def cross_and_lag(count, columns, shift, taper_ref, w_ref, high_ref, low_ref, scalar_ref, xh_ref, xl_ref):
     def one_block(a, carry):
         seconds = [a + scalar_ref[a, PER + k] for k in range(PARTNERS)]
-        for n in range(RADIX):
-            here = 2 * n * LANES
+        for n in columns:
+            here = 2 * n * LANES - shift
 
             def load(index):
                 both = w_ref[index, :, here : here + 2 * LANES].astype(jnp.float32)
@@ -309,64 +316,89 @@
                 for side, both in enumerate((re, im)):
                     cross = jnp.concatenate(both, axis=0)
                     high = cross.astype(jnp.bfloat16)
-                    columns = slice(here + side * LANES, here + (side + 1) * LANES)
-                    xh_ref[at, columns] = high
-                    xl_ref[at, columns] = (cross - high.astype(jnp.float32)).astype(jnp.bfloat16)
+                    where = slice(here + side * LANES, here + (side + 1) * LANES)
+                    xh_ref[at, where] = high
+                    xl_ref[at, where] = (cross - high.astype(jnp.float32)).astype(jnp.bfloat16)
         return carry
 
-    lax.fori_loop(0, count, one_block, 0)
-    lagged = jnp.dot(xh_ref[...], high_ref[...], preferred_element_type=jnp.float32)
-    lagged += jnp.dot(xh_ref[...], low_ref[...], preferred_element_type=jnp.float32)
-    lagged += jnp.dot(xl_ref[...], high_ref[...], preferred_element_type=jnp.float32)
-    start = first_block * PARTNERS
-    out_ref[start : start + count * PARTNERS] = lagged.reshape(count * PARTNERS, MINE, LAGS)
-
-    def mask(a, carry):
-        for k in range(PARTNERS):
-
-            @pl.when(scalar_ref[a, PER + k] == 0)
-            def clear():
-                out_ref[start + a * PARTNERS + k] = jnp.zeros((MINE, LAGS), jnp.float32)
-
-        return carry
-
-    lax.fori_loop(0, count, mask, 0)
-
-
-def correlated(taper, plane, high, low, halo=None, done=None):
-    with_halo = halo is not None
-    first_block, count = (INNER, REACH) if with_halo else (0, INNER)
+    lax.fori_loop(0, count, one_block, 0, unroll=True)
+    rows = slice(shift, shift + xh_ref.shape[1])
+    lagged = jnp.dot(xh_ref[...], high_ref[rows, :], preferred_element_type=jnp.float32)
+    lagged += jnp.dot(xh_ref[...], low_ref[rows, :], preferred_element_type=jnp.float32)
+    lagged += jnp.dot(xl_ref[...], high_ref[rows, :], preferred_element_type=jnp.float32)
+    return lagged.reshape(count * PARTNERS, MINE, LAGS)
+
+
+def store_lags(out_ref, first_block, count, scalar_ref, lagged):
+    for i in range(count * PARTNERS):
+        valid = scalar_ref[i // PARTNERS, PER + i % PARTNERS] > 0
+        out_ref[first_block * PARTNERS + i] = jnp.where(valid, lagged[i], 0.0)
+
+
+def inner_kernel(
+    taper_ref, plane_ref, high_ref, low_ref, out_ref, number_ref, scalar_ref, sem, xh_ref, xl_ref
+):
+    read_offsets(plane_ref, 0, INNER, number_ref, scalar_ref, sem).wait()
+    lagged = cross_and_lag(
+        INNER, range(RADIX), 0, taper_ref, plane_ref, high_ref, low_ref, scalar_ref, xh_ref, xl_ref
+    )
+    store_lags(out_ref, 0, INNER, scalar_ref, lagged)
+
+
+def halo_kernel(
+    part,
+    taper_ref,
+    plane_ref,
+    halo_ref,
+    high_ref,
+    low_ref,
+    before_ref,
+    out_ref,
+    number_ref,
+    scalar_ref,
+    sem,
+    xh_ref,
+    xl_ref,
+    w_ref,
+):
+    numbers = read_offsets(plane_ref, INNER, REACH, number_ref, scalar_ref, sem)
+    shift = part * HALF_WIDE
+    for i in range(REACH):
+        w_ref[i] = plane_ref[INNER + i, :, shift : shift + HALF_WIDE]
+        w_ref[REACH + i] = halo_ref[i]
+    numbers.wait()
+    columns = range(part * RADIX // 2, (part + 1) * RADIX // 2)
+    lagged = cross_and_lag(
+        REACH, columns, shift, taper_ref, w_ref, high_ref, low_ref, scalar_ref, xh_ref, xl_ref
+    )
+    if part == 0:
+        out_ref[...] = lagged
+    else:
+        store_lags(out_ref, INNER, REACH, scalar_ref, lagged + before_ref[...])
+
+
+def correlated_call(body, name, operands, out_blocks, count, width, aliases, extra):
     rows = count * PARTNERS * MINE
     vmem = pl.BlockSpec(memory_space=pltpu.VMEM)
-    operands = [taper, plane] + ([halo] if with_halo else []) + [high, low]
-    aliases = {}
-    scratch = [
-        pltpu.VMEM((rows, WIDE), jnp.bfloat16),
-        pltpu.VMEM((rows, WIDE), jnp.bfloat16),
-        pltpu.VMEM((PLANE, LANES), jnp.int32),
-        pltpu.SMEM((PLANE, LANES), jnp.int32),
-        pltpu.SemaphoreType.DMA(()),
-    ]
-    if with_halo:
-        aliases = {len(operands): 0}
-        operands.append(done)
-        scratch.append(pltpu.VMEM((2 * REACH, 2 * MINE, WIDE), jnp.bfloat16))
-
-    def body(*refs):
-        corr_kernel(first_block, count, *refs)
-
     return pl.pallas_call(
         body,
         in_specs=[vmem] * len(operands),
         out_specs=vmem,
-        out_shape=pltpu.VMEM((PLANE * PARTNERS, MINE, LAGS), jnp.float32),
-        scratch_shapes=scratch,
+        out_shape=pltpu.VMEM((out_blocks * PARTNERS, MINE, LAGS), jnp.float32),
+        scratch_shapes=[
+            pltpu.VMEM((PLANE, LANES), jnp.int32),
+            pltpu.SMEM((PLANE, LANES), jnp.int32),
+            pltpu.SemaphoreType.DMA(()),
+            pltpu.VMEM((rows, width), jnp.bfloat16),
+            pltpu.VMEM((rows, width), jnp.bfloat16),
+        ]
+        + extra,
         input_output_aliases=aliases,
         compiler_params=pltpu.CompilerParams(vmem_limit_bytes=10 << 20),
         cost_estimate=pl.CostEstimate(
-            flops=6 * rows * WIDE * LAGS, bytes_accessed=4 << 20, transcendentals=0
+            flops=6 * rows * width * LAGS, bytes_accessed=4 << 20, transcendentals=0
         ),
-        name="correlate_halo" if with_halo else "correlate_inner",
+        name=name,
     )(*[in_vmem(operand) for operand in operands])
 
 
@@ -377,14 +409,44 @@
     send = mine.at[:, MINE:].set(got.reshape(PLANE, MINE, WIDE))
     plane = lax.all_to_all(send, "col", 0, 0, tiled=True)
     count = lax.axis_size("row")
-    halo = lax.ppermute(plane[:REACH], "row", [(z, z - 1) for z in range(1, count)])
+    down = [(z, z - 1) for z in range(1, count)]
+    halos = [lax.ppermute(half, "row", down) for half in plane_head(plane)]
     plane, taper = lax.optimization_barrier((plane, taper))
     squared = taper_columns(taper)
     high, low = (jnp.asarray(table) for table in lag_tables())
-    lagged = correlated(squared, plane, high, low)
-    lagged = correlated(squared, plane, high, low, halo, lagged)
+    w = [pltpu.VMEM((2 * REACH, 2 * MINE, HALF_WIDE), jnp.bfloat16)]
+    lagged = correlated_call(
+        inner_kernel, "correlate_inner", [squared, plane, high, low], PLANE, INNER, WIDE, {}, []
+    )
+
+    def first(*refs):
+        halo_kernel(0, *refs[:5], None, *refs[5:])
+
+    def second(taper_ref, plane_ref, halo_ref, high_ref, low_ref, before_ref, _, *refs):
+        halo_kernel(1, taper_ref, plane_ref, halo_ref, high_ref, low_ref, before_ref, *refs)
+
+    partial = correlated_call(
+        first,
+        "correlate_halo_first",
+        [squared, plane, halos[0], high, low],
+        REACH,
+        REACH,
+        HALF_WIDE,
+        {},
+        w,
+    )
+    lagged = correlated_call(
+        second,
+        "correlate_halo_second",
+        [squared, plane, halos[1], high, low, partial, lagged],
+        PLANE,
+        REACH,
+        HALF_WIDE,
+        {6: 0},
+        w,
+    )
     lagged = lagged.reshape(PLANE, PARTNERS, MINE, LAGS)
-    back = lax.all_to_all(lagged, "col", 0, 0, tiled=True)
+    back = lax.all_to_all(lagged.astype(jnp.bfloat16), "col", 0, 0, tiled=True).astype(jnp.float32)
     return back.transpose(1, 0, 2, 3).reshape(1, PARTNERS, HALF, LAGS)
 
 

time: 73.8 us -> 68.7 us (0.931)
  blocking collectives: 41.5 us -> 39 us
  waiting for transfers between devices: 9.68 us -> 7.53 us
  starting transfers between devices: 2.1 us -> 4.11 us
  Pallas kernels: 16.9 us -> 15.1 us
  local copies, waits for them, and re-layouts: 3.33 us -> 1.65 us
  other arithmetic: 0.01 us -> 0.87 us
    ppermute x1 -> x2, waiting for transfers between devices: 9.67 us -> 6.77 us  [per_device(): halos = [lax.ppermute(half, 'row', down) for half in plane_head(plane)]]
    all_to_all x1, blocking collectives: 14.3 us -> 12.2 us  [per_device(): lax.all_to_all(lagged.astype(jnp.bfloat16), 'col', 0, 0, tiled=True)]
    ppermute x1 -> x2, starting transfers between devices: 2 us -> 4.02 us  [per_device(): halos = [lax.ppermute(half, 'row', down) for half in plane_head(plane)]]
    pallas_call x1, Pallas kernels: 2.55 us -> 1.31 us  [own_half(): pl.pallas_call(own_kernel, in_specs=[pl.BlockSpec(memory_space=pltpu.SMEM...]
    slice x1 -> x0, local copies, waits for them, and re-layouts: 0.85 us -> none  [per_device(): plane[:REACH]]
    reshape x1 -> x0, local copies, waits for them, and re-layouts: 0.83 us -> none  [per_device(): return back.transpose(1, 0, 2, 3).reshape(1, PARTNERS, HALF, LAGS)]
    reshape x0 -> x1, other arithmetic: none -> 0.83 us  [per_device(): return back.transpose(1, 0, 2, 3).reshape(1, PARTNERS, HALF, LAGS)]
    ppermute x1, waiting for transfers between devices: 0.01 us -> 0.76 us  [per_device(): got = lax.ppermute(theirs, 'tm', [(0, 1), (1, 0)])]
  transfers between devices with their start and end apart: 2 -> 3, of which waited for: 1 -> 3; matrix products, arithmetic and copies ran while one was open for 0% -> 0% of each run, Pallas kernels for 9% -> 9%
where the time goes in v4:
time: 68.7 us; the launch traced here: 68.4 us
  blocking collectives  39 us (57%)
  Pallas kernels  15.1 us (22%)
  waiting for transfers between devices  7.53 us (11%)
  starting transfers between devices  4.11 us (6%)
  local copies, waits for them, and re-layouts  1.65 us (2%)
  other arithmetic  0.87 us (1%)
    all_to_all x1, blocking collectives, per_device(): plane = lax.all_to_all(send, 'col', 0, 0, tiled=True)  26.9 us
    all_to_all x1, blocking collectives, per_device(): lax.all_to_all(lagged.astype(jnp.bfloat16), 'col', 0, 0, tiled=True)  12.2 us
    ppermute x2, waiting for transfers between devices, per_device(): halos = [lax.ppermute(half, 'row', down) for half in plane_head(plane)]  6.77 us
    pallas_call x1, Pallas kernels, spectra(): pl.pallas_call(dft_kernel, in_specs=[hbm, hbm], out_specs=[vmem, vmem, vm...  6.72 us
    pallas_call x3, Pallas kernels, correlated_call(): pl.pallas_call(body, in_specs=[vmem] * len(operands), out_specs=vmem, out...  6.31 us
    ppermute x2, starting transfers between devices, per_device(): halos = [lax.ppermute(half, 'row', down) for half in plane_head(plane)]  4.02 us
  transfers between devices with their start and end apart: 3, of which 3 were waited for; matrix products, arithmetic and copies ran while one was open for 0% of the time, Pallas kernels for 9%

profile of v4, /device:TPU:96, one launch (start us, length us, event | category | flops | bytes accessed | tf_op | source)
XLA Modules:
  0.0 68.4 jit_solution(16604163259872426629)
XLA Ops:
  0.0 0.0 copy-start.2
  0.0 6.7 %dft_whiten.1 = (bf16[128,2560]{1,0:T(8,128)(2,1)S(1)}, f32[2,256,256]{2,1,0:T(8,128)S(1)}, f32[4,512,512]{2,1,0:T(8,128)S(1)}) custom-call(bf16[256,7680]{1,0:T(8,128)(2,1)} %bitcast.10, bf16[5,768,512]{2,1,0:T(8,128)(2,1)} %constant.38.clone.table_hbm), custom_call_target="tpu_custom_call" | custom-call | tf_op jit(solution)/shard_map/dft_whiten/pallas_call | solution.py:229
  6.7 0.1 collective-permute-start
  6.8 0.0 copy-done.2
  6.8 1.3 %whiten_own.1 = bf16[16,16,2560]{2,1,0:T(8,128)(2,1)S(1)} custom-call(s32[1,4]{1,0:T(1,128)S(1)} %copy-done.2, f32[2,256,256]{2,1,0:T(8,128)S(1)} %get-tuple-element.24.real_ref, f32[4,512,512]{2,1,0:T(8,128)S(1)} %get-tuple-element.25.pair_ref), custom_call_target="tpu_custom_call" | custom-call | flops 13107200 | bytes 5242880 | tf_op jit(solution)/shard_map/whiten_own/pallas_call | solution.py:252
  8.2 0.8 %collective-permute-done = bf16[128,2560]{1,0:T(8,128)(2,1)S(1)} collective-permute-done((bf16[128,2560]{1,0:T(8,128)(2,1)S(1)}, bf16[128,2560]{1,0:T(8,128)(2,1)S(1)}, u32[]{:S(2)}, u32[]{:S(2)}) %collective-permute-start) | collective-permute-done | bytes 655392 | tf_op jit(solution)/shard_map/ppermute | solution.py:407
  8.9 0.1 bitcast_dynamic-update-slice_fusion
  9.0 0.0 copy-start.3
  9.0 26.9 %all_to_all.10.plane_ref.refs_1_ = bf16[16,16,2560]{2,1,0:T(8,128)(2,1)S(1)} all-to-all(bf16[16,16,2560]{2,1,0:T(8,128)(2,1)S(1)} %bitcast_dynamic-update-slice_fusion), channel_id=1, replica_groups=mesh['row'=8,'col'=16,'tm'=2] {'col'}, dimensions={0} | all-to-all | bytes 2621440 | tf_op jit(solution)/shard_map/all_to_all | solution.py:410
  35.9 0.0 copy-start
  35.9 0.7 %plane_head.1 = (bf16[7,16,1280]{2,1,0:T(8,128)(2,1)}, bf16[7,16,1280]{2,1,0:T(8,128)(2,1)S(1)}) custom-call(bf16[16,16,2560]{2,1,0:T(8,128)(2,1)S(1)} %all_to_all.10.plane_ref.refs_1_), custom_call_target="tpu_custom_call" | custom-call | tf_op jit(solution)/shard_map/plane_head/pallas_call | solution.py:273
  36.6 2.0 %collective-permute-start.2 = (bf16[7,16,1280]{2,1,0:T(8,128)(2,1)}, bf16[7,16,1280]{2,1,0:T(8,128)(2,1)S(1)}, u32[]{:S(2)}, u32[]{:S(2)}) collective-permute-start(bf16[7,16,1280]{2,1,0:T(8,128)(2,1)} %get-tuple-element.30), channel_id=1, source_target_pairs={{32,0},{64,32},{96,64},{128,96},{160,128},{192,160},{224,192},{33,... | collective-permute-start | bytes 860168 | tf_op jit(solution)/shard_map/ppermute | solution.py:413
  38.6 2.0 %collective-permute-start.1 = (bf16[7,16,1280]{2,1,0:T(8,128)(2,1)S(1)}, bf16[7,16,1280]{2,1,0:T(8,128)(2,1)S(1)}, u32[]{:S(2)}, u32[]{:S(2)}) collective-permute-start(bf16[7,16,1280]{2,1,0:T(8,128)(2,1)S(1)} %get-tuple-element.29), channel_id=1, source_target_pairs={{32,0},{64,32},{96,64},{128,96},{160,128},{192,160},{224,192},{33,... | collective-permute-start | bytes 860168 | tf_op jit(solution)/shard_map/ppermute | solution.py:413
  40.7 0.0 copy-done.3
  40.7 0.1 reshape.46
  40.8 0.1 copy.9
  41.0 0.0 copy-done
  41.0 0.0 copy-start.1
  41.0 1.3 %copy-done.1 = bf16[2560,256]{1,0:T(8,128)(2,1)S(1)} copy-done((bf16[2560,256]{1,0:T(8,128)(2,1)S(1)}, bf16[2560,256]{1,0:T(8,128)(2,1)}, u32[]{:S(2)}) %copy-start.1) | copy-done | bytes 1310744
  42.3 3.0 %correlate_inner.1._ = f32[64,8,256]{2,1,0:T(8,128)S(1)} custom-call(f32[10,128]{1,0:T(8,128)S(1)} %stack.3.refs_0_.taper_ref, bf16[16,16,2560]{2,1,0:T(8,128)(2,1)S(1)} %all_to_all.10.plane_ref.refs_1_, bf16[2560,256]{1,0:T(8,128)(2,1)S(1)} %copy-done.1, bf16[2560,256]{1,0:T(8,128)(2,1)S(1)} %copy-done), custom_call_target="tpu_custom_call" | custom-call | flops 1132462080 | bytes 4194304 | tf_op jit(solution)/shard_map/correlate_inner/pallas_call | solution.py:383
  45.3 4.4 %collective-permute-done.2.refs_2_ = bf16[7,16,1280]{2,1,0:T(8,128)(2,1)S(1)} collective-permute-done((bf16[7,16,1280]{2,1,0:T(8,128)(2,1)}, bf16[7,16,1280]{2,1,0:T(8,128)(2,1)S(1)}, u32[]{:S(2)}, u32[]{:S(2)}) %collective-permute-start.2) | collective-permute-done | bytes 286752 | tf_op jit(solution)/shard_map/ppermute | solution.py:413
  49.7 1.7 %correlate_halo_first.1.before_ref = f32[28,8,256]{2,1,0:T(8,128)S(1)} custom-call(f32[10,128]{1,0:T(8,128)S(1)} %stack.3.refs_0_.taper_ref, bf16[16,16,2560]{2,1,0:T(8,128)(2,1)S(1)} %all_to_all.10.plane_ref.refs_1_, bf16[7,16,1280]{2,1,0:T(8,128)(2,1)S(1)} %collective-permute-done.2.refs_2_, bf16[2560,256]{1,0:T(8,128)(2,1)S(1)} %copy-done.1, ...), custom_call_target="tpu_custom_call" | custom-call | flops 440401920 | bytes 4194304 | tf_op jit(solution)/shard_map/correlate_halo_first/pallas_call | solution.py:383
  51.4 2.3 %collective-permute-done.1.halo_ref = bf16[7,16,1280]{2,1,0:T(8,128)(2,1)S(1)} collective-permute-done((bf16[7,16,1280]{2,1,0:T(8,128)(2,1)S(1)}, bf16[7,16,1280]{2,1,0:T(8,128)(2,1)S(1)}, u32[]{:S(2)}, u32[]{:S(2)}) %collective-permute-start.1) | collective-permute-done | bytes 286752 | tf_op jit(solution)/shard_map/ppermute | solution.py:413
  53.7 1.7 %correlate_halo_second.1 = f32[64,8,256]{2,1,0:T(8,128)S(1)} custom-call(f32[10,128]{1,0:T(8,128)S(1)} %stack.3.refs_0_.taper_ref, bf16[16,16,2560]{2,1,0:T(8,128)(2,1)S(1)} %all_to_all.10.plane_ref.refs_1_, bf16[7,16,1280]{2,1,0:T(8,128)(2,1)S(1)} %collective-permute-done.1.halo_ref, ...), custom_call_target="tpu_custom_call", output_to_operand_aliasing={{}: (6, {})} | custom-call | flops 440401920 | bytes 4194304 | tf_op jit(solution)/shard_map/correlate_halo_second/pallas_call | solution.py:383
  55.4 12.2 %all_to_all.11 = bf16[16,4,8,256]{3,2,1,0:T(8,128)(2,1)S(1)} all-to-all(bf16[16,4,8,256]{3,2,1,0:T(8,128)(2,1)S(1)} %bitcast.11), channel_id=1, replica_groups=mesh['row'=8,'col'=16,'tm'=2] {'col'}, dimensions={0} | all-to-all | bytes 524288 | tf_op jit(solution)/shard_map/all_to_all | solution.py:449
  67.6 0.8 %copy_bitcast_fusion = f32[1,4,128,256]{3,2,1,0:T(8,128)} fusion(bf16[16,4,8,256]{3,2,1,0:T(8,128)(2,1)S(1)} %all_to_all.11), kind=kLoop, calls=%fused_computation.1 | loop fusion | flops 131072 | bytes 786432 | tf_op jit(solution)/shard_map/reshape | solution.py:450
  (4 shorter events, 0.1 us)
Async XLA Ops:
  0.0 6.8 %copy-start.2 = (s32[1,4]{1,0:T(1,128)S(1)}, s32[1,4]{1,0:T(1,128)}, u32[]{:S(2)}) copy-start(s32[1,4]{1,0:T(1,128)} %pairs_ref.1) | copy-start | bytes 52
  6.7 2.2 %collective-permute-start = (bf16[128,2560]{1,0:T(8,128)(2,1)S(1)}, bf16[128,2560]{1,0:T(8,128)(2,1)S(1)}, u32[]{:S(2)}, u32[]{:S(2)}) collective-permute-start(bf16[128,2560]{1,0:T(8,128)(2,1)S(1)} %get-tuple-element.26), channel_id=1, source_target_pairs={{0,1},{1,0},{2,3},{3,2},{4,5},{5,4},{6,7},{7,6},{8,9},{9,8},{10,11... | collective-permute-start | bytes 1966088 | tf_op jit(solution)/shard_map/ppermute | solution.py:407
  9.0 31.7 %copy-start.3 = (f32[1200]{0:T(1024)S(1)}, f32[1200]{0:T(1024)}, u32[]{:S(2)}) copy-start(f32[1200]{0:T(1024)} %param.9) | copy-start | bytes 14404
  35.9 5.1 %copy-start = (bf16[2560,256]{1,0:T(8,128)(2,1)S(1)}, bf16[2560,256]{1,0:T(8,128)(2,1)}, u32[]{:S(2)}) copy-start(bf16[2560,256]{1,0:T(8,128)(2,1)} %constant.40.clone.refs_4_.low_ref) | copy-start | bytes 3932164
  36.6 13.1 %collective-permute-start.2 = (bf16[7,16,1280]{2,1,0:T(8,128)(2,1)}, bf16[7,16,1280]{2,1,0:T(8,128)(2,1)S(1)}, u32[]{:S(2)}, u32[]{:S(2)}) collective-permute-start(bf16[7,16,1280]{2,1,0:T(8,128)(2,1)} %get-tuple-element.30), channel_id=1, source_target_pairs={{32,0},{64,32},{96,64},{128,96},{160,128},{192,160},{224,192},{33,... | collective-permute-start | bytes 860168 | tf_op jit(solution)/shard_map/ppermute | solution.py:413
  38.6 15.1 %collective-permute-start.1 = (bf16[7,16,1280]{2,1,0:T(8,128)(2,1)S(1)}, bf16[7,16,1280]{2,1,0:T(8,128)(2,1)S(1)}, u32[]{:S(2)}, u32[]{:S(2)}) collective-permute-start(bf16[7,16,1280]{2,1,0:T(8,128)(2,1)S(1)} %get-tuple-element.29), channel_id=1, source_target_pairs={{32,0},{64,32},{96,64},{128,96},{160,128},{192,160},{224,192},{33,... | collective-permute-start | bytes 860168 | tf_op jit(solution)/shard_map/ppermute | solution.py:413
  41.0 1.3 %copy-start.1 = (bf16[2560,256]{1,0:T(8,128)(2,1)S(1)}, bf16[2560,256]{1,0:T(8,128)(2,1)}, u32[]{:S(2)}) copy-start(bf16[2560,256]{1,0:T(8,128)(2,1)} %constant.39.clone.refs_3_.high_ref) | copy-start | bytes 3932164

commit v5 on v4

--- a/solution.py
+++ b/solution.py
@@ -26,8 +26,13 @@
 HALF = BLOCK // 2
 PER = FREQS // RADIX
 LANES = 128
-WIDE = RADIX * 2 * LANES
-HALF_WIDE = WIDE // 2
+SPARE = LANES - PER
+FULL = RADIX - 1
+REST = PER - FULL * SPARE
+TAIL = 2 * FULL
+SIDE = LANES // 2
+WIDE = (TAIL + 1) * LANES
+HALO_PARTS = ((5, FULL, True), (0, 5, False))
 ORDER = (0, 5, 2, 8, 4, 6, 3, 7, 1, 9)
 PAIRS = len(ORDER) // 2 - 1
 PLANE = 16
@@ -61,7 +66,15 @@
 def lag_tables():
     lag_steps = np.arange(LAGS) - LAGS // 2 + SAMPLES
     factor = RESCALE / math.sqrt(FREQS * WINDOWS)
-    table = np.concatenate([angles(lag_steps, residue).T for residue in ORDER]) * factor
+    rows = [angles(lag_steps, residue).T for residue in ORDER]
+    last = rows[FULL].reshape(2, LANES, LAGS)
+    for place in range(FULL):
+        for side in range(2):
+            spare = slice(side * LANES + PER, (side + 1) * LANES)
+            rows[place][spare] = last[side, place * SPARE : (place + 1) * SPARE]
+    tail = np.zeros((2, SIDE, LAGS))
+    tail[:, :REST] = last[:, FULL * SPARE : PER]
+    table = np.concatenate(rows[:FULL] + [tail.reshape(LANES, LAGS)]) * factor
     table = table.astype(np.float32)
     high = table.astype(ml_dtypes.bfloat16)
     low = (table - high.astype(np.float32)).astype(ml_dtypes.bfloat16)
@@ -69,8 +82,12 @@
 
 
 def taper_columns(taper):
-    parts = jnp.pad((taper * taper).reshape(PER, RADIX).T, ((0, 0), (0, LANES - PER)))
-    return jnp.stack([parts[place_in_band(residue)] for residue in ORDER])
+    parts = (taper * taper).reshape(PER, RADIX).T
+    parts = [parts[place_in_band(residue)] for residue in ORDER]
+    spare = parts[FULL][: FULL * SPARE].reshape(FULL, SPARE)
+    full = jnp.concatenate([jnp.stack(parts[:FULL]), spare], axis=1)
+    tail = jnp.pad(parts[FULL][FULL * SPARE :], (0, SIDE - REST))
+    return jnp.concatenate([full, jnp.concatenate([tail, tail])[None]], axis=0)
 
 
 def five_point(x):
@@ -146,7 +163,7 @@
     def rows(i, carry):
         row = (1 - core) * HALF + i * 16
         parts = [white_rows(real_ref, pair_ref, row + j * MINE) for j in range(2)]
-        for n in range(2 * RADIX):
+        for n in range(TAIL + 1):
             theirs_ref[pl.ds(pl.multiple_of(i * 16, 16), 16), n * LANES : (n + 1) * LANES] = (
                 jnp.concatenate([parts[0][n], parts[1][n]], axis=0).astype(jnp.bfloat16)
             )
@@ -194,7 +211,15 @@
         scale = scale * (2.0 - level * scale)
         re, im = spectrum_part(real_ref, pair_ref, row, place)
         out += [re * scale, im * scale]
-    return out
+    lane = lax.broadcasted_iota(jnp.int32, (MINE, LANES), 1)
+    last = out[TAIL:]
+    for place in range(FULL):
+        for side in range(2):
+            moved = pltpu.roll(last[side], PER - place * SPARE, 1)
+            here = 2 * place + side
+            out[here] = jnp.where(lane >= PER, moved, out[here])
+    moved = [pltpu.roll(last[0], LANES - FULL * SPARE, 1), pltpu.roll(last[1], LANES + SIDE - FULL * SPARE, 1)]
+    return out[:TAIL] + [jnp.where(lane < SIDE, moved[0], moved[1])]
 
 
 def own_kernel(pairs_ref, real_ref, pair_ref, mine_ref):
@@ -205,11 +230,11 @@
     for k in range(PARTNERS):
         partner = pairs_ref[0, k]
         offset = jnp.where(partner < 0, 0, partner - block).astype(jnp.float32)
-        offsets = jnp.where(lane == PER + k, offset, offsets)
+        offsets = jnp.where(lane == REST + k, offset, offsets)
 
     def rows(j, carry):
         parts = white_rows(real_ref, pair_ref, core * HALF + j * MINE)
-        parts[0] = jnp.where(lane >= PER, offsets, parts[0])
+        parts[TAIL] = jnp.where((lane >= REST) & (lane < SIDE), offsets, parts[TAIL])
         for n, part in enumerate(parts):
             mine_ref[j, :, n * LANES : (n + 1) * LANES] = jnp.concatenate(
                 [part, part], axis=0
@@ -262,10 +287,20 @@
     )(pairs, in_vmem(real), in_vmem(pair))
 
 
+def part_columns(part):
+    begin, end, tail = part
+    return slice(2 * begin * LANES, (2 * end + tail) * LANES)
+
+
+def part_width(part):
+    columns = part_columns(part)
+    return columns.stop - columns.start
+
+
 def head_kernel(plane_ref, *halves):
-    for part, half_ref in enumerate(halves):
+    for part, half_ref in zip(HALO_PARTS, halves):
         for i in range(REACH):
-            half_ref[i] = plane_ref[i, :, part * HALF_WIDE : (part + 1) * HALF_WIDE]
+            half_ref[i] = plane_ref[i, :, part_columns(part)]
 
 
 def plane_head(plane):
@@ -274,7 +309,9 @@
         head_kernel,
         in_specs=[vmem],
         out_specs=[vmem, vmem],
-        out_shape=[pltpu.VMEM((REACH, 2 * MINE, HALF_WIDE), jnp.bfloat16)] * 2,
+        out_shape=[
+            pltpu.VMEM((REACH, 2 * MINE, part_width(part)), jnp.bfloat16) for part in HALO_PARTS
+        ],
         compiler_params=pltpu.CompilerParams(vmem_limit_bytes=2 << 20),
         name="plane_head",
     )(in_vmem(plane))
@@ -283,46 +320,70 @@
 def read_offsets(plane_ref, first_block, count, number_ref, scalar_ref, sem):
     for a in range(count):
         number_ref[a : a + 1, :] = (
-            plane_ref[first_block + a, :, :LANES].astype(jnp.float32)[:1].astype(jnp.int32)
+            plane_ref[first_block + a, :, TAIL * LANES :].astype(jnp.float32)[:1].astype(jnp.int32)
         )
     numbers = pltpu.make_async_copy(number_ref, scalar_ref, sem)
     numbers.start()
     return numbers
 
 
-def cross_and_lag(count, columns, shift, taper_ref, w_ref, high_ref, low_ref, scalar_ref, xh_ref, xl_ref):
+def cross_and_lag(count, part, taper_ref, w_ref, high_ref, low_ref, scalar_ref, xh_ref, xl_ref):
+    begin, end, with_tail = part
+    shift = 2 * begin * LANES
+    low_side = lax.broadcasted_iota(jnp.int32, (MINE, LANES), 1) < SIDE
+
     def one_block(a, carry):
-        seconds = [a + scalar_ref[a, PER + k] for k in range(PARTNERS)]
-        for n in columns:
-            here = 2 * n * LANES - shift
-
-            def load(index):
-                both = w_ref[index, :, here : here + 2 * LANES].astype(jnp.float32)
-                return [
-                    (both[w * MINE : (w + 1) * MINE, :LANES], both[w * MINE : (w + 1) * MINE, LANES:])
-                    for w in range(WINDOWS)
-                ]
-
+        seconds = [a + scalar_ref[a, REST + k] for k in range(PARTNERS)]
+
+        def load(index, block, blocks):
+            here = block * LANES - shift
+            both = w_ref[index, :, here : here + blocks * LANES].astype(jnp.float32)
+            return [both[w * MINE : (w + 1) * MINE] for w in range(WINDOWS)]
+
+        def store(slot, block, both):
+            at = pl.ds(pl.multiple_of((a * PARTNERS + slot) * MINE, 16), 2 * MINE)
+            columns = slice(block * LANES - shift, (block + 1) * LANES - shift)
+            cross = jnp.concatenate(both, axis=0)
+            high = cross.astype(jnp.bfloat16)
+            xh_ref[at, columns] = high
+            xl_ref[at, columns] = (cross - high.astype(jnp.float32)).astype(jnp.bfloat16)
+
+        for n in range(begin, end):
             taper = taper_ref[n : n + 1, :]
-            first = [(re * taper, im * taper) for re, im in load(a)]
+            first = [(x[:, :LANES] * taper, x[:, LANES:] * taper) for x in load(a, 2 * n, 2)]
             for slot in range(0, PARTNERS, 2):
-                at = pl.ds(pl.multiple_of((a * PARTNERS + slot) * MINE, 16), 2 * MINE)
                 re, im = [], []
                 for k in (slot, slot + 1):
                     (a_re, a_im), (c_re, c_im) = first
-                    (b_re, b_im), (d_re, d_im) = load(seconds[k])
+                    (b_re, b_im), (d_re, d_im) = [
+                        (x[:, :LANES], x[:, LANES:]) for x in load(seconds[k], 2 * n, 2)
+                    ]
                     re.append((a_re * b_re + a_im * b_im) + (c_re * d_re + c_im * d_im))
                     im.append((a_im * b_re - a_re * b_im) + (c_im * d_re - c_re * d_im))
-                for side, both in enumerate((re, im)):
-                    cross = jnp.concatenate(both, axis=0)
-                    high = cross.astype(jnp.bfloat16)
-                    where = slice(here + side * LANES, here + (side + 1) * LANES)
-                    xh_ref[at, where] = high
-                    xl_ref[at, where] = (cross - high.astype(jnp.float32)).astype(jnp.bfloat16)
+                store(slot, 2 * n, re)
+                store(slot, 2 * n + 1, im)
+        if with_tail:
+            taper = taper_ref[FULL : FULL + 1, :]
+            first = [x * taper for x in load(a, TAIL, 1)]
+            for slot in range(0, PARTNERS, 2):
+                both = []
+                for k in (slot, slot + 1):
+                    second = load(seconds[k], TAIL, 1)
+                    straight = first[0] * second[0] + first[1] * second[1]
+                    crossed = first[0] * pltpu.roll(second[0], SIDE, 1)
+                    crossed = crossed + first[1] * pltpu.roll(second[1], SIDE, 1)
+                    both.append(
+                        jnp.where(
+                            low_side,
+                            straight + pltpu.roll(straight, SIDE, 1),
+                            crossed - pltpu.roll(crossed, SIDE, 1),
+                        )
+                    )
+                store(slot, TAIL, both)
         return carry
 
     lax.fori_loop(0, count, one_block, 0, unroll=True)
-    rows = slice(shift, shift + xh_ref.shape[1])
+    rows = part_columns(part)
     lagged = jnp.dot(xh_ref[...], high_ref[rows, :], preferred_element_type=jnp.float32)
     lagged += jnp.dot(xh_ref[...], low_ref[rows, :], preferred_element_type=jnp.float32)
     lagged += jnp.dot(xl_ref[...], high_ref[rows, :], preferred_element_type=jnp.float32)
@@ -331,7 +392,7 @@
 
 def store_lags(out_ref, first_block, count, scalar_ref, lagged):
     for i in range(count * PARTNERS):
-        valid = scalar_ref[i // PARTNERS, PER + i % PARTNERS] > 0
+        valid = scalar_ref[i // PARTNERS, REST + i % PARTNERS] > 0
         out_ref[first_block * PARTNERS + i] = jnp.where(valid, lagged[i], 0.0)
 
 
@@ -340,7 +401,7 @@
 ):
     read_offsets(plane_ref, 0, INNER, number_ref, scalar_ref, sem).wait()
     lagged = cross_and_lag(
-        INNER, range(RADIX), 0, taper_ref, plane_ref, high_ref, low_ref, scalar_ref, xh_ref, xl_ref
+        INNER, (0, FULL, True), taper_ref, plane_ref, high_ref, low_ref, scalar_ref, xh_ref, xl_ref
     )
     store_lags(out_ref, 0, INNER, scalar_ref, lagged)
 
@@ -362,16 +423,14 @@
     w_ref,
 ):
     numbers = read_offsets(plane_ref, INNER, REACH, number_ref, scalar_ref, sem)
-    shift = part * HALF_WIDE
     for i in range(REACH):
-        w_ref[i] = plane_ref[INNER + i, :, shift : shift + HALF_WIDE]
+        w_ref[i] = plane_ref[INNER + i, :, part_columns(part)]
         w_ref[REACH + i] = halo_ref[i]
     numbers.wait()
-    columns = range(part * RADIX // 2, (part + 1) * RADIX // 2)
     lagged = cross_and_lag(
-        REACH, columns, shift, taper_ref, w_ref, high_ref, low_ref, scalar_ref, xh_ref, xl_ref
-    )
-    if part == 0:
+        REACH, part, taper_ref, w_ref, high_ref, low_ref, scalar_ref, xh_ref, xl_ref
+    )
+    if before_ref is None:
         out_ref[...] = lagged
     else:
         store_lags(out_ref, INNER, REACH, scalar_ref, lagged + before_ref[...])
@@ -414,16 +473,19 @@
     plane, taper = lax.optimization_barrier((plane, taper))
     squared = taper_columns(taper)
     high, low = (jnp.asarray(table) for table in lag_tables())
-    w = [pltpu.VMEM((2 * REACH, 2 * MINE, HALF_WIDE), jnp.bfloat16)]
+    widths = [part_width(part) for part in HALO_PARTS]
+    w = [[pltpu.VMEM((2 * REACH, 2 * MINE, width), jnp.bfloat16)] for width in widths]
     lagged = correlated_call(
         inner_kernel, "correlate_inner", [squared, plane, high, low], PLANE, INNER, WIDE, {}, []
     )
 
     def first(*refs):
-        halo_kernel(0, *refs[:5], None, *refs[5:])
+        halo_kernel(HALO_PARTS[0], *refs[:5], None, *refs[5:])
 
     def second(taper_ref, plane_ref, halo_ref, high_ref, low_ref, before_ref, _, *refs):
-        halo_kernel(1, taper_ref, plane_ref, halo_ref, high_ref, low_ref, before_ref, *refs)
+        halo_kernel(
+            HALO_PARTS[1], taper_ref, plane_ref, halo_ref, high_ref, low_ref, before_ref, *refs
+        )
 
     partial = correlated_call(
         first,
@@ -431,9 +493,9 @@
         [squared, plane, halos[0], high, low],
         REACH,
         REACH,
-        HALF_WIDE,
+        widths[0],
         {},
-        w,
+        w[0],
     )
     lagged = correlated_call(
         second,
@@ -441,9 +503,9 @@
         [squared, plane, halos[1], high, low, partial, lagged],
         PLANE,
         REACH,
-        HALF_WIDE,
+        widths[1],
         {6: 0},
-        w,
+        w[1],
     )
     lagged = lagged.reshape(PLANE, PARTNERS, MINE, LAGS)
     back = lax.all_to_all(lagged.astype(jnp.bfloat16), "col", 0, 0, tiled=True).astype(jnp.float32)

time: 68.7 us -> 67.9 us (0.988)
  waiting for transfers between devices: 7.53 us -> 6.56 us
    all_to_all x1, blocking collectives: 26.9 us -> 26.2 us  [per_device(): plane = lax.all_to_all(send, 'col', 0, 0, tiled=True)]
where the time goes in v5:
time: 67.9 us; the launch traced here: 67.7 us
  blocking collectives  38.4 us (57%)
  Pallas kernels  15.6 us (23%)
  waiting for transfers between devices  6.56 us (10%)
  starting transfers between devices  4.11 us (6%)
  local copies, waits for them, and re-layouts  1.8 us (3%)
  other arithmetic  1.02 us (2%)
    all_to_all x1, blocking collectives, per_device(): plane = lax.all_to_all(send, 'col', 0, 0, tiled=True)  26.2 us
    all_to_all x1, blocking collectives, per_device(): lax.all_to_all(lagged.astype(jnp.bfloat16), 'col', 0, 0, tiled=True)  12.2 us
    pallas_call x1, Pallas kernels, spectra(): pl.pallas_call(dft_kernel, in_specs=[hbm, hbm], out_specs=[vmem, vmem, vm...  7.04 us
    pallas_call x3, Pallas kernels, correlated_call(): pl.pallas_call(body, in_specs=[vmem] * len(operands), out_specs=vmem, out...  6.23 us
    ppermute x2, waiting for transfers between devices, per_device(): halos = [lax.ppermute(half, 'row', down) for half in plane_head(plane)]  6.14 us
    ppermute x2, starting transfers between devices, per_device(): halos = [lax.ppermute(half, 'row', down) for half in plane_head(plane)]  4.02 us
    pallas_call x1, Pallas kernels, own_half(): pl.pallas_call(own_kernel, in_specs=[pl.BlockSpec(memory_space=pltpu.SMEM...  1.59 us
  transfers between devices with their start and end apart: 3, of which 3 were waited for; matrix products, arithmetic and copies ran while one was open for 0% of the time, Pallas kernels for 9%

profile of v5, /device:TPU:96, one launch (start us, length us, event | category | flops | bytes accessed | tf_op | source)
XLA Modules:
  0.0 67.7 jit_solution(15434189533270724110)
XLA Ops:
  0.0 0.0 copy-start.2
  0.0 7.0 %dft_whiten.1 = (bf16[128,2432]{1,0:T(8,128)(2,1)S(1)}, f32[2,256,256]{2,1,0:T(8,128)S(1)}, f32[4,512,512]{2,1,0:T(8,128)S(1)}) custom-call(bf16[256,7680]{1,0:T(8,128)(2,1)} %bitcast.14, bf16[5,768,512]{2,1,0:T(8,128)(2,1)} %constant.38.clone.table_hbm), custom_call_target="tpu_custom_call" | custom-call | tf_op jit(solution)/shard_map/dft_whiten/pallas_call | solution.py:254
  7.1 0.1 collective-permute-start
  7.2 0.0 copy-done.2
  7.2 1.6 %whiten_own.1 = bf16[16,16,2432]{2,1,0:T(8,128)(2,1)S(1)} custom-call(s32[1,4]{1,0:T(1,128)S(1)} %copy-done.2, f32[2,256,256]{2,1,0:T(8,128)S(1)} %get-tuple-element.24.real_ref, f32[4,512,512]{2,1,0:T(8,128)S(1)} %get-tuple-element.25.pair_ref), custom_call_target="tpu_custom_call" | custom-call | flops 12451840 | bytes 5242880 | tf_op jit(solution)/shard_map/whiten_own/pallas_call | solution.py:277
  8.8 0.4 collective-permute-done
  9.2 0.1 bitcast_dynamic-update-slice_fusion
  9.3 0.0 copy-start.3
  9.3 26.2 %all_to_all.10.plane_ref.refs_1_ = bf16[16,16,2432]{2,1,0:T(8,128)(2,1)S(1)} all-to-all(bf16[16,16,2432]{2,1,0:T(8,128)(2,1)S(1)} %bitcast_dynamic-update-slice_fusion), channel_id=1, replica_groups=mesh['row'=8,'col'=16,'tm'=2] {'col'}, dimensions={0} | all-to-all | bytes 2490368 | tf_op jit(solution)/shard_map/all_to_all | solution.py:469
  35.5 0.0 copy-done.3
  35.5 0.0 copy-start
  35.5 0.1 reshape.52
  35.6 0.1 copy.9
  35.7 0.1 slice_bitcast_fusion
  35.8 0.7 %plane_head.1 = (bf16[7,16,1152]{2,1,0:T(8,128)(2,1)}, bf16[7,16,1280]{2,1,0:T(8,128)(2,1)S(1)}) custom-call(bf16[16,16,2432]{2,1,0:T(8,128)(2,1)S(1)} %all_to_all.10.plane_ref.refs_1_), custom_call_target="tpu_custom_call" | custom-call | tf_op jit(solution)/shard_map/plane_head/pallas_call | solution.py:308
  36.5 2.0 %collective-permute-start.2 = (bf16[7,16,1152]{2,1,0:T(8,128)(2,1)}, bf16[7,16,1152]{2,1,0:T(8,128)(2,1)S(1)}, u32[]{:S(2)}, u32[]{:S(2)}) collective-permute-start(bf16[7,16,1152]{2,1,0:T(8,128)(2,1)} %get-tuple-element.30), channel_id=1, source_target_pairs={{32,0},{64,32},{96,64},{128,96},{160,128},{192,160},{224,192},{33,... | collective-permute-start | bytes 774152 | tf_op jit(solution)/shard_map/ppermute | solution.py:472
  38.5 2.0 %collective-permute-start.1 = (bf16[7,16,1280]{2,1,0:T(8,128)(2,1)S(1)}, bf16[7,16,1280]{2,1,0:T(8,128)(2,1)S(1)}, u32[]{:S(2)}, u32[]{:S(2)}) collective-permute-start(bf16[7,16,1280]{2,1,0:T(8,128)(2,1)S(1)} %get-tuple-element.29), channel_id=1, source_target_pairs={{32,0},{64,32},{96,64},{128,96},{160,128},{192,160},{224,192},{33,... | collective-permute-start | bytes 860168 | tf_op jit(solution)/shard_map/ppermute | solution.py:472
  40.6 0.1 maximum_bitcast_fusion
  40.7 0.1 reshape.53
  40.8 0.1 pad_maximum_fusion.refs_0_.taper_ref
  40.8 0.0 copy-done
  40.8 0.0 copy-start.1
  40.8 1.3 %copy-done.1 = bf16[2432,256]{1,0:T(8,128)(2,1)S(1)} copy-done((bf16[2432,256]{1,0:T(8,128)(2,1)S(1)}, bf16[2432,256]{1,0:T(8,128)(2,1)}, u32[]{:S(2)}) %copy-start.1) | copy-done | bytes 1245208
  42.1 2.9 %correlate_inner.1._ = f32[64,8,256]{2,1,0:T(8,128)S(1)} custom-call(f32[10,128]{1,0:T(8,128)S(1)} %pad_maximum_fusion.refs_0_.taper_ref, bf16[16,16,2432]{2,1,0:T(8,128)(2,1)S(1)} %all_to_all.10.plane_ref.refs_1_, bf16[2432,256]{1,0:T(8,128)(2,1)S(1)} %copy-done.1, bf16[2432,256]{1,0:T(8,128)(2,1)S(1)} %copy-done), custom_call_target="tpu_custom_call" | custom-call | flops 1075838976 | bytes 4194304 | tf_op jit(solution)/shard_map/correlate_inner/pallas_call | solution.py:442
  45.1 3.9 %collective-permute-done.2.refs_2_ = bf16[7,16,1152]{2,1,0:T(8,128)(2,1)S(1)} collective-permute-done((bf16[7,16,1152]{2,1,0:T(8,128)(2,1)}, bf16[7,16,1152]{2,1,0:T(8,128)(2,1)S(1)}, u32[]{:S(2)}, u32[]{:S(2)}) %collective-permute-start.2) | collective-permute-done | bytes 258080 | tf_op jit(solution)/shard_map/ppermute | solution.py:472
  49.0 1.7 %correlate_halo_first.1.before_ref = f32[28,8,256]{2,1,0:T(8,128)S(1)} custom-call(f32[10,128]{1,0:T(8,128)S(1)} %pad_maximum_fusion.refs_0_.taper_ref, bf16[16,16,2432]{2,1,0:T(8,128)(2,1)S(1)} %all_to_all.10.plane_ref.refs_1_, bf16[7,16,1152]{2,1,0:T(8,128)(2,1)S(1)} %collective-permute-done.2.refs_2_, bf16[2432,256]{1,0:T(8,128)(2,1)S(1)} %copy-done.1, ...), custom_call_target="tpu_custom_call" | custom-call | flops 396361728 | bytes 4194304 | tf_op jit(solution)/shard_map/correlate_halo_first/pallas_call | solution.py:442
  50.7 2.2 %collective-permute-done.1.halo_ref = bf16[7,16,1280]{2,1,0:T(8,128)(2,1)S(1)} collective-permute-done((bf16[7,16,1280]{2,1,0:T(8,128)(2,1)S(1)}, bf16[7,16,1280]{2,1,0:T(8,128)(2,1)S(1)}, u32[]{:S(2)}, u32[]{:S(2)}) %collective-permute-start.1) | collective-permute-done | bytes 286752 | tf_op jit(solution)/shard_map/ppermute | solution.py:472
  52.9 1.6 %correlate_halo_second.1 = f32[64,8,256]{2,1,0:T(8,128)S(1)} custom-call(f32[10,128]{1,0:T(8,128)S(1)} %pad_maximum_fusion.refs_0_.taper_ref, bf16[16,16,2432]{2,1,0:T(8,128)(2,1)S(1)} %all_to_all.10.plane_ref.refs_1_, bf16[7,16,1280]{2,1,0:T(8,128)(2,1)S(1)} %collective-permute-done.1.halo_ref, ...), custom_call_target="tpu_custom_call", output_to_operand_aliasing={{}: (6, {})} | custom-call | flops 440401920 | bytes 4194304 | tf_op jit(solution)/shard_map/correlate_halo_second/pallas_call | solution.py:442
  54.6 12.2 %all_to_all.11 = bf16[16,4,8,256]{3,2,1,0:T(8,128)(2,1)S(1)} all-to-all(bf16[16,4,8,256]{3,2,1,0:T(8,128)(2,1)S(1)} %bitcast.15), channel_id=1, replica_groups=mesh['row'=8,'col'=16,'tm'=2] {'col'}, dimensions={0} | all-to-all | bytes 524288 | tf_op jit(solution)/shard_map/all_to_all | solution.py:511
  66.8 0.8 %copy_bitcast_fusion = f32[1,4,128,256]{3,2,1,0:T(8,128)} fusion(bf16[16,4,8,256]{3,2,1,0:T(8,128)(2,1)S(1)} %all_to_all.11), kind=kLoop, calls=%fused_computation.1 | loop fusion | flops 131072 | bytes 786432 | tf_op jit(solution)/shard_map/reshape | solution.py:512
  (6 shorter events, 0.1 us)
Async XLA Ops:
  0.0 7.2 %copy-start.2 = (s32[1,4]{1,0:T(1,128)S(1)}, s32[1,4]{1,0:T(1,128)}, u32[]{:S(2)}) copy-start(s32[1,4]{1,0:T(1,128)} %pairs_ref.1) | copy-start | bytes 52
  7.1 2.1 %collective-permute-start = (bf16[128,2432]{1,0:T(8,128)(2,1)S(1)}, bf16[128,2432]{1,0:T(8,128)(2,1)S(1)}, u32[]{:S(2)}, u32[]{:S(2)}) collective-permute-start(bf16[128,2432]{1,0:T(8,128)(2,1)S(1)} %get-tuple-element.26), channel_id=1, source_target_pairs={{0,1},{1,0},{2,3},{3,2},{4,5},{5,4},{6,7},{7,6},{8,9},{9,8},{10,11... | collective-permute-start | bytes 1867784 | tf_op jit(solution)/shard_map/ppermute | solution.py:466
  9.3 26.2 %copy-start.3 = (f32[1200]{0:T(1024)S(1)}, f32[1200]{0:T(1024)}, u32[]{:S(2)}) copy-start(f32[1200]{0:T(1024)} %param.9) | copy-start | bytes 14404
  35.5 5.4 %copy-start = (bf16[2432,256]{1,0:T(8,128)(2,1)S(1)}, bf16[2432,256]{1,0:T(8,128)(2,1)}, u32[]{:S(2)}) copy-start(bf16[2432,256]{1,0:T(8,128)(2,1)} %constant.40.clone.refs_4_.low_ref) | copy-start | bytes 3735556
  36.5 12.5 %collective-permute-start.2 = (bf16[7,16,1152]{2,1,0:T(8,128)(2,1)}, bf16[7,16,1152]{2,1,0:T(8,128)(2,1)S(1)}, u32[]{:S(2)}, u32[]{:S(2)}) collective-permute-start(bf16[7,16,1152]{2,1,0:T(8,128)(2,1)} %get-tuple-element.30), channel_id=1, source_target_pairs={{32,0},{64,32},{96,64},{128,96},{160,128},{192,160},{224,192},{33,... | collective-permute-start | bytes 774152 | tf_op jit(solution)/shard_map/ppermute | solution.py:472
  38.5 14.4 %collective-permute-start.1 = (bf16[7,16,1280]{2,1,0:T(8,128)(2,1)S(1)}, bf16[7,16,1280]{2,1,0:T(8,128)(2,1)S(1)}, u32[]{:S(2)}, u32[]{:S(2)}) collective-permute-start(bf16[7,16,1280]{2,1,0:T(8,128)(2,1)S(1)} %get-tuple-element.29), channel_id=1, source_target_pairs={{32,0},{64,32},{96,64},{128,96},{160,128},{192,160},{224,192},{33,... | collective-permute-start | bytes 860168 | tf_op jit(solution)/shard_map/ppermute | solution.py:472
  40.8 1.3 %copy-start.1 = (bf16[2432,256]{1,0:T(8,128)(2,1)S(1)}, bf16[2432,256]{1,0:T(8,128)(2,1)}, u32[]{:S(2)}) copy-start(bf16[2432,256]{1,0:T(8,128)(2,1)} %constant.39.clone.refs_3_.high_ref) | copy-start | bytes 3735556

commit v6 on v5

--- a/solution.py
+++ b/solution.py
@@ -32,7 +32,7 @@
 TAIL = 2 * FULL
 SIDE = LANES // 2
 WIDE = (TAIL + 1) * LANES
-HALO_PARTS = ((5, FULL, True), (0, 5, False))
+HALO_PARTS = ((3, FULL, True), (0, 3, False))
 ORDER = (0, 5, 2, 8, 4, 6, 3, 7, 1, 9)
 PAIRS = len(ORDER) // 2 - 1
 PLANE = 16
@@ -81,8 +81,8 @@
     return high, low
 
 
-def taper_columns(taper):
-    parts = (taper * taper).reshape(PER, RADIX).T
+def taper_columns(squared):
+    parts = squared.reshape(PER, RADIX).T
     parts = [parts[place_in_band(residue)] for residue in ORDER]
     spare = parts[FULL][: FULL * SPARE].reshape(FULL, SPARE)
     full = jnp.concatenate([jnp.stack(parts[:FULL]), spare], axis=1)
@@ -222,7 +222,8 @@
     return out[:TAIL] + [jnp.where(lane < SIDE, moved[0], moved[1])]
 
 
-def own_kernel(pairs_ref, real_ref, pair_ref, mine_ref):
+def own_kernel(pairs_ref, taper_ref, real_ref, pair_ref, mine_ref, squared_ref):
+    squared_ref[...] = taper_ref[...] * taper_ref[...]
     core = lax.axis_index("tm")
     block = lax.axis_index("row") * PLANE + lax.axis_index("col")
     lane = lax.broadcasted_iota(jnp.int32, (MINE, LANES), 1)
@@ -272,19 +273,22 @@
     )(*[pltpu.with_memory_space_constraint(a, pltpu.HBM) for a in (series, jnp.asarray(dft_table()))])
 
 
-def own_half(pairs, real, pair):
+def own_half(pairs, taper, real, pair):
     vmem = pl.BlockSpec(memory_space=pltpu.VMEM)
     return pl.pallas_call(
         own_kernel,
-        in_specs=[pl.BlockSpec(memory_space=pltpu.SMEM), vmem, vmem],
-        out_specs=vmem,
-        out_shape=pltpu.VMEM((PLANE, 2 * MINE, WIDE), jnp.bfloat16),
+        in_specs=[pl.BlockSpec(memory_space=pltpu.SMEM), vmem, vmem, vmem],
+        out_specs=[vmem, vmem],
+        out_shape=[
+            pltpu.VMEM((PLANE, 2 * MINE, WIDE), jnp.bfloat16),
+            pltpu.VMEM((FREQS,), jnp.float32),
+        ],
         compiler_params=pltpu.CompilerParams(vmem_limit_bytes=4 << 20),
         cost_estimate=pl.CostEstimate(
             flops=40 * HALF * WIDE, bytes_accessed=5 << 20, transcendentals=0
         ),
         name="whiten_own",
-    )(pairs, in_vmem(real), in_vmem(pair))
+    )(pairs, taper, in_vmem(real), in_vmem(pair))
 
 
 def part_columns(part):
@@ -297,43 +301,32 @@
     return columns.stop - columns.start
 
 
-def head_kernel(plane_ref, *halves):
-    for part, half_ref in zip(HALO_PARTS, halves):
+def plane_head(plane, part):
+    vmem = pl.BlockSpec(memory_space=pltpu.VMEM)
+
+    def body(plane_ref, head_ref):
         for i in range(REACH):
-            half_ref[i] = plane_ref[i, :, part_columns(part)]
-
-
-def plane_head(plane):
-    vmem = pl.BlockSpec(memory_space=pltpu.VMEM)
+            head_ref[i] = plane_ref[i, :, part_columns(part)]
+
     return pl.pallas_call(
-        head_kernel,
+        body,
         in_specs=[vmem],
-        out_specs=[vmem, vmem],
-        out_shape=[
-            pltpu.VMEM((REACH, 2 * MINE, part_width(part)), jnp.bfloat16) for part in HALO_PARTS
-        ],
+        out_specs=vmem,
+        out_shape=pltpu.VMEM((REACH, 2 * MINE, part_width(part)), jnp.bfloat16),
         compiler_params=pltpu.CompilerParams(vmem_limit_bytes=2 << 20),
         name="plane_head",
     )(in_vmem(plane))
 
 
-def read_offsets(plane_ref, first_block, count, number_ref, scalar_ref, sem):
-    for a in range(count):
-        number_ref[a : a + 1, :] = (
-            plane_ref[first_block + a, :, TAIL * LANES :].astype(jnp.float32)[:1].astype(jnp.int32)
-        )
-    numbers = pltpu.make_async_copy(number_ref, scalar_ref, sem)
-    numbers.start()
-    return numbers
-
-
-def cross_and_lag(count, part, taper_ref, w_ref, high_ref, low_ref, scalar_ref, xh_ref, xl_ref):
+def cross_and_lag(
+    first_block, count, part, taper_ref, w_ref, high_ref, low_ref, scalar_ref, xh_ref, xl_ref
+):
     begin, end, with_tail = part
     shift = 2 * begin * LANES
     low_side = lax.broadcasted_iota(jnp.int32, (MINE, LANES), 1) < SIDE
 
     def one_block(a, carry):
-        seconds = [a + scalar_ref[a, REST + k] for k in range(PARTNERS)]
+        seconds = [a + scalar_ref[first_block + a, REST + k] for k in range(PARTNERS)]
 
         def load(index, block, blocks):
             here = block * LANES - shift
@@ -392,22 +385,29 @@
 
 def store_lags(out_ref, first_block, count, scalar_ref, lagged):
     for i in range(count * PARTNERS):
-        valid = scalar_ref[i // PARTNERS, REST + i % PARTNERS] > 0
+        valid = scalar_ref[first_block + i // PARTNERS, REST + i % PARTNERS] > 0
         out_ref[first_block * PARTNERS + i] = jnp.where(valid, lagged[i], 0.0)
 
 
 def inner_kernel(
-    taper_ref, plane_ref, high_ref, low_ref, out_ref, number_ref, scalar_ref, sem, xh_ref, xl_ref
+    taper_ref, plane_ref, high_ref, low_ref, out_ref, scalar_ref, xh_ref, xl_ref, number_ref, sem
 ):
-    read_offsets(plane_ref, 0, INNER, number_ref, scalar_ref, sem).wait()
+    for a in range(PLANE):
+        number_ref[a : a + 1, :] = (
+            plane_ref[a, :, TAIL * LANES :].astype(jnp.float32)[:1].astype(jnp.int32)
+        )
+    numbers = pltpu.make_async_copy(number_ref, scalar_ref, sem)
+    numbers.start()
+    numbers.wait()
     lagged = cross_and_lag(
-        INNER, (0, FULL, True), taper_ref, plane_ref, high_ref, low_ref, scalar_ref, xh_ref, xl_ref
+        0, INNER, (0, FULL, True), taper_ref, plane_ref, high_ref, low_ref, scalar_ref, xh_ref, xl_ref
     )
     store_lags(out_ref, 0, INNER, scalar_ref, lagged)
 
 
 def halo_kernel(
     part,
+    scalar_ref,
     taper_ref,
     plane_ref,
     halo_ref,
@@ -415,20 +415,15 @@
     low_ref,
     before_ref,
     out_ref,
-    number_ref,
-    scalar_ref,
-    sem,
     xh_ref,
     xl_ref,
     w_ref,
 ):
-    numbers = read_offsets(plane_ref, INNER, REACH, number_ref, scalar_ref, sem)
     for i in range(REACH):
         w_ref[i] = plane_ref[INNER + i, :, part_columns(part)]
         w_ref[REACH + i] = halo_ref[i]
-    numbers.wait()
     lagged = cross_and_lag(
-        REACH, part, taper_ref, w_ref, high_ref, low_ref, scalar_ref, xh_ref, xl_ref
+        INNER, REACH, part, taper_ref, w_ref, high_ref, low_ref, scalar_ref, xh_ref, xl_ref
     )
     if before_ref is None:
         out_ref[...] = lagged
@@ -436,18 +431,26 @@
         store_lags(out_ref, INNER, REACH, scalar_ref, lagged + before_ref[...])
 
 
-def correlated_call(body, name, operands, out_blocks, count, width, aliases, extra):
+def correlated_call(body, name, scalars, operands, out_blocks, count, width, aliases, extra):
     rows = count * PARTNERS * MINE
     vmem = pl.BlockSpec(memory_space=pltpu.VMEM)
+    smem = pl.BlockSpec(memory_space=pltpu.SMEM)
+    out_specs = [vmem]
+    out_shape = [pltpu.VMEM((out_blocks * PARTNERS, MINE, LAGS), jnp.float32)]
+    operands = [in_vmem(operand) for operand in operands]
+    in_specs = [vmem] * len(operands)
+    if scalars is None:
+        out_specs.append(smem)
+        out_shape.append(pltpu.SMEM((PLANE, LANES), jnp.int32))
+    else:
+        in_specs.insert(0, smem)
+        operands.insert(0, pltpu.with_memory_space_constraint(scalars, pltpu.SMEM))
     return pl.pallas_call(
         body,
-        in_specs=[vmem] * len(operands),
-        out_specs=vmem,
-        out_shape=pltpu.VMEM((out_blocks * PARTNERS, MINE, LAGS), jnp.float32),
+        in_specs=in_specs,
+        out_specs=out_specs,
+        out_shape=out_shape,
         scratch_shapes=[
-            pltpu.VMEM((PLANE, LANES), jnp.int32),
-            pltpu.SMEM((PLANE, LANES), jnp.int32),
-            pltpu.SemaphoreType.DMA(()),
             pltpu.VMEM((rows, width), jnp.bfloat16),
             pltpu.VMEM((rows, width), jnp.bfloat16),
         ]
@@ -458,38 +461,48 @@
             flops=6 * rows * width * LAGS, bytes_accessed=4 << 20, transcendentals=0
         ),
         name=name,
-    )(*[in_vmem(operand) for operand in operands])
+    )(*operands)
 
 
 def per_device(records, taper, pairs):
     theirs, real, pair = spectra(records[0])
     got = lax.ppermute(theirs, "tm", [(0, 1), (1, 0)])
-    mine = own_half(pairs, real, pair)
+    mine, squared = own_half(pairs, taper, real, pair)
     send = mine.at[:, MINE:].set(got.reshape(PLANE, MINE, WIDE))
     plane = lax.all_to_all(send, "col", 0, 0, tiled=True)
     count = lax.axis_size("row")
     down = [(z, z - 1) for z in range(1, count)]
-    halos = [lax.ppermute(half, "row", down) for half in plane_head(plane)]
-    plane, taper = lax.optimization_barrier((plane, taper))
-    squared = taper_columns(taper)
+    head, squared = lax.optimization_barrier((plane_head(plane, HALO_PARTS[0]), squared))
+    halos = [lax.ppermute(head, "row", down)]
+    squared = taper_columns(squared)
     high, low = (jnp.asarray(table) for table in lag_tables())
     widths = [part_width(part) for part in HALO_PARTS]
     w = [[pltpu.VMEM((2 * REACH, 2 * MINE, width), jnp.bfloat16)] for width in widths]
-    lagged = correlated_call(
-        inner_kernel, "correlate_inner", [squared, plane, high, low], PLANE, INNER, WIDE, {}, []
-    )
+    lagged, scalars = correlated_call(
+        inner_kernel,
+        "correlate_inner",
+        None,
+        [squared, plane, high, low],
+        PLANE,
+        INNER,
+        WIDE,
+        {},
+        [pltpu.VMEM((PLANE, LANES), jnp.int32), pltpu.SemaphoreType.DMA(())],
+    )
+
+    later, scalars = lax.optimization_barrier((plane, scalars))
+    halos.append(lax.ppermute(plane_head(later, HALO_PARTS[1]), "row", down))
 
     def first(*refs):
-        halo_kernel(HALO_PARTS[0], *refs[:5], None, *refs[5:])
-
-    def second(taper_ref, plane_ref, halo_ref, high_ref, low_ref, before_ref, _, *refs):
-        halo_kernel(
-            HALO_PARTS[1], taper_ref, plane_ref, halo_ref, high_ref, low_ref, before_ref, *refs
-        )
-
-    partial = correlated_call(
+        halo_kernel(HALO_PARTS[0], *refs[:6], None, *refs[6:])
+
+    def second(*refs):
+        halo_kernel(HALO_PARTS[1], *refs[:7], *refs[8:])
+
+    (partial,) = correlated_call(
         first,
         "correlate_halo_first",
+        scalars,
         [squared, plane, halos[0], high, low],
         REACH,
         REACH,
@@ -497,14 +510,15 @@
         {},
         w[0],
     )
-    lagged = correlated_call(
+    (lagged,) = correlated_call(
         second,
         "correlate_halo_second",
+        scalars,
         [squared, plane, halos[1], high, low, partial, lagged],
         PLANE,
         REACH,
         widths[1],
-        {6: 0},
+        {7: 0},
         w[1],
     )
     lagged = lagged.reshape(PLANE, PARTNERS, MINE, LAGS)

time: 67.9 us -> 66.1 us (0.973)
  Pallas kernels: 15.6 us -> 13.8 us
    pallas_call x4 -> x5, Pallas kernels: 6.96 us -> 5.12 us  [the longest x3 5.08 us: correlated_call(): pl.pallas_call(body, in_specs=in_specs, out_specs=out_specs, out_shape=ou...]
where the time goes in v6:
time: 66.1 us; the launch traced here: 65.9 us
  blocking collectives  38.4 us (58%)
  Pallas kernels  13.8 us (21%)
  waiting for transfers between devices  6.49 us (10%)
  starting transfers between devices  4.25 us (6%)
  local copies, waits for them, and re-layouts  1.8 us (3%)
  other arithmetic  1.01 us (2%)
    all_to_all x1, blocking collectives, per_device(): plane = lax.all_to_all(send, 'col', 0, 0, tiled=True)  26.2 us
    all_to_all x1, blocking collectives, per_device(): lax.all_to_all(lagged.astype(jnp.bfloat16), 'col', 0, 0, tiled=True)  12.2 us
    pallas_call x1, Pallas kernels, spectra(): pl.pallas_call(dft_kernel, in_specs=[hbm, hbm], out_specs=[vmem, vmem, vm...  7.05 us
    ppermute x1, waiting for transfers between devices, per_device(): halos = [lax.ppermute(head, 'row', down)]  5.14 us
    pallas_call x3, Pallas kernels, correlated_call(): pl.pallas_call(body, in_specs=in_specs, out_specs=out_specs, out_shape=ou...  5.08 us
    ppermute x1, starting transfers between devices, per_device(): halos = [lax.ppermute(head, 'row', down)]  2.15 us
    ppermute x1, starting transfers between devices, per_device(): halos.append(lax.ppermute(plane_head(later, HALO_PARTS[1]), 'row', down))  2.01 us
    pallas_call x1, Pallas kernels, own_half(): pl.pallas_call(own_kernel, in_specs=[pl.BlockSpec(memory_space=pltpu.SMEM...  1.59 us
  transfers between devices with their start and end apart: 3, of which 3 were waited for; matrix products, arithmetic and copies ran while one was open for 0% of the time, Pallas kernels for 9%

profile of v6, /device:TPU:96, one launch (start us, length us, event | category | flops | bytes accessed | tf_op | source)
XLA Modules:
  0.0 65.9 jit_solution(6895178123564820828)
XLA Ops:
  0.0 0.0 copy-start.2
  0.0 0.0 copy-start.3
  0.0 7.1 %dft_whiten.1 = (bf16[128,2432]{1,0:T(8,128)(2,1)S(1)}, f32[2,256,256]{2,1,0:T(8,128)S(1)}, f32[4,512,512]{2,1,0:T(8,128)S(1)}) custom-call(bf16[256,7680]{1,0:T(8,128)(2,1)} %bitcast.14, bf16[5,768,512]{2,1,0:T(8,128)(2,1)} %constant.38.clone.table_hbm), custom_call_target="tpu_custom_call" | custom-call | tf_op jit(solution)/shard_map/dft_whiten/pallas_call | solution.py:255
  7.1 0.1 collective-permute-start
  7.2 0.0 copy-done.2
  7.2 0.0 copy-done.3
  7.2 1.6 %whiten_own.1 = (bf16[16,16,2432]{2,1,0:T(8,128)(2,1)S(1)}, f32[1200]{0:T(1024)S(1)}) custom-call(s32[1,4]{1,0:T(1,128)S(1)} %copy-done.3, f32[1200]{0:T(1024)S(1)} %copy-done.2, f32[2,256,256]{2,1,0:T(8,128)S(1)} %get-tuple-element.28.real_ref, f32[4,512,512]{2,1,0:T(8,128)S(1)} %get-tuple-element.29.pair_ref), custom_call_target="tpu_custom_call" | custom-call | flops 12451840 | bytes 5242880 | tf_op jit(solution)/shard_map/whiten_own/pallas_call | solution.py:278
  8.8 0.4 collective-permute-done
  9.2 0.1 bitcast_dynamic-update-slice_fusion
  9.3 26.2 %all_to_all.10.plane_ref.refs_2_ = bf16[16,16,2432]{2,1,0:T(8,128)(2,1)S(1)} all-to-all(bf16[16,16,2432]{2,1,0:T(8,128)(2,1)S(1)} %bitcast_dynamic-update-slice_fusion), channel_id=1, replica_groups=mesh['row'=8,'col'=16,'tm'=2] {'col'}, dimensions={0} | all-to-all | bytes 2490368 | tf_op jit(solution)/shard_map/all_to_all | solution.py:472
  35.5 0.0 copy-start
  35.5 0.1 reshape.52
  35.6 0.1 copy.9
  35.7 0.1 slice_bitcast_fusion
  35.8 2.2 %collective-permute-start.2 = (bf16[7,16,1664]{2,1,0:T(8,128)(2,1)S(1)}, bf16[7,16,1664]{2,1,0:T(8,128)(2,1)S(1)}, u32[]{:S(2)}, u32[]{:S(2)}) collective-permute-start(bf16[7,16,1664]{2,1,0:T(8,128)(2,1)S(1)} %plane_head.2), channel_id=1, source_target_pairs={{32,0},{64,32},{96,64},{128,96},{160,128},{192,160},{224,192},{33,... | collective-permute-start | bytes 1118216 | tf_op jit(solution)/shard_map/ppermute | solution.py:476
  38.0 0.1 maximum_bitcast_fusion
  38.1 0.1 reshape.53
  38.2 0.1 pad_maximum_fusion.taper_ref.refs_1_
  38.3 0.0 copy-done
  38.3 0.0 copy-start.1
  38.3 1.3 %copy-done.1 = bf16[2432,256]{1,0:T(8,128)(2,1)S(1)} copy-done((bf16[2432,256]{1,0:T(8,128)(2,1)S(1)}, bf16[2432,256]{1,0:T(8,128)(2,1)}, u32[]{:S(2)}) %copy-start.1) | copy-done | bytes 1245208
  39.6 3.0 %correlate_inner.1 = (f32[64,8,256]{2,1,0:T(8,128)S(1)}, s32[16,128]{1,0:T(8,128)S(4)}) custom-call(f32[10,128]{1,0:T(8,128)S(1)} %pad_maximum_fusion.taper_ref.refs_1_, bf16[16,16,2432]{2,1,0:T(8,128)(2,1)S(1)} %all_to_all.10.plane_ref.refs_2_, bf16[2432,256]{1,0:T(8,128)(2,1)S(1)} %copy-done.1, bf16[2432,256]{1,0:T(8,128)(2,1)S(1)} %copy-done), custom_call_target="tpu_custom_call" | custom-call | flops 1075838976 | bytes 4194304 | tf_op jit(solution)/shard_map/correlate_inner/pallas_call | solution.py:448
  42.6 2.0 %collective-permute-start.1 = (bf16[7,16,768]{2,1,0:T(8,128)(2,1)S(1)}, bf16[7,16,768]{2,1,0:T(8,128)(2,1)S(1)}, u32[]{:S(2)}, u32[]{:S(2)}) collective-permute-start(bf16[7,16,768]{2,1,0:T(8,128)(2,1)S(1)} %plane_head.3), channel_id=1, source_target_pairs={{32,0},{64,32},{96,64},{128,96},{160,128},{192,160},{224,192},{33,... | collective-permute-start | bytes 516104 | tf_op jit(solution)/shard_map/ppermute | solution.py:494
  44.6 5.1 %collective-permute-done.2.refs_3_ = bf16[7,16,1664]{2,1,0:T(8,128)(2,1)S(1)} collective-permute-done((bf16[7,16,1664]{2,1,0:T(8,128)(2,1)S(1)}, bf16[7,16,1664]{2,1,0:T(8,128)(2,1)S(1)}, u32[]{:S(2)}, u32[]{:S(2)}) %collective-permute-start.2) | collective-permute-done | bytes 372768 | tf_op jit(solution)/shard_map/ppermute | solution.py:476
  49.8 1.4 %correlate_halo_first.1.refs_6_ = f32[28,8,256]{2,1,0:T(8,128)S(1)} custom-call(s32[16,128]{1,0:T(8,128)S(4)} %get-tuple-element.35.refs_0_, f32[10,128]{1,0:T(8,128)S(1)} %pad_maximum_fusion.taper_ref.refs_1_, bf16[16,16,2432]{2,1,0:T(8,128)(2,1)S(1)} %all_to_all.10.plane_ref.refs_2_, bf16[7,16,1664]{2,1,0:T(8,128)(2,1)S(1)} %collective-permute-done.2.refs_3_, ...), custom_call_target="tpu_custom_call" | custom-call | flops 572522496 | bytes 4194304 | tf_op jit(solution)/shard_map/correlate_halo_first/pallas_call | solution.py:448
  51.2 0.9 %collective-permute-done.1.refs_3_ = bf16[7,16,768]{2,1,0:T(8,128)(2,1)S(1)} collective-permute-done((bf16[7,16,768]{2,1,0:T(8,128)(2,1)S(1)}, bf16[7,16,768]{2,1,0:T(8,128)(2,1)S(1)}, u32[]{:S(2)}, u32[]{:S(2)}) %collective-permute-start.1) | collective-permute-done | bytes 172064 | tf_op jit(solution)/shard_map/ppermute | solution.py:494
  52.1 0.7 correlate_halo_second.1
  52.8 12.2 %all_to_all.11 = bf16[16,4,8,256]{3,2,1,0:T(8,128)(2,1)S(1)} all-to-all(bf16[16,4,8,256]{3,2,1,0:T(8,128)(2,1)S(1)} %bitcast.15), channel_id=1, replica_groups=mesh['row'=8,'col'=16,'tm'=2] {'col'}, dimensions={0} | all-to-all | bytes 524288 | tf_op jit(solution)/shard_map/all_to_all | solution.py:525
  65.1 0.8 %copy_bitcast_fusion = f32[1,4,128,256]{3,2,1,0:T(8,128)} fusion(bf16[16,4,8,256]{3,2,1,0:T(8,128)(2,1)S(1)} %all_to_all.11), kind=kLoop, calls=%fused_computation.1 | loop fusion | flops 131072 | bytes 786432 | tf_op jit(solution)/shard_map/reshape | solution.py:526
  (7 shorter events, 0.2 us)
Async XLA Ops:
  0.0 7.2 %copy-start.2 = (f32[1200]{0:T(1024)S(1)}, f32[1200]{0:T(1024)}, u32[]{:S(2)}) copy-start(f32[1200]{0:T(1024)} %taper_ref.1) | copy-start | bytes 14404
  0.0 7.2 %copy-start.3 = (s32[1,4]{1,0:T(1,128)S(1)}, s32[1,4]{1,0:T(1,128)}, u32[]{:S(2)}) copy-start(s32[1,4]{1,0:T(1,128)} %pairs_ref.1) | copy-start | bytes 52
  7.1 2.1 %collective-permute-start = (bf16[128,2432]{1,0:T(8,128)(2,1)S(1)}, bf16[128,2432]{1,0:T(8,128)(2,1)S(1)}, u32[]{:S(2)}, u32[]{:S(2)}) collective-permute-start(bf16[128,2432]{1,0:T(8,128)(2,1)S(1)} %get-tuple-element.31), channel_id=1, source_target_pairs={{0,1},{1,0},{2,3},{3,2},{4,5},{5,4},{6,7},{7,6},{8,9},{9,8},{10,11... | collective-permute-start | bytes 1867784 | tf_op jit(solution)/shard_map/ppermute | solution.py:469
  35.5 2.8 %copy-start = (bf16[2432,256]{1,0:T(8,128)(2,1)S(1)}, bf16[2432,256]{1,0:T(8,128)(2,1)}, u32[]{:S(2)}) copy-start(bf16[2432,256]{1,0:T(8,128)(2,1)} %constant.40.clone.low_ref.refs_5_) | copy-start | bytes 3735556
  35.8 14.0 %collective-permute-start.2 = (bf16[7,16,1664]{2,1,0:T(8,128)(2,1)S(1)}, bf16[7,16,1664]{2,1,0:T(8,128)(2,1)S(1)}, u32[]{:S(2)}, u32[]{:S(2)}) collective-permute-start(bf16[7,16,1664]{2,1,0:T(8,128)(2,1)S(1)} %plane_head.2), channel_id=1, source_target_pairs={{32,0},{64,32},{96,64},{128,96},{160,128},{192,160},{224,192},{33,... | collective-permute-start | bytes 1118216 | tf_op jit(solution)/shard_map/ppermute | solution.py:476
  38.3 1.3 %copy-start.1 = (bf16[2432,256]{1,0:T(8,128)(2,1)S(1)}, bf16[2432,256]{1,0:T(8,128)(2,1)}, u32[]{:S(2)}) copy-start(bf16[2432,256]{1,0:T(8,128)(2,1)} %constant.39.clone.high_ref.refs_4_) | copy-start | bytes 3735556
  42.6 9.5 %collective-permute-start.1 = (bf16[7,16,768]{2,1,0:T(8,128)(2,1)S(1)}, bf16[7,16,768]{2,1,0:T(8,128)(2,1)S(1)}, u32[]{:S(2)}, u32[]{:S(2)}) collective-permute-start(bf16[7,16,768]{2,1,0:T(8,128)(2,1)S(1)} %plane_head.3), channel_id=1, source_target_pairs={{32,0},{64,32},{96,64},{128,96},{160,128},{192,160},{224,192},{33,... | collective-permute-start | bytes 516104 | tf_op jit(solution)/shard_map/ppermute | solution.py:494

commit v7 on v6

--- a/solution.py
+++ b/solution.py
@@ -33,61 +33,77 @@
 SIDE = LANES // 2
 WIDE = (TAIL + 1) * LANES
 HALO_PARTS = ((3, FULL, True), (0, 3, False))
-ORDER = (0, 5, 2, 8, 4, 6, 3, 7, 1, 9)
-PAIRS = len(ORDER) // 2 - 1
+BASE = 3
+TURNS = 4
+ORDER = (0, 1, -1, 2, -2, 3, -3, 4, -4, 5)
+ROWS = (1 + 2 * (TURNS + 1)) * BLOCK
 PLANE = 16
 INNER = PLANE - REACH
 MINE = HALF // PLANE
 CHUNKS = 4
 
 
-def residue_bins(residue):
-    first = (residue - FIRST_BIN) % RADIX
-    return FIRST_BIN + first + RADIX * np.arange(PER)
+def lowest_lane(residue):
+    return 0 if residue + RADIX * BASE >= FIRST_BIN else 1
 
 
 def place_in_band(residue):
-    return (residue - FIRST_BIN) % RADIX
-
-
-def angles(steps, residue):
-    phase = steps[:, None] * residue_bins(residue)[None, :] % SAMPLES
-    angle = phase * (2.0 * math.pi / SAMPLES)
-    fill = ((0, 0), (0, LANES - PER))
-    return np.concatenate([np.pad(np.cos(angle), fill), np.pad(-np.sin(angle), fill)], axis=1)
-
-
-def dft_table():
-    columns = [angles(np.arange(PART), residue) for residue in ORDER]
-    chunks = [np.concatenate(columns[i : i + 2], axis=1) for i in range(0, RADIX, 2)]
-    return np.stack(chunks).astype(np.float32).astype(ml_dtypes.bfloat16)
+    return residue + SMOOTH
+
+
+def turn(phase):
+    angle = phase % SAMPLES * (2.0 * math.pi / SAMPLES)
+    return np.cos(angle), -np.sin(angle)
+
+
+def base_table():
+    steps = np.arange(PART)[:, None] * (RADIX * (BASE + np.arange(LANES)))[None, :]
+    return np.concatenate(turn(steps), axis=1).astype(np.float32).astype(ml_dtypes.bfloat16)
+
+
+def twiddles():
+    steps = np.arange(1, TURNS + 2)[:, None] * np.arange(PART)[None, :]
+    return np.stack(turn(steps), axis=1).reshape(-1, PART).astype(np.float32)
 
 
 def lag_tables():
     lag_steps = np.arange(LAGS) - LAGS // 2 + SAMPLES
     factor = RESCALE / math.sqrt(FREQS * WINDOWS)
-    rows = [angles(lag_steps, residue).T for residue in ORDER]
-    last = rows[FULL].reshape(2, LANES, LAGS)
-    for place in range(FULL):
-        for side in range(2):
-            spare = slice(side * LANES + PER, (side + 1) * LANES)
-            rows[place][spare] = last[side, place * SPARE : (place + 1) * SPARE]
+    rows = []
+    for residue in ORDER:
+        bins = residue + RADIX * (BASE + lowest_lane(residue) + np.arange(PER))
+        rows.append(np.stack(turn(bins[:, None] * lag_steps[None, :])))
+    blocks = []
+    for place, residue in enumerate(ORDER[:FULL]):
+        spare = rows[FULL][:, place * SPARE : (place + 1) * SPARE]
+        block = np.concatenate([rows[place], spare], axis=1)
+        blocks.append(np.roll(block, lowest_lane(residue), axis=1).reshape(-1, LAGS))
     tail = np.zeros((2, SIDE, LAGS))
-    tail[:, :REST] = last[:, FULL * SPARE : PER]
-    table = np.concatenate(rows[:FULL] + [tail.reshape(LANES, LAGS)]) * factor
+    tail[:, :REST] = rows[FULL][:, FULL * SPARE :]
+    table = np.concatenate(blocks + [tail.reshape(LANES, LAGS)]) * factor
     table = table.astype(np.float32)
     high = table.astype(ml_dtypes.bfloat16)
     low = (table - high.astype(np.float32)).astype(ml_dtypes.bfloat16)
     return high, low
 
 
-def taper_columns(squared):
-    parts = squared.reshape(PER, RADIX).T
-    parts = [parts[place_in_band(residue)] for residue in ORDER]
-    spare = parts[FULL][: FULL * SPARE].reshape(FULL, SPARE)
-    full = jnp.concatenate([jnp.stack(parts[:FULL]), spare], axis=1)
-    tail = jnp.pad(parts[FULL][FULL * SPARE :], (0, SIDE - REST))
-    return jnp.concatenate([full, jnp.concatenate([tail, tail])[None]], axis=0)
+def taper_columns(square_ref, taper_ref):
+    rows = jnp.transpose(square_ref[...])
+    lane = lax.broadcasted_iota(jnp.int32, (1, LANES), 1)
+    spare = [lane >= PER, (lane > PER) | (lane < 1)]
+
+    def row(residue):
+        index = residue + RADIX * (BASE + lowest_lane(residue)) - FIRST_BIN
+        return rows[index : index + 1, :]
+
+    last = row(ORDER[FULL])
+    for place, residue in enumerate(ORDER[:FULL]):
+        low = lowest_lane(residue)
+        own = pltpu.roll(row(residue), 1, 1) if low else row(residue)
+        moved = pltpu.roll(last, PER + low - place * SPARE, 1)
+        taper_ref[place : place + 1, :] = jnp.where(spare[low], moved, own)
+    moved = [pltpu.roll(last, LANES + side * SIDE - FULL * SPARE, 1) for side in range(2)]
+    taper_ref[FULL : FULL + 1, :] = jnp.where(lane < SIDE, moved[0], moved[1])
 
 
 def five_point(x):
@@ -105,7 +121,17 @@
 
 
 def dft_kernel(
-    x_hbm, table_hbm, theirs_ref, real_ref, pair_ref, x_ref, table_ref, y_ref, x_sems, t_sems
+    x_hbm,
+    table_hbm,
+    turn_hbm,
+    theirs_ref,
+    sums_ref,
+    x_ref,
+    table_ref,
+    turn_ref,
+    y_ref,
+    x_sems,
+    t_sems,
 ):
     core = lax.axis_index("tm")
     size = BLOCK // CHUNKS
@@ -115,11 +141,9 @@
         )
         for c in range(CHUNKS)
     ]
-    t_copies = [
-        pltpu.make_async_copy(table_hbm.at[c], table_ref.at[c], t_sems.at[c])
-        for c in range(PAIRS + 1)
-    ]
-    for copy in x_copies:
+    turn_copy = pltpu.make_async_copy(turn_hbm, turn_ref, t_sems.at[0])
+    table_copy = pltpu.make_async_copy(table_hbm, table_ref, t_sems.at[1])
+    for copy in [turn_copy] + x_copies + [table_copy]:
         copy.start()
 
     def split(i, carry):
@@ -131,38 +155,35 @@
             ]
             even = five_point([x[n] + x[n + 5] for n in range(5)])
             odd = five_point([x[n] - x[n + 5] if n % 2 == 0 else x[n + 5] - x[n] for n in range(5)])
-            parts = (even[0], odd[0]) + even[1:] + odd[1:]
+            sums = [(odd[3], -odd[4]), even[1:3], (odd[1], -odd[2]), even[3:5]]
+            parts = [even[0]]
+            for r in range(TURNS + 1):
+                cos = turn_ref[2 * r : 2 * r + 1, lane : lane + LANES]
+                sin = turn_ref[2 * r + 1 : 2 * r + 2, lane : lane + LANES]
+                if r < TURNS:
+                    real, imag = sums[r]
+                    parts += [real * cos + imag * sin, real * sin - imag * cos]
+                else:
+                    parts += [odd[0] * cos, odd[0] * sin]
             for n, part in enumerate(parts):
                 y_ref[
                     pl.ds(pl.multiple_of(n * BLOCK + i * 16, 16), 16), lane : lane + LANES
                 ] = part.astype(jnp.bfloat16)
         return carry
 
+    turn_copy.wait()
     for c in range(CHUNKS):
         x_copies[c].wait()
-        if c == CHUNKS - 2:
-            for copy in t_copies:
-                copy.start()
         lax.fori_loop(c * size // 16, (c + 1) * size // 16, split, 0, unroll=2)
 
-    t_copies[0].wait()
-    for n in range(2):
-        real_ref[n] = jnp.dot(
-            y_ref[n * BLOCK : (n + 1) * BLOCK, :],
-            table_ref[0, :, n * 2 * LANES : (n + 1) * 2 * LANES],
-            preferred_element_type=jnp.float32,
-        )
-    for n in range(PAIRS):
-        t_copies[n + 1].wait()
-        pair_ref[n] = jnp.dot(
-            y_ref[(n + 1) * 2 * BLOCK : (n + 2) * 2 * BLOCK, :],
-            table_ref[n + 1],
-            preferred_element_type=jnp.float32,
-        )
+    table_copy.wait()
+    for begin in range(0, ROWS, 2 * BLOCK):
+        at = slice(begin, min(begin + 2 * BLOCK, ROWS))
+        sums_ref[at] = jnp.dot(y_ref[at], table_ref[...], preferred_element_type=jnp.float32)
 
     def rows(i, carry):
         row = (1 - core) * HALF + i * 16
-        parts = [white_rows(real_ref, pair_ref, row + j * MINE) for j in range(2)]
+        parts = [white_rows(sums_ref, row + j * MINE) for j in range(2)]
         for n in range(TAIL + 1):
             theirs_ref[pl.ds(pl.multiple_of(i * 16, 16), 16), n * LANES : (n + 1) * LANES] = (
                 jnp.concatenate([parts[0][n], parts[1][n]], axis=0).astype(jnp.bfloat16)
@@ -172,28 +193,28 @@
     lax.fori_loop(0, HALF // 16, rows, 0, unroll=2)
 
 
-def spectrum_part(real_ref, pair_ref, row, place):
-    at = pl.ds(pl.multiple_of(row, MINE), MINE)
-    if place < 2:
-        return real_ref[place, at, :LANES], real_ref[place, at, LANES:]
-    n, side = (place - 2) // 2, place % 2
-    plain = (side == 0) == (n < PAIRS // 2)
-    under = pl.ds(pl.multiple_of(row + BLOCK, MINE), MINE)
-    first = slice(2 * side * LANES, (2 * side + 1) * LANES)
-    second = slice((2 * side + 1) * LANES, (2 * side + 2) * LANES)
-    u_cos, u_sin = pair_ref[n, at, first], pair_ref[n, at, second]
-    v_cos, v_sin = pair_ref[n, under, first], pair_ref[n, under, second]
-    if plain:
-        return u_cos + v_sin, u_sin - v_cos
-    return u_cos - v_sin, u_sin + v_cos
-
-
-def white_rows(real_ref, pair_ref, row):
+def spectrum_parts(sums_ref, row):
+    def load(index):
+        at = pl.ds(pl.multiple_of(index * BLOCK + row, MINE), MINE)
+        return sums_ref[at, :LANES], sums_ref[at, LANES:]
+
+    parts = [load(0)]
+    for r in range(TURNS + 1):
+        (real_cos, real_sin), (imag_cos, imag_sin) = load(1 + 2 * r), load(2 + 2 * r)
+        parts.append((real_cos - imag_sin, real_sin + imag_cos))
+        if r < TURNS:
+            parts.append((real_cos + imag_sin, real_sin - imag_cos))
+    return parts
+
+
+def white_rows(sums_ref, row):
+    lane = lax.broadcasted_iota(jnp.int32, (MINE, LANES), 1)
+    spare = [lane >= PER, (lane > PER) | (lane < 1)]
     band = [None] * RADIX
-    for place, residue in enumerate(ORDER):
-        re, im = spectrum_part(real_ref, pair_ref, row, place)
+    for residue, (re, im) in zip(ORDER, spectrum_parts(sums_ref, row)):
         square = re * re + im * im
-        band[place_in_band(residue)] = square * lax.rsqrt(jnp.maximum(square, 1e-30))
+        amplitude = square * lax.rsqrt(jnp.maximum(square, 1e-30))
+        band[place_in_band(residue)] = jnp.where(spare[lowest_lane(residue)], 0.0, amplitude)
     total = band[0]
     for amplitude in band[1:]:
         total = total + amplitude
@@ -203,26 +224,27 @@
     two = [line[i] + line[i + 1] for i in range(len(line) - 1)]
     four = [two[i] + two[i + 2] for i in range(len(two) - 2)]
     out = []
-    for place, residue in enumerate(ORDER):
+    for residue, (re, im) in zip(ORDER, spectrum_parts(sums_ref, row)):
         i = place_in_band(residue)
         smoothed = (four[i] + four[i + 4] + line[i + 8]) * (1.0 / (2 * SMOOTH + 1))
         level = smoothed + floor
         scale = pl.reciprocal(level, approx=True)
         scale = scale * (2.0 - level * scale)
-        re, im = spectrum_part(real_ref, pair_ref, row, place)
         out += [re * scale, im * scale]
-    lane = lax.broadcasted_iota(jnp.int32, (MINE, LANES), 1)
     last = out[TAIL:]
-    for place in range(FULL):
+    for place, residue in enumerate(ORDER[:FULL]):
+        low = lowest_lane(residue)
         for side in range(2):
-            moved = pltpu.roll(last[side], PER - place * SPARE, 1)
+            moved = pltpu.roll(last[side], PER + low - place * SPARE, 1)
             here = 2 * place + side
-            out[here] = jnp.where(lane >= PER, moved, out[here])
-    moved = [pltpu.roll(last[0], LANES - FULL * SPARE, 1), pltpu.roll(last[1], LANES + SIDE - FULL * SPARE, 1)]
+            out[here] = jnp.where(spare[low], moved, out[here])
+    moved = [
+        pltpu.roll(last[side], LANES + side * SIDE - FULL * SPARE, 1) for side in range(2)
+    ]
     return out[:TAIL] + [jnp.where(lane < SIDE, moved[0], moved[1])]
 
 
-def own_kernel(pairs_ref, taper_ref, real_ref, pair_ref, mine_ref, squared_ref):
+def own_kernel(pairs_ref, taper_ref, sums_ref, mine_ref, squared_ref):
     squared_ref[...] = taper_ref[...] * taper_ref[...]
     core = lax.axis_index("tm")
     block = lax.axis_index("row") * PLANE + lax.axis_index("col")
@@ -234,7 +256,7 @@
         offsets = jnp.where(lane == REST + k, offset, offsets)
 
     def rows(j, carry):
-        parts = white_rows(real_ref, pair_ref, core * HALF + j * MINE)
+        parts = white_rows(sums_ref, core * HALF + j * MINE)
         parts[TAIL] = jnp.where((lane >= REST) & (lane < SIDE), offsets, parts[TAIL])
         for n, part in enumerate(parts):
             mine_ref[j, :, n * LANES : (n + 1) * LANES] = jnp.concatenate(
@@ -252,32 +274,36 @@
 def spectra(series):
     hbm = pl.BlockSpec(memory_space=pltpu.HBM)
     vmem = pl.BlockSpec(memory_space=pltpu.VMEM)
+    operands = [
+        pltpu.with_memory_space_constraint(a, pltpu.HBM)
+        for a in (series, jnp.asarray(base_table()), jnp.asarray(twiddles()))
+    ]
     return pl.pallas_call(
         dft_kernel,
-        in_specs=[hbm, hbm],
-        out_specs=[vmem, vmem, vmem],
+        in_specs=[hbm, hbm, hbm],
+        out_specs=[vmem, vmem],
         out_shape=[
             pltpu.VMEM((HALF, WIDE), jnp.bfloat16),
-            pltpu.VMEM((2, BLOCK, 2 * LANES), jnp.float32),
-            pltpu.VMEM((PAIRS, 2 * BLOCK, 4 * LANES), jnp.float32),
+            pltpu.VMEM((ROWS, 2 * LANES), jnp.float32),
         ],
         scratch_shapes=[
             pltpu.VMEM((BLOCK, SAMPLES), jnp.bfloat16),
-            pltpu.VMEM((PAIRS + 1, PART, 4 * LANES), jnp.bfloat16),
-            pltpu.VMEM((RADIX * BLOCK, PART), jnp.bfloat16),
+            pltpu.VMEM((PART, 2 * LANES), jnp.bfloat16),
+            pltpu.VMEM((2 * (TURNS + 1), PART), jnp.float32),
+            pltpu.VMEM((ROWS, PART), jnp.bfloat16),
             pltpu.SemaphoreType.DMA((CHUNKS,)),
-            pltpu.SemaphoreType.DMA((PAIRS + 1,)),
+            pltpu.SemaphoreType.DMA((2,)),
         ],
-        compiler_params=pltpu.CompilerParams(vmem_limit_bytes=20 << 20),
+        compiler_params=pltpu.CompilerParams(vmem_limit_bytes=16 << 20),
         name="dft_whiten",
-    )(*[pltpu.with_memory_space_constraint(a, pltpu.HBM) for a in (series, jnp.asarray(dft_table()))])
-
-
-def own_half(pairs, taper, real, pair):
+    )(*operands)
+
+
+def own_half(pairs, taper, sums):
     vmem = pl.BlockSpec(memory_space=pltpu.VMEM)
     return pl.pallas_call(
         own_kernel,
-        in_specs=[pl.BlockSpec(memory_space=pltpu.SMEM), vmem, vmem, vmem],
+        in_specs=[pl.BlockSpec(memory_space=pltpu.SMEM), vmem, vmem],
         out_specs=[vmem, vmem],
         out_shape=[
             pltpu.VMEM((PLANE, 2 * MINE, WIDE), jnp.bfloat16),
@@ -288,7 +314,7 @@
             flops=40 * HALF * WIDE, bytes_accessed=5 << 20, transcendentals=0
         ),
         name="whiten_own",
-    )(pairs, taper, in_vmem(real), in_vmem(pair))
+    )(pairs, taper, in_vmem(sums))
 
 
 def part_columns(part):
@@ -390,7 +416,18 @@
 
 
 def inner_kernel(
-    taper_ref, plane_ref, high_ref, low_ref, out_ref, scalar_ref, xh_ref, xl_ref, number_ref, sem
+    squared_ref,
+    plane_ref,
+    high_ref,
+    low_ref,
+    out_ref,
+    scalar_ref,
+    taper_ref,
+    xh_ref,
+    xl_ref,
+    number_ref,
+    sem,
+    square_ref,
 ):
     for a in range(PLANE):
         number_ref[a : a + 1, :] = (
@@ -398,6 +435,9 @@
         )
     numbers = pltpu.make_async_copy(number_ref, scalar_ref, sem)
     numbers.start()
+    square_ref[...] = jnp.zeros_like(square_ref)
+    square_ref[:PER, :RADIX] = squared_ref[...]
+    taper_columns(square_ref, taper_ref)
     numbers.wait()
     lagged = cross_and_lag(
         0, INNER, (0, FULL, True), taper_ref, plane_ref, high_ref, low_ref, scalar_ref, xh_ref, xl_ref
@@ -440,8 +480,9 @@
     operands = [in_vmem(operand) for operand in operands]
     in_specs = [vmem] * len(operands)
     if scalars is None:
-        out_specs.append(smem)
+        out_specs += [smem, vmem]
         out_shape.append(pltpu.SMEM((PLANE, LANES), jnp.int32))
+        out_shape.append(pltpu.VMEM((RADIX, LANES), jnp.float32))
     else:
         in_specs.insert(0, smem)
         operands.insert(0, pltpu.with_memory_space_constraint(scalars, pltpu.SMEM))
@@ -465,20 +506,20 @@
 
 
 def per_device(records, taper, pairs):
-    theirs, real, pair = spectra(records[0])
+    theirs, sums = spectra(records[0])
     got = lax.ppermute(theirs, "tm", [(0, 1), (1, 0)])
-    mine, squared = own_half(pairs, taper, real, pair)
+    mine, squared = own_half(pairs, taper, sums)
     send = mine.at[:, MINE:].set(got.reshape(PLANE, MINE, WIDE))
     plane = lax.all_to_all(send, "col", 0, 0, tiled=True)
     count = lax.axis_size("row")
     down = [(z, z - 1) for z in range(1, count)]
     head, squared = lax.optimization_barrier((plane_head(plane, HALO_PARTS[0]), squared))
     halos = [lax.ppermute(head, "row", down)]
-    squared = taper_columns(squared)
+    squared = squared.reshape(PER, RADIX)
     high, low = (jnp.asarray(table) for table in lag_tables())
     widths = [part_width(part) for part in HALO_PARTS]
     w = [[pltpu.VMEM((2 * REACH, 2 * MINE, width), jnp.bfloat16)] for width in widths]
-    lagged, scalars = correlated_call(
+    lagged, scalars, columns = correlated_call(
         inner_kernel,
         "correlate_inner",
         None,
@@ -487,7 +528,11 @@
         INNER,
         WIDE,
         {},
-        [pltpu.VMEM((PLANE, LANES), jnp.int32), pltpu.SemaphoreType.DMA(())],
+        [
+            pltpu.VMEM((PLANE, LANES), jnp.int32),
+            pltpu.SemaphoreType.DMA(()),
+            pltpu.VMEM((LANES, LANES), jnp.float32),
+        ],
     )
 
     later, scalars = lax.optimization_barrier((plane, scalars))
@@ -503,7 +548,7 @@
         first,
         "correlate_halo_first",
         scalars,
-        [squared, plane, halos[0], high, low],
+        [columns, plane, halos[0], high, low],
         REACH,
         REACH,
         widths[0],
@@ -514,7 +559,7 @@
         second,
         "correlate_halo_second",
         scalars,
-        [squared, plane, halos[1], high, low, partial, lagged],
+        [columns, plane, halos[1], high, low, partial, lagged],
         PLANE,
         REACH,
         widths[1],

time: 66.1 us -> 65.2 us (0.986)
  no operation moved by 1% of the time
where the time goes in v7:
time: 65.2 us; the launch traced here: 65 us
  blocking collectives  38.4 us (59%)
  Pallas kernels  13.2 us (20%)
  waiting for transfers between devices  6.55 us (10%)
  starting transfers between devices  4.26 us (7%)
  local copies, waits for them, and re-layouts  1.49 us (2%)
  other arithmetic  0.86 us (1%)
    all_to_all x1, blocking collectives, per_device(): plane = lax.all_to_all(send, 'col', 0, 0, tiled=True)  26.2 us
    all_to_all x1, blocking collectives, per_device(): lax.all_to_all(lagged.astype(jnp.bfloat16), 'col', 0, 0, tiled=True)  12.2 us
    pallas_call x1, Pallas kernels, spectra(): pl.pallas_call(dft_kernel, in_specs=[hbm, hbm, hbm], out_specs=[vmem, vme...  6.45 us
    ppermute x1, waiting for transfers between devices, per_device(): halos = [lax.ppermute(head, 'row', down)]  5.29 us
    pallas_call x3, Pallas kernels, correlated_call(): pl.pallas_call(body, in_specs=in_specs, out_specs=out_specs, out_shape=ou...  5.12 us
    ppermute x1, starting transfers between devices, per_device(): halos = [lax.ppermute(head, 'row', down)]  2.15 us
    ppermute x1, starting transfers between devices, per_device(): halos.append(lax.ppermute(plane_head(later, HALO_PARTS[1]), 'row', down))  2.02 us
    pallas_call x1, Pallas kernels, own_half(): pl.pallas_call(own_kernel, in_specs=[pl.BlockSpec(memory_space=pltpu.SMEM...  1.63 us
  transfers between devices with their start and end apart: 3, of which 3 were waited for; matrix products, arithmetic and copies ran while one was open for 0% of the time, Pallas kernels for 9%

profile of v7, /device:TPU:96, one launch (start us, length us, event | category | flops | bytes accessed | tf_op | source)
XLA Modules:
  0.0 65.0 jit_solution(18357300482765743097)
XLA Ops:
  0.0 0.0 copy-start.2
  0.0 0.0 copy-start.3
  0.0 6.5 %dft_whiten.1 = (bf16[128,2432]{1,0:T(8,128)(2,1)S(1)}, f32[2816,256]{1,0:T(8,128)S(1)}) custom-call(bf16[256,7680]{1,0:T(8,128)(2,1)} %bitcast.9, bf16[768,256]{1,0:T(8,128)(2,1)} %constant.37.clone.table_hbm, f32[10,768]{1,0:T(8,128)} %constant.38.clone.turn_hbm), custom_call_target="tpu_custom_call" | custom-call | tf_op jit(solution)/shard_map/dft_whiten/pallas_call | solution.py:281
  6.5 0.1 collective-permute-start
  6.6 0.0 copy-done.2
  6.6 0.0 copy-done.3
  6.6 1.6 %whiten_own.1 = (bf16[16,16,2432]{2,1,0:T(8,128)(2,1)S(1)}, f32[1200]{0:T(1024)S(1)}) custom-call(s32[1,4]{1,0:T(1,128)S(1)} %copy-done.3, f32[1200]{0:T(1024)S(1)} %copy-done.2, f32[2816,256]{1,0:T(8,128)S(1)} %get-tuple-element.28.sums_ref), custom_call_target="tpu_custom_call" | custom-call | flops 12451840 | bytes 5242880 | tf_op jit(solution)/shard_map/whiten_own/pallas_call | solution.py:304
  8.2 0.4 collective-permute-done
  8.6 0.1 bitcast_dynamic-update-slice_fusion
  8.7 26.2 %all_to_all.10.plane_ref.refs_2_ = bf16[16,16,2432]{2,1,0:T(8,128)(2,1)S(1)} all-to-all(bf16[16,16,2432]{2,1,0:T(8,128)(2,1)S(1)} %bitcast_dynamic-update-slice_fusion), channel_id=1, replica_groups=mesh['row'=8,'col'=16,'tm'=2] {'col'}, dimensions={0} | all-to-all | bytes 2490368 | tf_op jit(solution)/shard_map/all_to_all | solution.py:513
  34.9 0.0 copy-start
  34.9 2.1 %collective-permute-start.2 = (bf16[7,16,1664]{2,1,0:T(8,128)(2,1)S(1)}, bf16[7,16,1664]{2,1,0:T(8,128)(2,1)S(1)}, u32[]{:S(2)}, u32[]{:S(2)}) collective-permute-start(bf16[7,16,1664]{2,1,0:T(8,128)(2,1)S(1)} %plane_head.2), channel_id=1, source_target_pairs={{32,0},{64,32},{96,64},{128,96},{160,128},{192,160},{224,192},{33,... | collective-permute-start | bytes 1118216 | tf_op jit(solution)/shard_map/ppermute | solution.py:517
  37.0 0.1 reshape.46.squared_ref
  37.2 0.0 copy-done
  37.2 0.0 copy-start.1
  37.2 1.3 %copy-done.1 = bf16[2432,256]{1,0:T(8,128)(2,1)S(1)} copy-done((bf16[2432,256]{1,0:T(8,128)(2,1)S(1)}, bf16[2432,256]{1,0:T(8,128)(2,1)}, u32[]{:S(2)}) %copy-start.1) | copy-done | bytes 1245208
  38.5 3.1 %correlate_inner.1 = (f32[64,8,256]{2,1,0:T(8,128)S(1)}, s32[16,128]{1,0:T(8,128)S(4)}, f32[10,128]{1,0:T(8,128)S(1)}) custom-call(f32[120,10]{1,0:T(8,128)S(1)} %reshape.46.squared_ref, bf16[16,16,2432]{2,1,0:T(8,128)(2,1)S(1)} %all_to_all.10.plane_ref.refs_2_, bf16[2432,256]{1,0:T(8,128)(2,1)S(1)} %copy-done.1, bf16[2432,256]{1,0:T(8,128)(2,1)S(1)} %copy-done), custom_call_target="tpu_custom_call" | custom-call | flops 1075838976 | bytes 4194304 | tf_op jit(solution)/shard_map/correlate_inner/pallas_call | solution.py:489
  41.6 2.0 %collective-permute-start.1 = (bf16[7,16,768]{2,1,0:T(8,128)(2,1)S(1)}, bf16[7,16,768]{2,1,0:T(8,128)(2,1)S(1)}, u32[]{:S(2)}, u32[]{:S(2)}) collective-permute-start(bf16[7,16,768]{2,1,0:T(8,128)(2,1)S(1)} %plane_head.3), channel_id=1, source_target_pairs={{32,0},{64,32},{96,64},{128,96},{160,128},{192,160},{224,192},{33,... | collective-permute-start | bytes 516104 | tf_op jit(solution)/shard_map/ppermute | solution.py:539
  43.6 5.3 %collective-permute-done.2.refs_3_ = bf16[7,16,1664]{2,1,0:T(8,128)(2,1)S(1)} collective-permute-done((bf16[7,16,1664]{2,1,0:T(8,128)(2,1)S(1)}, bf16[7,16,1664]{2,1,0:T(8,128)(2,1)S(1)}, u32[]{:S(2)}, u32[]{:S(2)}) %collective-permute-start.2) | collective-permute-done | bytes 372768 | tf_op jit(solution)/shard_map/ppermute | solution.py:517
  48.9 1.4 %correlate_halo_first.1.refs_6_ = f32[28,8,256]{2,1,0:T(8,128)S(1)} custom-call(s32[16,128]{1,0:T(8,128)S(4)} %get-tuple-element.34.refs_0_, f32[10,128]{1,0:T(8,128)S(1)} %get-tuple-element.35.refs_1_, bf16[16,16,2432]{2,1,0:T(8,128)(2,1)S(1)} %all_to_all.10.plane_ref.refs_2_, bf16[7,16,1664]{2,1,0:T(8,128)(2,1)S(1)} %collective-permute-done.2.refs_3_, ...), custom_call_target="tpu_custom_call" | custom-call | flops 572522496 | bytes 4194304 | tf_op jit(solution)/shard_map/correlate_halo_first/pallas_call | solution.py:489
  50.3 0.9 %collective-permute-done.1.refs_3_ = bf16[7,16,768]{2,1,0:T(8,128)(2,1)S(1)} collective-permute-done((bf16[7,16,768]{2,1,0:T(8,128)(2,1)S(1)}, bf16[7,16,768]{2,1,0:T(8,128)(2,1)S(1)}, u32[]{:S(2)}, u32[]{:S(2)}) %collective-permute-start.1) | collective-permute-done | bytes 172064 | tf_op jit(solution)/shard_map/ppermute | solution.py:539
  51.2 0.6 correlate_halo_second.1
  51.9 12.2 %all_to_all.11 = bf16[16,4,8,256]{3,2,1,0:T(8,128)(2,1)S(1)} all-to-all(bf16[16,4,8,256]{3,2,1,0:T(8,128)(2,1)S(1)} %bitcast.10), channel_id=1, replica_groups=mesh['row'=8,'col'=16,'tm'=2] {'col'}, dimensions={0} | all-to-all | bytes 524288 | tf_op jit(solution)/shard_map/all_to_all | solution.py:570
  64.1 0.8 %copy_bitcast_fusion = f32[1,4,128,256]{3,2,1,0:T(8,128)} fusion(bf16[16,4,8,256]{3,2,1,0:T(8,128)(2,1)S(1)} %all_to_all.11), kind=kLoop, calls=%fused_computation.1 | loop fusion | flops 131072 | bytes 786432 | tf_op jit(solution)/shard_map/reshape | solution.py:571
  (3 shorter events, 0.1 us)
Async XLA Ops:
  0.0 6.6 %copy-start.2 = (f32[1200]{0:T(1024)S(1)}, f32[1200]{0:T(1024)}, u32[]{:S(2)}) copy-start(f32[1200]{0:T(1024)} %taper_ref.1) | copy-start | bytes 14404
  0.0 6.6 %copy-start.3 = (s32[1,4]{1,0:T(1,128)S(1)}, s32[1,4]{1,0:T(1,128)}, u32[]{:S(2)}) copy-start(s32[1,4]{1,0:T(1,128)} %pairs_ref.1) | copy-start | bytes 52
  6.5 2.1 %collective-permute-start = (bf16[128,2432]{1,0:T(8,128)(2,1)S(1)}, bf16[128,2432]{1,0:T(8,128)(2,1)S(1)}, u32[]{:S(2)}, u32[]{:S(2)}) collective-permute-start(bf16[128,2432]{1,0:T(8,128)(2,1)S(1)} %get-tuple-element.30), channel_id=1, source_target_pairs={{0,1},{1,0},{2,3},{3,2},{4,5},{5,4},{6,7},{7,6},{8,9},{9,8},{10,11... | collective-permute-start | bytes 1867784 | tf_op jit(solution)/shard_map/ppermute | solution.py:510
  34.9 2.3 %copy-start = (bf16[2432,256]{1,0:T(8,128)(2,1)S(1)}, bf16[2432,256]{1,0:T(8,128)(2,1)}, u32[]{:S(2)}) copy-start(bf16[2432,256]{1,0:T(8,128)(2,1)} %constant.40.clone.low_ref.refs_5_) | copy-start | bytes 3735556
  34.9 14.0 %collective-permute-start.2 = (bf16[7,16,1664]{2,1,0:T(8,128)(2,1)S(1)}, bf16[7,16,1664]{2,1,0:T(8,128)(2,1)S(1)}, u32[]{:S(2)}, u32[]{:S(2)}) collective-permute-start(bf16[7,16,1664]{2,1,0:T(8,128)(2,1)S(1)} %plane_head.2), channel_id=1, source_target_pairs={{32,0},{64,32},{96,64},{128,96},{160,128},{192,160},{224,192},{33,... | collective-permute-start | bytes 1118216 | tf_op jit(solution)/shard_map/ppermute | solution.py:517
  37.2 1.3 %copy-start.1 = (bf16[2432,256]{1,0:T(8,128)(2,1)S(1)}, bf16[2432,256]{1,0:T(8,128)(2,1)}, u32[]{:S(2)}) copy-start(bf16[2432,256]{1,0:T(8,128)(2,1)} %constant.39.clone.high_ref.refs_4_) | copy-start | bytes 3735556
  41.6 9.6 %collective-permute-start.1 = (bf16[7,16,768]{2,1,0:T(8,128)(2,1)S(1)}, bf16[7,16,768]{2,1,0:T(8,128)(2,1)S(1)}, u32[]{:S(2)}, u32[]{:S(2)}) collective-permute-start(bf16[7,16,768]{2,1,0:T(8,128)(2,1)S(1)} %plane_head.3), channel_id=1, source_target_pairs={{32,0},{64,32},{96,64},{128,96},{160,128},{192,160},{224,192},{33,... | collective-permute-start | bytes 516104 | tf_op jit(solution)/shard_map/ppermute | solution.py:539

commit v8 on v7

--- a/solution.py
+++ b/solution.py
@@ -36,7 +36,8 @@
 BASE = 3
 TURNS = 4
 ORDER = (0, 1, -1, 2, -2, 3, -3, 4, -4, 5)
-ROWS = (1 + 2 * (TURNS + 1)) * BLOCK
+PRODUCTS = 1 + 2 * TURNS
+FINE = 256
 PLANE = 16
 INNER = PLANE - REACH
 MINE = HALF // PLANE
@@ -56,13 +57,19 @@
     return np.cos(angle), -np.sin(angle)
 
 
-def base_table():
-    steps = np.arange(PART)[:, None] * (RADIX * (BASE + np.arange(LANES)))[None, :]
-    return np.concatenate(turn(steps), axis=1).astype(np.float32).astype(ml_dtypes.bfloat16)
+def dft_tables():
+    def table(residue):
+        steps = np.arange(PART)[:, None] * (residue + RADIX * (BASE + np.arange(LANES)))[None, :]
+        return np.concatenate(turn(steps), axis=1).astype(np.float32)
+
+    base, last = table(0), table(ORDER[-1])
+    high = base.astype(ml_dtypes.bfloat16)
+    low = (base - high.astype(np.float32))[:FINE].astype(ml_dtypes.bfloat16)
+    return np.concatenate([high, last.astype(ml_dtypes.bfloat16), low])
 
 
 def twiddles():
-    steps = np.arange(1, TURNS + 2)[:, None] * np.arange(PART)[None, :]
+    steps = np.arange(1, TURNS + 1)[:, None] * np.arange(PART)[None, :]
     return np.stack(turn(steps), axis=1).reshape(-1, PART).astype(np.float32)
 
 
@@ -129,12 +136,15 @@
     x_ref,
     table_ref,
     turn_ref,
-    y_ref,
+    even_ref,
+    odd_ref,
+    last_ref,
     x_sems,
     t_sems,
 ):
     core = lax.axis_index("tm")
     size = BLOCK // CHUNKS
+    y_refs = (even_ref, odd_ref)
     x_copies = [
         pltpu.make_async_copy(
             x_hbm.at[pl.ds(c * size, size)], x_ref.at[pl.ds(c * size, size)], x_sems.at[c]
@@ -146,8 +156,9 @@
     for copy in [turn_copy] + x_copies + [table_copy]:
         copy.start()
 
-    def split(i, carry):
-        at = pl.ds(pl.multiple_of(i * 16, 16), 16)
+    def split(c, i):
+        y_ref = y_refs[c % 2]
+        at = slice(c * size + i * 16, c * size + (i + 1) * 16)
         for lane in range(0, PART, LANES):
             x = [
                 x_ref[at, n * PART + lane : n * PART + lane + LANES].astype(jnp.float32)
@@ -157,29 +168,43 @@
             odd = five_point([x[n] - x[n + 5] if n % 2 == 0 else x[n + 5] - x[n] for n in range(5)])
             sums = [(odd[3], -odd[4]), even[1:3], (odd[1], -odd[2]), even[3:5]]
             parts = [even[0]]
-            for r in range(TURNS + 1):
+            for r, (real, imag) in enumerate(sums):
                 cos = turn_ref[2 * r : 2 * r + 1, lane : lane + LANES]
                 sin = turn_ref[2 * r + 1 : 2 * r + 2, lane : lane + LANES]
-                if r < TURNS:
-                    real, imag = sums[r]
-                    parts += [real * cos + imag * sin, real * sin - imag * cos]
-                else:
-                    parts += [odd[0] * cos, odd[0] * sin]
+                parts += [real * cos + imag * sin, real * sin - imag * cos]
+            last_ref[at, lane : lane + LANES] = odd[0].astype(jnp.bfloat16)
             for n, part in enumerate(parts):
-                y_ref[
-                    pl.ds(pl.multiple_of(n * BLOCK + i * 16, 16), 16), lane : lane + LANES
-                ] = part.astype(jnp.bfloat16)
-        return carry
+                y_ref[n * size + i * 16 : n * size + (i + 1) * 16, lane : lane + LANES] = part.astype(
+                    jnp.bfloat16
+                )
+
+    def multiply(c):
+        y_ref = y_refs[c % 2]
+        product = jnp.dot(y_ref[...], table_ref[:PART], preferred_element_type=jnp.float32)
+        for n in range(PRODUCTS):
+            sums_ref[n * BLOCK + c * size : n * BLOCK + (c + 1) * size] = product[
+                n * size : (n + 1) * size
+            ]
+        product = jnp.dot(
+            y_ref[size:, :FINE], table_ref[2 * PART :], preferred_element_type=jnp.float32
+        )
+        for n in range(1, PRODUCTS):
+            at = slice(n * BLOCK + c * size, n * BLOCK + (c + 1) * size)
+            sums_ref[at] = sums_ref[at] + product[(n - 1) * size : n * size]
 
     turn_copy.wait()
     for c in range(CHUNKS):
         x_copies[c].wait()
-        lax.fori_loop(c * size // 16, (c + 1) * size // 16, split, 0, unroll=2)
-
-    table_copy.wait()
-    for begin in range(0, ROWS, 2 * BLOCK):
-        at = slice(begin, min(begin + 2 * BLOCK, ROWS))
-        sums_ref[at] = jnp.dot(y_ref[at], table_ref[...], preferred_element_type=jnp.float32)
+        if c == 1:
+            table_copy.wait()
+        if c > 0:
+            multiply(c - 1)
+        for i in range(size // 16):
+            split(c, i)
+    multiply(CHUNKS - 1)
+    sums_ref[PRODUCTS * BLOCK :] = jnp.dot(
+        last_ref[...], table_ref[PART : 2 * PART], preferred_element_type=jnp.float32
+    )
 
     def rows(i, carry):
         row = (1 - core) * HALF + i * 16
@@ -199,12 +224,11 @@
         return sums_ref[at, :LANES], sums_ref[at, LANES:]
 
     parts = [load(0)]
-    for r in range(TURNS + 1):
+    for r in range(TURNS):
         (real_cos, real_sin), (imag_cos, imag_sin) = load(1 + 2 * r), load(2 + 2 * r)
         parts.append((real_cos - imag_sin, real_sin + imag_cos))
-        if r < TURNS:
-            parts.append((real_cos + imag_sin, real_sin - imag_cos))
-    return parts
+        parts.append((real_cos + imag_sin, real_sin - imag_cos))
+    return parts + [load(PRODUCTS)]
 
 
 def white_rows(sums_ref, row):
@@ -276,7 +300,7 @@
     vmem = pl.BlockSpec(memory_space=pltpu.VMEM)
     operands = [
         pltpu.with_memory_space_constraint(a, pltpu.HBM)
-        for a in (series, jnp.asarray(base_table()), jnp.asarray(twiddles()))
+        for a in (series, jnp.asarray(dft_tables()), jnp.asarray(twiddles()))
     ]
     return pl.pallas_call(
         dft_kernel,
@@ -284,13 +308,15 @@
         out_specs=[vmem, vmem],
         out_shape=[
             pltpu.VMEM((HALF, WIDE), jnp.bfloat16),
-            pltpu.VMEM((ROWS, 2 * LANES), jnp.float32),
+            pltpu.VMEM(((PRODUCTS + 1) * BLOCK, 2 * LANES), jnp.float32),
         ],
         scratch_shapes=[
             pltpu.VMEM((BLOCK, SAMPLES), jnp.bfloat16),
-            pltpu.VMEM((PART, 2 * LANES), jnp.bfloat16),
-            pltpu.VMEM((2 * (TURNS + 1), PART), jnp.float32),
-            pltpu.VMEM((ROWS, PART), jnp.bfloat16),
+            pltpu.VMEM((2 * PART + FINE, 2 * LANES), jnp.bfloat16),
+            pltpu.VMEM((2 * TURNS, PART), jnp.float32),
+            pltpu.VMEM((PRODUCTS * BLOCK // CHUNKS, PART), jnp.bfloat16),
+            pltpu.VMEM((PRODUCTS * BLOCK // CHUNKS, PART), jnp.bfloat16),
+            pltpu.VMEM((BLOCK, PART), jnp.bfloat16),
             pltpu.SemaphoreType.DMA((CHUNKS,)),
             pltpu.SemaphoreType.DMA((2,)),
         ],

time: 65.2 us -> 65 us (level)
  no operation moved by 1% of the time
where the time goes in v8:
time: 65 us; the launch traced here: 64.8 us
  blocking collectives  38.4 us (59%)
  Pallas kernels  13 us (20%)
  waiting for transfers between devices  6.55 us (10%)
  starting transfers between devices  4.26 us (7%)
  local copies, waits for them, and re-layouts  1.49 us (2%)
  other arithmetic  0.86 us (1%)
    all_to_all x1, blocking collectives, per_device(): plane = lax.all_to_all(send, 'col', 0, 0, tiled=True)  26.2 us
    all_to_all x1, blocking collectives, per_device(): lax.all_to_all(lagged.astype(jnp.bfloat16), 'col', 0, 0, tiled=True)  12.2 us
    pallas_call x1, Pallas kernels, spectra(): pl.pallas_call(dft_kernel, in_specs=[hbm, hbm, hbm], out_specs=[vmem, vme...  6.25 us
    ppermute x1, waiting for transfers between devices, per_device(): halos = [lax.ppermute(head, 'row', down)]  5.3 us
    pallas_call x3, Pallas kernels, correlated_call(): pl.pallas_call(body, in_specs=in_specs, out_specs=out_specs, out_shape=ou...  5.13 us
    ppermute x1, starting transfers between devices, per_device(): halos = [lax.ppermute(head, 'row', down)]  2.15 us
    ppermute x1, starting transfers between devices, per_device(): halos.append(lax.ppermute(plane_head(later, HALO_PARTS[1]), 'row', down))  2.02 us
    pallas_call x1, Pallas kernels, own_half(): pl.pallas_call(own_kernel, in_specs=[pl.BlockSpec(memory_space=pltpu.SMEM...  1.63 us
  transfers between devices with their start and end apart: 3, of which 3 were waited for; matrix products, arithmetic and copies ran while one was open for 0% of the time, Pallas kernels for 9%

profile of v8, /device:TPU:96, one launch (start us, length us, event | category | flops | bytes accessed | tf_op | source)
XLA Modules:
  0.0 64.8 jit_solution(10278068417353565521)
XLA Ops:
  0.0 0.0 copy-start.2
  0.0 0.0 copy-start.3
  0.0 6.3 %dft_whiten.1 = (bf16[128,2432]{1,0:T(8,128)(2,1)S(1)}, f32[2560,256]{1,0:T(8,128)S(1)}) custom-call(bf16[256,7680]{1,0:T(8,128)(2,1)} %bitcast.9, bf16[1792,256]{1,0:T(8,128)(2,1)} %constant.37.clone.table_hbm, f32[8,768]{1,0:T(8,128)} %constant.38.clone.turn_hbm), custom_call_target="tpu_custom_call" | custom-call | tf_op jit(solution)/shard_map/dft_whiten/pallas_call | solution.py:305
  6.3 0.1 collective-permute-start
  6.4 0.0 copy-done.2
  6.4 0.0 copy-done.3
  6.4 1.6 %whiten_own.1 = (bf16[16,16,2432]{2,1,0:T(8,128)(2,1)S(1)}, f32[1200]{0:T(1024)S(1)}) custom-call(s32[1,4]{1,0:T(1,128)S(1)} %copy-done.3, f32[1200]{0:T(1024)S(1)} %copy-done.2, f32[2560,256]{1,0:T(8,128)S(1)} %get-tuple-element.28.sums_ref), custom_call_target="tpu_custom_call" | custom-call | flops 12451840 | bytes 5242880 | tf_op jit(solution)/shard_map/whiten_own/pallas_call | solution.py:330
  8.0 0.4 collective-permute-done
  8.4 0.1 bitcast_dynamic-update-slice_fusion
  8.5 26.2 %all_to_all.10.plane_ref.refs_2_ = bf16[16,16,2432]{2,1,0:T(8,128)(2,1)S(1)} all-to-all(bf16[16,16,2432]{2,1,0:T(8,128)(2,1)S(1)} %bitcast_dynamic-update-slice_fusion), channel_id=1, replica_groups=mesh['row'=8,'col'=16,'tm'=2] {'col'}, dimensions={0} | all-to-all | bytes 2490368 | tf_op jit(solution)/shard_map/all_to_all | solution.py:539
  34.7 0.0 copy-start
  34.7 2.1 %collective-permute-start.2 = (bf16[7,16,1664]{2,1,0:T(8,128)(2,1)S(1)}, bf16[7,16,1664]{2,1,0:T(8,128)(2,1)S(1)}, u32[]{:S(2)}, u32[]{:S(2)}) collective-permute-start(bf16[7,16,1664]{2,1,0:T(8,128)(2,1)S(1)} %plane_head.2), channel_id=1, source_target_pairs={{32,0},{64,32},{96,64},{128,96},{160,128},{192,160},{224,192},{33,... | collective-permute-start | bytes 1118216 | tf_op jit(solution)/shard_map/ppermute | solution.py:543
  36.8 0.1 reshape.46.squared_ref
  37.0 0.0 copy-done
  37.0 0.0 copy-start.1
  37.0 1.3 %copy-done.1 = bf16[2432,256]{1,0:T(8,128)(2,1)S(1)} copy-done((bf16[2432,256]{1,0:T(8,128)(2,1)S(1)}, bf16[2432,256]{1,0:T(8,128)(2,1)}, u32[]{:S(2)}) %copy-start.1) | copy-done | bytes 1245208
  38.3 3.1 %correlate_inner.1 = (f32[64,8,256]{2,1,0:T(8,128)S(1)}, s32[16,128]{1,0:T(8,128)S(4)}, f32[10,128]{1,0:T(8,128)S(1)}) custom-call(f32[120,10]{1,0:T(8,128)S(1)} %reshape.46.squared_ref, bf16[16,16,2432]{2,1,0:T(8,128)(2,1)S(1)} %all_to_all.10.plane_ref.refs_2_, bf16[2432,256]{1,0:T(8,128)(2,1)S(1)} %copy-done.1, bf16[2432,256]{1,0:T(8,128)(2,1)S(1)} %copy-done), custom_call_target="tpu_custom_call" | custom-call | flops 1075838976 | bytes 4194304 | tf_op jit(solution)/shard_map/correlate_inner/pallas_call | solution.py:515
  41.4 2.0 %collective-permute-start.1 = (bf16[7,16,768]{2,1,0:T(8,128)(2,1)S(1)}, bf16[7,16,768]{2,1,0:T(8,128)(2,1)S(1)}, u32[]{:S(2)}, u32[]{:S(2)}) collective-permute-start(bf16[7,16,768]{2,1,0:T(8,128)(2,1)S(1)} %plane_head.3), channel_id=1, source_target_pairs={{32,0},{64,32},{96,64},{128,96},{160,128},{192,160},{224,192},{33,... | collective-permute-start | bytes 516104 | tf_op jit(solution)/shard_map/ppermute | solution.py:565
  43.4 5.3 %collective-permute-done.2.refs_3_ = bf16[7,16,1664]{2,1,0:T(8,128)(2,1)S(1)} collective-permute-done((bf16[7,16,1664]{2,1,0:T(8,128)(2,1)S(1)}, bf16[7,16,1664]{2,1,0:T(8,128)(2,1)S(1)}, u32[]{:S(2)}, u32[]{:S(2)}) %collective-permute-start.2) | collective-permute-done | bytes 372768 | tf_op jit(solution)/shard_map/ppermute | solution.py:543
  48.7 1.4 %correlate_halo_first.1.refs_6_ = f32[28,8,256]{2,1,0:T(8,128)S(1)} custom-call(s32[16,128]{1,0:T(8,128)S(4)} %get-tuple-element.34.refs_0_, f32[10,128]{1,0:T(8,128)S(1)} %get-tuple-element.35.refs_1_, bf16[16,16,2432]{2,1,0:T(8,128)(2,1)S(1)} %all_to_all.10.plane_ref.refs_2_, bf16[7,16,1664]{2,1,0:T(8,128)(2,1)S(1)} %collective-permute-done.2.refs_3_, ...), custom_call_target="tpu_custom_call" | custom-call | flops 572522496 | bytes 4194304 | tf_op jit(solution)/shard_map/correlate_halo_first/pallas_call | solution.py:515
  50.1 0.9 %collective-permute-done.1.refs_3_ = bf16[7,16,768]{2,1,0:T(8,128)(2,1)S(1)} collective-permute-done((bf16[7,16,768]{2,1,0:T(8,128)(2,1)S(1)}, bf16[7,16,768]{2,1,0:T(8,128)(2,1)S(1)}, u32[]{:S(2)}, u32[]{:S(2)}) %collective-permute-start.1) | collective-permute-done | bytes 172064 | tf_op jit(solution)/shard_map/ppermute | solution.py:565
  51.0 0.6 correlate_halo_second.1
  51.7 12.2 %all_to_all.11 = bf16[16,4,8,256]{3,2,1,0:T(8,128)(2,1)S(1)} all-to-all(bf16[16,4,8,256]{3,2,1,0:T(8,128)(2,1)S(1)} %bitcast.10), channel_id=1, replica_groups=mesh['row'=8,'col'=16,'tm'=2] {'col'}, dimensions={0} | all-to-all | bytes 524288 | tf_op jit(solution)/shard_map/all_to_all | solution.py:596
  63.9 0.8 %copy_bitcast_fusion = f32[1,4,128,256]{3,2,1,0:T(8,128)} fusion(bf16[16,4,8,256]{3,2,1,0:T(8,128)(2,1)S(1)} %all_to_all.11), kind=kLoop, calls=%fused_computation.1 | loop fusion | flops 131072 | bytes 786432 | tf_op jit(solution)/shard_map/reshape | solution.py:597
  (3 shorter events, 0.1 us)
Async XLA Ops:
  0.0 6.4 %copy-start.2 = (f32[1200]{0:T(1024)S(1)}, f32[1200]{0:T(1024)}, u32[]{:S(2)}) copy-start(f32[1200]{0:T(1024)} %taper_ref.1) | copy-start | bytes 14404
  0.0 6.4 %copy-start.3 = (s32[1,4]{1,0:T(1,128)S(1)}, s32[1,4]{1,0:T(1,128)}, u32[]{:S(2)}) copy-start(s32[1,4]{1,0:T(1,128)} %pairs_ref.1) | copy-start | bytes 52
  6.3 2.1 %collective-permute-start = (bf16[128,2432]{1,0:T(8,128)(2,1)S(1)}, bf16[128,2432]{1,0:T(8,128)(2,1)S(1)}, u32[]{:S(2)}, u32[]{:S(2)}) collective-permute-start(bf16[128,2432]{1,0:T(8,128)(2,1)S(1)} %get-tuple-element.30), channel_id=1, source_target_pairs={{0,1},{1,0},{2,3},{3,2},{4,5},{5,4},{6,7},{7,6},{8,9},{9,8},{10,11... | collective-permute-start | bytes 1867784 | tf_op jit(solution)/shard_map/ppermute | solution.py:536
  34.7 2.3 %copy-start = (bf16[2432,256]{1,0:T(8,128)(2,1)S(1)}, bf16[2432,256]{1,0:T(8,128)(2,1)}, u32[]{:S(2)}) copy-start(bf16[2432,256]{1,0:T(8,128)(2,1)} %constant.40.clone.low_ref.refs_5_) | copy-start | bytes 3735556
  34.7 14.0 %collective-permute-start.2 = (bf16[7,16,1664]{2,1,0:T(8,128)(2,1)S(1)}, bf16[7,16,1664]{2,1,0:T(8,128)(2,1)S(1)}, u32[]{:S(2)}, u32[]{:S(2)}) collective-permute-start(bf16[7,16,1664]{2,1,0:T(8,128)(2,1)S(1)} %plane_head.2), channel_id=1, source_target_pairs={{32,0},{64,32},{96,64},{128,96},{160,128},{192,160},{224,192},{33,... | collective-permute-start | bytes 1118216 | tf_op jit(solution)/shard_map/ppermute | solution.py:543
  37.0 1.3 %copy-start.1 = (bf16[2432,256]{1,0:T(8,128)(2,1)S(1)}, bf16[2432,256]{1,0:T(8,128)(2,1)}, u32[]{:S(2)}) copy-start(bf16[2432,256]{1,0:T(8,128)(2,1)} %constant.39.clone.high_ref.refs_4_) | copy-start | bytes 3735556
  41.4 9.6 %collective-permute-start.1 = (bf16[7,16,768]{2,1,0:T(8,128)(2,1)S(1)}, bf16[7,16,768]{2,1,0:T(8,128)(2,1)S(1)}, u32[]{:S(2)}, u32[]{:S(2)}) collective-permute-start(bf16[7,16,768]{2,1,0:T(8,128)(2,1)S(1)} %plane_head.3), channel_id=1, source_target_pairs={{32,0},{64,32},{96,64},{128,96},{160,128},{192,160},{224,192},{33,... | collective-permute-start | bytes 516104 | tf_op jit(solution)/shard_map/ppermute | solution.py:565

commit v9 on v8

--- a/solution.py
+++ b/solution.py
@@ -145,9 +145,15 @@
     core = lax.axis_index("tm")
     size = BLOCK // CHUNKS
     y_refs = (even_ref, odd_ref)
+
+    def rows_of(c):
+        half, rest = c * size // HALF, c * size % HALF
+        side = 1 - core if half == 0 else core
+        return pl.ds(pl.multiple_of(side * HALF + rest, size), size)
+
     x_copies = [
         pltpu.make_async_copy(
-            x_hbm.at[pl.ds(c * size, size)], x_ref.at[pl.ds(c * size, size)], x_sems.at[c]
+            x_hbm.at[rows_of(c)], x_ref.at[pl.ds(c * size, size)], x_sems.at[c]
         )
         for c in range(CHUNKS)
     ]
@@ -192,35 +198,37 @@
             at = slice(n * BLOCK + c * size, n * BLOCK + (c + 1) * size)
             sums_ref[at] = sums_ref[at] + product[(n - 1) * size : n * size]
 
+    def multiply_last(half):
+        at = slice(half * HALF, (half + 1) * HALF)
+        sums_ref[PRODUCTS * BLOCK + half * HALF : PRODUCTS * BLOCK + (half + 1) * HALF] = jnp.dot(
+            last_ref[at], table_ref[PART : 2 * PART], preferred_element_type=jnp.float32
+        )
+
     turn_copy.wait()
     for c in range(CHUNKS):
         x_copies[c].wait()
         if c == 1:
             table_copy.wait()
+        for i in range(size // 16):
+            split(c, i)
         if c > 0:
             multiply(c - 1)
-        for i in range(size // 16):
-            split(c, i)
+        if c == CHUNKS // 2:
+            multiply_last(0)
+    for i in range(HALF // 16):
+        parts = [white_rows(sums_ref, i * 16 + j * MINE) for j in range(2)]
+        for n in range(TAIL + 1):
+            theirs_ref[i * 16 : (i + 1) * 16, n * LANES : (n + 1) * LANES] = jnp.concatenate(
+                [parts[0][n], parts[1][n]], axis=0
+            ).astype(jnp.bfloat16)
     multiply(CHUNKS - 1)
-    sums_ref[PRODUCTS * BLOCK :] = jnp.dot(
-        last_ref[...], table_ref[PART : 2 * PART], preferred_element_type=jnp.float32
-    )
-
-    def rows(i, carry):
-        row = (1 - core) * HALF + i * 16
-        parts = [white_rows(sums_ref, row + j * MINE) for j in range(2)]
-        for n in range(TAIL + 1):
-            theirs_ref[pl.ds(pl.multiple_of(i * 16, 16), 16), n * LANES : (n + 1) * LANES] = (
-                jnp.concatenate([parts[0][n], parts[1][n]], axis=0).astype(jnp.bfloat16)
-            )
-        return carry
-
-    lax.fori_loop(0, HALF // 16, rows, 0, unroll=2)
+    multiply_last(1)
 
 
 def spectrum_parts(sums_ref, row):
     def load(index):
-        at = pl.ds(pl.multiple_of(index * BLOCK + row, MINE), MINE)
+        first = index * BLOCK + row
+        at = pl.ds(first if isinstance(first, int) else pl.multiple_of(first, MINE), MINE)
         return sums_ref[at, :LANES], sums_ref[at, LANES:]
 
     parts = [load(0)]
@@ -270,7 +278,6 @@
 
 def own_kernel(pairs_ref, taper_ref, sums_ref, mine_ref, squared_ref):
     squared_ref[...] = taper_ref[...] * taper_ref[...]
-    core = lax.axis_index("tm")
     block = lax.axis_index("row") * PLANE + lax.axis_index("col")
     lane = lax.broadcasted_iota(jnp.int32, (MINE, LANES), 1)
     offsets = jnp.zeros((MINE, LANES), jnp.float32)
@@ -280,7 +287,7 @@
         offsets = jnp.where(lane == REST + k, offset, offsets)
 
     def rows(j, carry):
-        parts = white_rows(sums_ref, core * HALF + j * MINE)
+        parts = white_rows(sums_ref, HALF + j * MINE)
         parts[TAIL] = jnp.where((lane >= REST) & (lane < SIDE), offsets, parts[TAIL])
         for n, part in enumerate(parts):
             mine_ref[j, :, n * LANES : (n + 1) * LANES] = jnp.concatenate(

time: 65 us -> 64.6 us (level)
  transfers between devices with their start and end apart: 3 -> 3, of which waited for: 3 -> 3; matrix products, arithmetic and copies ran while one was open for 0% -> 0% of each run, Pallas kernels for 9% -> 10%
where the time goes in v9:
time: 64.6 us; the launch traced here: 64.4 us
  blocking collectives  38.4 us (59%)
  Pallas kernels  12.7 us (20%)
  waiting for transfers between devices  6.55 us (10%)
  starting transfers between devices  4.25 us (7%)
  local copies, waits for them, and re-layouts  1.49 us (2%)
  other arithmetic  0.86 us (1%)
    all_to_all x1, blocking collectives, per_device(): plane = lax.all_to_all(send, 'col', 0, 0, tiled=True)  26.2 us
    all_to_all x1, blocking collectives, per_device(): lax.all_to_all(lagged.astype(jnp.bfloat16), 'col', 0, 0, tiled=True)  12.2 us
    pallas_call x1, Pallas kernels, spectra(): pl.pallas_call(dft_kernel, in_specs=[hbm, hbm, hbm], out_specs=[vmem, vme...  5.85 us
    ppermute x1, waiting for transfers between devices, per_device(): halos = [lax.ppermute(head, 'row', down)]  5.3 us
    pallas_call x3, Pallas kernels, correlated_call(): pl.pallas_call(body, in_specs=in_specs, out_specs=out_specs, out_shape=ou...  5.13 us
    ppermute x1, starting transfers between devices, per_device(): halos = [lax.ppermute(head, 'row', down)]  2.15 us
    ppermute x1, starting transfers between devices, per_device(): halos.append(lax.ppermute(plane_head(later, HALO_PARTS[1]), 'row', down))  2.01 us
    pallas_call x1, Pallas kernels, own_half(): pl.pallas_call(own_kernel, in_specs=[pl.BlockSpec(memory_space=pltpu.SMEM...  1.63 us
  transfers between devices with their start and end apart: 3, of which 3 were waited for; matrix products, arithmetic and copies ran while one was open for 0% of the time, Pallas kernels for 10%

profile of v9, /device:TPU:96, one launch (start us, length us, event | category | flops | bytes accessed | tf_op | source)
XLA Modules:
  0.0 64.4 jit_solution(2091865989647942181)
XLA Ops:
  0.0 0.0 copy-start.2
  0.0 0.0 copy-start.3
  0.0 5.8 %dft_whiten.1 = (bf16[128,2432]{1,0:T(8,128)(2,1)S(1)}, f32[2560,256]{1,0:T(8,128)S(1)}) custom-call(bf16[256,7680]{1,0:T(8,128)(2,1)} %bitcast.9, bf16[1792,256]{1,0:T(8,128)(2,1)} %constant.37.clone.table_hbm, f32[8,768]{1,0:T(8,128)} %constant.38.clone.turn_hbm), custom_call_target="tpu_custom_call" | custom-call | tf_op jit(solution)/shard_map/dft_whiten/pallas_call | solution.py:312
  5.9 0.1 collective-permute-start
  6.0 0.0 copy-done.2
  6.0 0.0 copy-done.3
  6.0 1.6 %whiten_own.1 = (bf16[16,16,2432]{2,1,0:T(8,128)(2,1)S(1)}, f32[1200]{0:T(1024)S(1)}) custom-call(s32[1,4]{1,0:T(1,128)S(1)} %copy-done.3, f32[1200]{0:T(1024)S(1)} %copy-done.2, f32[2560,256]{1,0:T(8,128)S(1)} %get-tuple-element.28.sums_ref), custom_call_target="tpu_custom_call" | custom-call | flops 12451840 | bytes 5242880 | tf_op jit(solution)/shard_map/whiten_own/pallas_call | solution.py:337
  7.6 0.4 collective-permute-done
  8.0 0.1 bitcast_dynamic-update-slice_fusion
  8.1 26.2 %all_to_all.10.plane_ref.refs_2_ = bf16[16,16,2432]{2,1,0:T(8,128)(2,1)S(1)} all-to-all(bf16[16,16,2432]{2,1,0:T(8,128)(2,1)S(1)} %bitcast_dynamic-update-slice_fusion), channel_id=1, replica_groups=mesh['row'=8,'col'=16,'tm'=2] {'col'}, dimensions={0} | all-to-all | bytes 2490368 | tf_op jit(solution)/shard_map/all_to_all | solution.py:546
  34.3 0.0 copy-start
  34.3 2.1 %collective-permute-start.2 = (bf16[7,16,1664]{2,1,0:T(8,128)(2,1)S(1)}, bf16[7,16,1664]{2,1,0:T(8,128)(2,1)S(1)}, u32[]{:S(2)}, u32[]{:S(2)}) collective-permute-start(bf16[7,16,1664]{2,1,0:T(8,128)(2,1)S(1)} %plane_head.2), channel_id=1, source_target_pairs={{32,0},{64,32},{96,64},{128,96},{160,128},{192,160},{224,192},{33,... | collective-permute-start | bytes 1118216 | tf_op jit(solution)/shard_map/ppermute | solution.py:550
  36.4 0.1 reshape.46.squared_ref
  36.6 0.0 copy-done
  36.6 0.0 copy-start.1
  36.6 1.3 %copy-done.1 = bf16[2432,256]{1,0:T(8,128)(2,1)S(1)} copy-done((bf16[2432,256]{1,0:T(8,128)(2,1)S(1)}, bf16[2432,256]{1,0:T(8,128)(2,1)}, u32[]{:S(2)}) %copy-start.1) | copy-done | bytes 1245208
  37.9 3.1 %correlate_inner.1 = (f32[64,8,256]{2,1,0:T(8,128)S(1)}, s32[16,128]{1,0:T(8,128)S(4)}, f32[10,128]{1,0:T(8,128)S(1)}) custom-call(f32[120,10]{1,0:T(8,128)S(1)} %reshape.46.squared_ref, bf16[16,16,2432]{2,1,0:T(8,128)(2,1)S(1)} %all_to_all.10.plane_ref.refs_2_, bf16[2432,256]{1,0:T(8,128)(2,1)S(1)} %copy-done.1, bf16[2432,256]{1,0:T(8,128)(2,1)S(1)} %copy-done), custom_call_target="tpu_custom_call" | custom-call | flops 1075838976 | bytes 4194304 | tf_op jit(solution)/shard_map/correlate_inner/pallas_call | solution.py:522
  41.0 2.0 %collective-permute-start.1 = (bf16[7,16,768]{2,1,0:T(8,128)(2,1)S(1)}, bf16[7,16,768]{2,1,0:T(8,128)(2,1)S(1)}, u32[]{:S(2)}, u32[]{:S(2)}) collective-permute-start(bf16[7,16,768]{2,1,0:T(8,128)(2,1)S(1)} %plane_head.3), channel_id=1, source_target_pairs={{32,0},{64,32},{96,64},{128,96},{160,128},{192,160},{224,192},{33,... | collective-permute-start | bytes 516104 | tf_op jit(solution)/shard_map/ppermute | solution.py:572
  43.0 5.3 %collective-permute-done.2.refs_3_ = bf16[7,16,1664]{2,1,0:T(8,128)(2,1)S(1)} collective-permute-done((bf16[7,16,1664]{2,1,0:T(8,128)(2,1)S(1)}, bf16[7,16,1664]{2,1,0:T(8,128)(2,1)S(1)}, u32[]{:S(2)}, u32[]{:S(2)}) %collective-permute-start.2) | collective-permute-done | bytes 372768 | tf_op jit(solution)/shard_map/ppermute | solution.py:550
  48.3 1.4 %correlate_halo_first.1.refs_6_ = f32[28,8,256]{2,1,0:T(8,128)S(1)} custom-call(s32[16,128]{1,0:T(8,128)S(4)} %get-tuple-element.34.refs_0_, f32[10,128]{1,0:T(8,128)S(1)} %get-tuple-element.35.refs_1_, bf16[16,16,2432]{2,1,0:T(8,128)(2,1)S(1)} %all_to_all.10.plane_ref.refs_2_, bf16[7,16,1664]{2,1,0:T(8,128)(2,1)S(1)} %collective-permute-done.2.refs_3_, ...), custom_call_target="tpu_custom_call" | custom-call | flops 572522496 | bytes 4194304 | tf_op jit(solution)/shard_map/correlate_halo_first/pallas_call | solution.py:522
  49.7 0.9 %collective-permute-done.1.refs_3_ = bf16[7,16,768]{2,1,0:T(8,128)(2,1)S(1)} collective-permute-done((bf16[7,16,768]{2,1,0:T(8,128)(2,1)S(1)}, bf16[7,16,768]{2,1,0:T(8,128)(2,1)S(1)}, u32[]{:S(2)}, u32[]{:S(2)}) %collective-permute-start.1) | collective-permute-done | bytes 172064 | tf_op jit(solution)/shard_map/ppermute | solution.py:572
  50.6 0.6 %correlate_halo_second.1 = f32[64,8,256]{2,1,0:T(8,128)S(1)} custom-call(s32[16,128]{1,0:T(8,128)S(4)} %get-tuple-element.34.refs_0_, f32[10,128]{1,0:T(8,128)S(1)} %get-tuple-element.35.refs_1_, bf16[16,16,2432]{2,1,0:T(8,128)(2,1)S(1)} %all_to_all.10.plane_ref.refs_2_, ...), custom_call_target="tpu_custom_call", output_to_operand_aliasing={{}: (7, {})} | custom-call | flops 264241152 | bytes 4194304 | tf_op jit(solution)/shard_map/correlate_halo_second/pallas_call | solution.py:522
  51.3 12.2 %all_to_all.11 = bf16[16,4,8,256]{3,2,1,0:T(8,128)(2,1)S(1)} all-to-all(bf16[16,4,8,256]{3,2,1,0:T(8,128)(2,1)S(1)} %bitcast.10), channel_id=1, replica_groups=mesh['row'=8,'col'=16,'tm'=2] {'col'}, dimensions={0} | all-to-all | bytes 524288 | tf_op jit(solution)/shard_map/all_to_all | solution.py:603
  63.5 0.8 %copy_bitcast_fusion = f32[1,4,128,256]{3,2,1,0:T(8,128)} fusion(bf16[16,4,8,256]{3,2,1,0:T(8,128)(2,1)S(1)} %all_to_all.11), kind=kLoop, calls=%fused_computation.1 | loop fusion | flops 131072 | bytes 786432 | tf_op jit(solution)/shard_map/reshape | solution.py:604
  (3 shorter events, 0.1 us)
Async XLA Ops:
  0.0 6.0 %copy-start.2 = (f32[1200]{0:T(1024)S(1)}, f32[1200]{0:T(1024)}, u32[]{:S(2)}) copy-start(f32[1200]{0:T(1024)} %taper_ref.1) | copy-start | bytes 14404
  0.0 6.0 %copy-start.3 = (s32[1,4]{1,0:T(1,128)S(1)}, s32[1,4]{1,0:T(1,128)}, u32[]{:S(2)}) copy-start(s32[1,4]{1,0:T(1,128)} %pairs_ref.1) | copy-start | bytes 52
  5.9 2.1 %collective-permute-start = (bf16[128,2432]{1,0:T(8,128)(2,1)S(1)}, bf16[128,2432]{1,0:T(8,128)(2,1)S(1)}, u32[]{:S(2)}, u32[]{:S(2)}) collective-permute-start(bf16[128,2432]{1,0:T(8,128)(2,1)S(1)} %get-tuple-element.30), channel_id=1, source_target_pairs={{0,1},{1,0},{2,3},{3,2},{4,5},{5,4},{6,7},{7,6},{8,9},{9,8},{10,11... | collective-permute-start | bytes 1867784 | tf_op jit(solution)/shard_map/ppermute | solution.py:543
  34.3 2.3 %copy-start = (bf16[2432,256]{1,0:T(8,128)(2,1)S(1)}, bf16[2432,256]{1,0:T(8,128)(2,1)}, u32[]{:S(2)}) copy-start(bf16[2432,256]{1,0:T(8,128)(2,1)} %constant.40.clone.low_ref.refs_5_) | copy-start | bytes 3735556
  34.3 14.0 %collective-permute-start.2 = (bf16[7,16,1664]{2,1,0:T(8,128)(2,1)S(1)}, bf16[7,16,1664]{2,1,0:T(8,128)(2,1)S(1)}, u32[]{:S(2)}, u32[]{:S(2)}) collective-permute-start(bf16[7,16,1664]{2,1,0:T(8,128)(2,1)S(1)} %plane_head.2), channel_id=1, source_target_pairs={{32,0},{64,32},{96,64},{128,96},{160,128},{192,160},{224,192},{33,... | collective-permute-start | bytes 1118216 | tf_op jit(solution)/shard_map/ppermute | solution.py:550
  36.6 1.3 %copy-start.1 = (bf16[2432,256]{1,0:T(8,128)(2,1)S(1)}, bf16[2432,256]{1,0:T(8,128)(2,1)}, u32[]{:S(2)}) copy-start(bf16[2432,256]{1,0:T(8,128)(2,1)} %constant.39.clone.high_ref.refs_4_) | copy-start | bytes 3735556
  41.0 9.6 %collective-permute-start.1 = (bf16[7,16,768]{2,1,0:T(8,128)(2,1)S(1)}, bf16[7,16,768]{2,1,0:T(8,128)(2,1)S(1)}, u32[]{:S(2)}, u32[]{:S(2)}) collective-permute-start(bf16[7,16,768]{2,1,0:T(8,128)(2,1)S(1)} %plane_head.3), channel_id=1, source_target_pairs={{32,0},{64,32},{96,64},{128,96},{160,128},{192,160},{224,192},{33,... | collective-permute-start | bytes 516104 | tf_op jit(solution)/shard_map/ppermute | solution.py:572

commit v10 on v9

--- a/solution.py
+++ b/solution.py
@@ -37,7 +37,7 @@
 TURNS = 4
 ORDER = (0, 1, -1, 2, -2, 3, -3, 4, -4, 5)
 PRODUCTS = 1 + 2 * TURNS
-FINE = 256
+FINE = 512
 PLANE = 16
 INNER = PLANE - REACH
 MINE = HALF // PLANE

time: 64.6 us -> 65 us (level)
  transfers between devices with their start and end apart: 3 -> 3, of which waited for: 3 -> 3; matrix products, arithmetic and copies ran while one was open for 0% -> 0% of each run, Pallas kernels for 10% -> 9%
where the time goes in v10:
time: 65 us; the launch traced here: 64.8 us
  blocking collectives  38.4 us (59%)
  Pallas kernels  13 us (20%)
  waiting for transfers between devices  6.56 us (10%)
  starting transfers between devices  4.26 us (7%)
  local copies, waits for them, and re-layouts  1.49 us (2%)
  other arithmetic  0.86 us (1%)
    all_to_all x1, blocking collectives, per_device(): plane = lax.all_to_all(send, 'col', 0, 0, tiled=True)  26.2 us
    all_to_all x1, blocking collectives, per_device(): lax.all_to_all(lagged.astype(jnp.bfloat16), 'col', 0, 0, tiled=True)  12.2 us
    pallas_call x1, Pallas kernels, spectra(): pl.pallas_call(dft_kernel, in_specs=[hbm, hbm, hbm], out_specs=[vmem, vme...  6.23 us
    ppermute x1, waiting for transfers between devices, per_device(): halos = [lax.ppermute(head, 'row', down)]  5.3 us
    pallas_call x3, Pallas kernels, correlated_call(): pl.pallas_call(body, in_specs=in_specs, out_specs=out_specs, out_shape=ou...  5.11 us
    ppermute x1, starting transfers between devices, per_device(): halos = [lax.ppermute(head, 'row', down)]  2.15 us
    ppermute x1, starting transfers between devices, per_device(): halos.append(lax.ppermute(plane_head(later, HALO_PARTS[1]), 'row', down))  2.02 us
    pallas_call x1, Pallas kernels, own_half(): pl.pallas_call(own_kernel, in_specs=[pl.BlockSpec(memory_space=pltpu.SMEM...  1.63 us
  transfers between devices with their start and end apart: 3, of which 3 were waited for; matrix products, arithmetic and copies ran while one was open for 0% of the time, Pallas kernels for 9%

profile of v10, /device:TPU:96, one launch (start us, length us, event | category | flops | bytes accessed | tf_op | source)
XLA Modules:
  0.0 64.8 jit_solution(6629790573744376418)
XLA Ops:
  0.0 0.0 copy-start.2
  0.0 0.0 copy-start.3
  0.0 6.2 %dft_whiten.1 = (bf16[128,2432]{1,0:T(8,128)(2,1)S(1)}, f32[2560,256]{1,0:T(8,128)S(1)}) custom-call(bf16[256,7680]{1,0:T(8,128)(2,1)} %bitcast.9, bf16[2048,256]{1,0:T(8,128)(2,1)} %constant.37.clone.table_hbm, f32[8,768]{1,0:T(8,128)} %constant.38.clone.turn_hbm), custom_call_target="tpu_custom_call" | custom-call | tf_op jit(solution)/shard_map/dft_whiten/pallas_call | solution.py:312
  6.2 0.1 collective-permute-start
  6.3 0.0 copy-done.2
  6.4 0.0 copy-done.3
  6.4 1.6 %whiten_own.1 = (bf16[16,16,2432]{2,1,0:T(8,128)(2,1)S(1)}, f32[1200]{0:T(1024)S(1)}) custom-call(s32[1,4]{1,0:T(1,128)S(1)} %copy-done.3, f32[1200]{0:T(1024)S(1)} %copy-done.2, f32[2560,256]{1,0:T(8,128)S(1)} %get-tuple-element.28.sums_ref), custom_call_target="tpu_custom_call" | custom-call | flops 12451840 | bytes 5242880 | tf_op jit(solution)/shard_map/whiten_own/pallas_call | solution.py:337
  8.0 0.4 collective-permute-done
  8.4 0.1 bitcast_dynamic-update-slice_fusion
  8.4 26.2 %all_to_all.10.plane_ref.refs_2_ = bf16[16,16,2432]{2,1,0:T(8,128)(2,1)S(1)} all-to-all(bf16[16,16,2432]{2,1,0:T(8,128)(2,1)S(1)} %bitcast_dynamic-update-slice_fusion), channel_id=1, replica_groups=mesh['row'=8,'col'=16,'tm'=2] {'col'}, dimensions={0} | all-to-all | bytes 2490368 | tf_op jit(solution)/shard_map/all_to_all | solution.py:546
  34.6 0.0 copy-start
  34.7 2.2 %collective-permute-start.2 = (bf16[7,16,1664]{2,1,0:T(8,128)(2,1)S(1)}, bf16[7,16,1664]{2,1,0:T(8,128)(2,1)S(1)}, u32[]{:S(2)}, u32[]{:S(2)}) collective-permute-start(bf16[7,16,1664]{2,1,0:T(8,128)(2,1)S(1)} %plane_head.2), channel_id=1, source_target_pairs={{32,0},{64,32},{96,64},{128,96},{160,128},{192,160},{224,192},{33,... | collective-permute-start | bytes 1118216 | tf_op jit(solution)/shard_map/ppermute | solution.py:550
  36.8 0.1 reshape.46.squared_ref
  37.0 0.0 copy-done
  37.0 0.0 copy-start.1
  37.0 1.3 %copy-done.1 = bf16[2432,256]{1,0:T(8,128)(2,1)S(1)} copy-done((bf16[2432,256]{1,0:T(8,128)(2,1)S(1)}, bf16[2432,256]{1,0:T(8,128)(2,1)}, u32[]{:S(2)}) %copy-start.1) | copy-done | bytes 1245208
  38.3 3.1 %correlate_inner.1 = (f32[64,8,256]{2,1,0:T(8,128)S(1)}, s32[16,128]{1,0:T(8,128)S(4)}, f32[10,128]{1,0:T(8,128)S(1)}) custom-call(f32[120,10]{1,0:T(8,128)S(1)} %reshape.46.squared_ref, bf16[16,16,2432]{2,1,0:T(8,128)(2,1)S(1)} %all_to_all.10.plane_ref.refs_2_, bf16[2432,256]{1,0:T(8,128)(2,1)S(1)} %copy-done.1, bf16[2432,256]{1,0:T(8,128)(2,1)S(1)} %copy-done), custom_call_target="tpu_custom_call" | custom-call | flops 1075838976 | bytes 4194304 | tf_op jit(solution)/shard_map/correlate_inner/pallas_call | solution.py:522
  41.4 2.0 %collective-permute-start.1 = (bf16[7,16,768]{2,1,0:T(8,128)(2,1)S(1)}, bf16[7,16,768]{2,1,0:T(8,128)(2,1)S(1)}, u32[]{:S(2)}, u32[]{:S(2)}) collective-permute-start(bf16[7,16,768]{2,1,0:T(8,128)(2,1)S(1)} %plane_head.3), channel_id=1, source_target_pairs={{32,0},{64,32},{96,64},{128,96},{160,128},{192,160},{224,192},{33,... | collective-permute-start | bytes 516104 | tf_op jit(solution)/shard_map/ppermute | solution.py:572
  43.4 5.3 %collective-permute-done.2.refs_3_ = bf16[7,16,1664]{2,1,0:T(8,128)(2,1)S(1)} collective-permute-done((bf16[7,16,1664]{2,1,0:T(8,128)(2,1)S(1)}, bf16[7,16,1664]{2,1,0:T(8,128)(2,1)S(1)}, u32[]{:S(2)}, u32[]{:S(2)}) %collective-permute-start.2) | collective-permute-done | bytes 372768 | tf_op jit(solution)/shard_map/ppermute | solution.py:550
  48.7 1.4 %correlate_halo_first.1.refs_6_ = f32[28,8,256]{2,1,0:T(8,128)S(1)} custom-call(s32[16,128]{1,0:T(8,128)S(4)} %get-tuple-element.34.refs_0_, f32[10,128]{1,0:T(8,128)S(1)} %get-tuple-element.35.refs_1_, bf16[16,16,2432]{2,1,0:T(8,128)(2,1)S(1)} %all_to_all.10.plane_ref.refs_2_, bf16[7,16,1664]{2,1,0:T(8,128)(2,1)S(1)} %collective-permute-done.2.refs_3_, ...), custom_call_target="tpu_custom_call" | custom-call | flops 572522496 | bytes 4194304 | tf_op jit(solution)/shard_map/correlate_halo_first/pallas_call | solution.py:522
  50.1 0.9 %collective-permute-done.1.refs_3_ = bf16[7,16,768]{2,1,0:T(8,128)(2,1)S(1)} collective-permute-done((bf16[7,16,768]{2,1,0:T(8,128)(2,1)S(1)}, bf16[7,16,768]{2,1,0:T(8,128)(2,1)S(1)}, u32[]{:S(2)}, u32[]{:S(2)}) %collective-permute-start.1) | collective-permute-done | bytes 172064 | tf_op jit(solution)/shard_map/ppermute | solution.py:572
  51.0 0.6 correlate_halo_second.1
  51.7 12.2 %all_to_all.11 = bf16[16,4,8,256]{3,2,1,0:T(8,128)(2,1)S(1)} all-to-all(bf16[16,4,8,256]{3,2,1,0:T(8,128)(2,1)S(1)} %bitcast.10), channel_id=1, replica_groups=mesh['row'=8,'col'=16,'tm'=2] {'col'}, dimensions={0} | all-to-all | bytes 524288 | tf_op jit(solution)/shard_map/all_to_all | solution.py:603
  63.9 0.8 %copy_bitcast_fusion = f32[1,4,128,256]{3,2,1,0:T(8,128)} fusion(bf16[16,4,8,256]{3,2,1,0:T(8,128)(2,1)S(1)} %all_to_all.11), kind=kLoop, calls=%fused_computation.1 | loop fusion | flops 131072 | bytes 786432 | tf_op jit(solution)/shard_map/reshape | solution.py:604
  (3 shorter events, 0.1 us)
Async XLA Ops:
  0.0 6.3 %copy-start.2 = (f32[1200]{0:T(1024)S(1)}, f32[1200]{0:T(1024)}, u32[]{:S(2)}) copy-start(f32[1200]{0:T(1024)} %taper_ref.1) | copy-start | bytes 14404
  0.0 6.4 %copy-start.3 = (s32[1,4]{1,0:T(1,128)S(1)}, s32[1,4]{1,0:T(1,128)}, u32[]{:S(2)}) copy-start(s32[1,4]{1,0:T(1,128)} %pairs_ref.1) | copy-start | bytes 52
  6.2 2.1 %collective-permute-start = (bf16[128,2432]{1,0:T(8,128)(2,1)S(1)}, bf16[128,2432]{1,0:T(8,128)(2,1)S(1)}, u32[]{:S(2)}, u32[]{:S(2)}) collective-permute-start(bf16[128,2432]{1,0:T(8,128)(2,1)S(1)} %get-tuple-element.30), channel_id=1, source_target_pairs={{0,1},{1,0},{2,3},{3,2},{4,5},{5,4},{6,7},{7,6},{8,9},{9,8},{10,11... | collective-permute-start | bytes 1867784 | tf_op jit(solution)/shard_map/ppermute | solution.py:543
  34.6 2.3 %copy-start = (bf16[2432,256]{1,0:T(8,128)(2,1)S(1)}, bf16[2432,256]{1,0:T(8,128)(2,1)}, u32[]{:S(2)}) copy-start(bf16[2432,256]{1,0:T(8,128)(2,1)} %constant.40.clone.low_ref.refs_5_) | copy-start | bytes 3735556
  34.7 14.0 %collective-permute-start.2 = (bf16[7,16,1664]{2,1,0:T(8,128)(2,1)S(1)}, bf16[7,16,1664]{2,1,0:T(8,128)(2,1)S(1)}, u32[]{:S(2)}, u32[]{:S(2)}) collective-permute-start(bf16[7,16,1664]{2,1,0:T(8,128)(2,1)S(1)} %plane_head.2), channel_id=1, source_target_pairs={{32,0},{64,32},{96,64},{128,96},{160,128},{192,160},{224,192},{33,... | collective-permute-start | bytes 1118216 | tf_op jit(solution)/shard_map/ppermute | solution.py:550
  37.0 1.3 %copy-start.1 = (bf16[2432,256]{1,0:T(8,128)(2,1)S(1)}, bf16[2432,256]{1,0:T(8,128)(2,1)}, u32[]{:S(2)}) copy-start(bf16[2432,256]{1,0:T(8,128)(2,1)} %constant.39.clone.high_ref.refs_4_) | copy-start | bytes 3735556
  41.4 9.6 %collective-permute-start.1 = (bf16[7,16,768]{2,1,0:T(8,128)(2,1)S(1)}, bf16[7,16,768]{2,1,0:T(8,128)(2,1)S(1)}, u32[]{:S(2)}, u32[]{:S(2)}) collective-permute-start(bf16[7,16,768]{2,1,0:T(8,128)(2,1)S(1)} %plane_head.3), channel_id=1, source_target_pairs={{32,0},{64,32},{96,64},{128,96},{160,128},{192,160},{224,192},{33,... | collective-permute-start | bytes 516104 | tf_op jit(solution)/shard_map/ppermute | solution.py:572
